TPU v7x, 1024 devices: a whole 4x4x32 slice. The times are simulated.
1024 devices in a mesh: row: 64 (over z, core), col: 16 (over x, y).
Axes of the slice: x: 4, y: 4, z: 32, core: 2. Of those that a mesh axis runs over, the one named last changes fastest.
Arguments:
- grad_out: bfloat16 [131072, 256], P(('col', 'row')), may hold values from -384 to 384
- features: bfloat16 [131072, 256], P(('row', 'col')), may hold values from -24 to 24
- weight: bfloat16 [256, 256], replicated, may hold values from -0.375 to 0.375
- tile_values: bfloat16 [64, 16, 80, 128, 128], P('row', 'col'), may hold values from 0 to 0.00048828125
- tile_rows: int32 [64, 16, 80], P('row', 'col'), may hold values from 0 to 15
- tile_cols: int32 [64, 16, 80], P('row', 'col'), may hold values from 0 to 63
- tile_count: int32 [64, 16], P('row', 'col'), may hold values from 20 to 80, as said below
Outputs:
- input_grad: bfloat16 [131072, 256], P(('row', 'col'))
- weight_grad: float32 [256, 256], replicated
Inputs may be any that keep to these rules, and one draw needn't show every extreme that they name: Live slots of a block are its first tile_count entries; every draw has blocks with all 80 slots live.
All inputs are finite; a program needn't handle non-finite values.
Results may differ from a plain program's by a relative error of at most 0.0049.
Values may be sent and summed in bfloat16 or wider, within the bound.
No kernel may reach another device: no remote copies, remote signals or barrier semaphores. Data moves between devices by JAX's collectives and lax.ppermute only.
A program may use at most 32 MiB of HBM per device.

v0:
```python
import math

import jax
import jax.numpy as jnp
from jax import lax
from jax.sharding import PartitionSpec as P


def body(grad_out, features, weight, tile_values, tile_rows, tile_cols, tile_count):
    gathered = lax.all_gather(grad_out, "row", axis=0, tiled=True)
    values = tile_values[0, 0]
    rows_of = tile_rows[0, 0]
    cols_of = tile_cols[0, 0]
    count = tile_count[0, 0]
    tile = values.shape[-1]
    width = gathered.shape[1]
    capacity = values.shape[0]
    own_rows = features.shape[0]
    col_size = lax.axis_size("col")
    row_tiles = own_rows * col_size // tile
    col_blocks = gathered.reshape(-1, tile, width)
    live = jnp.arange(capacity, dtype=jnp.int32) < count
    group = 16
    stacked = (
        values.reshape(-1, group, tile, tile),
        rows_of.reshape(-1, group),
        cols_of.reshape(-1, group),
        live.reshape(-1, group),
    )
    targets = jnp.arange(row_tiles, dtype=jnp.int32)

    def accumulate(total, pieces):
        vals, row_ids, col_ids, alive = pieces
        picked = col_blocks[col_ids]
        prods = jnp.einsum("gij,gjw->giw", vals, picked, preferred_element_type=jnp.float32)
        placing = ((row_ids[:, None] == targets[None, :]) & alive[:, None]).astype(jnp.float32)
        return (
            total + jnp.einsum("gr,giw->riw", placing, prods, precision=lax.Precision.HIGHEST),
            None,
        )

    start = jnp.zeros((row_tiles, tile, width), jnp.float32)
    total, unused = lax.scan(accumulate, start, stacked)
    partial_value = total.reshape(row_tiles * tile, width)
    summed = lax.psum_scatter(partial_value, "col", scatter_dimension=0, tiled=True)
    carried_b = summed.astype(jnp.bfloat16)
    input_grad = jnp.dot(carried_b, weight.T, preferred_element_type=jnp.float32).astype(
        jnp.bfloat16
    )
    scale = 1.0 / math.sqrt(own_rows * lax.axis_size("row") * col_size)
    local_grad = (
        lax.dot_general(
            features, carried_b, (((0,), (0,)), ((), ())), preferred_element_type=jnp.float32
        )
        * scale
    )
    weight_grad = lax.psum(local_grad, ("row", "col"))
    return (input_grad, weight_grad)


def solution(mesh):
    placed = (
        P(("col", "row"), None),
        P(("row", "col"), None),
        P(),
        P("row", "col", None, None, None),
        P("row", "col", None),
        P("row", "col", None),
        P("row", "col"),
    )
    return jax.shard_map(
        body, mesh=mesh, in_specs=placed, out_specs=(P(("row", "col"), None), P()), check_vma=False
    )
```

profile of v0, /device:TPU:6, one launch (start us, length us, event | category | flops | bytes accessed | tf_op | source)
XLA Modules:
  0.0 1184.6 jit_solution(1615839552340375463)
XLA Ops:
  7.2 0.0 all-gather.2.cloned.1.call-start
  7.2 0.7 all-gather.2.cloned.1.call-update
  7.9 0.0 reduce-scatter.2.cloned.1.call-start
  8.6 0.5 broadcast.46
  9.1 1.3 reduce.6
  10.4 1.3 reduce.7
  11.8 0.1 reshape_squeeze.11
  11.8 0.1 reshape_squeeze.9
  11.9 145.7 %all-gather.2.cloned.1.call-done = bf16[8192,256]{1,0:T(8,128)(2,1)} async-done(((bf16[128,256]{1,0:T(8,128)(2,1)}), bf16[8192,256]{1,0:T(8,128)(2,1)}) %all-gather.2.cloned.1.call-update) | async-done | bytes 4194320 | tf_op jit(solution)/shard_map/all_gather | solution.py:10
  157.7 38.6 %while.11 = (s32[]{:T(128)}, f32[16,128,256]{2,0,1:T(8,128)S(1)}, s32[5,16]{1,0:T(8,128)S(1)}, pred[5,16]{1,0:T(8,128)(4,1)S(1)}, bf16[5,16,128,128]{3,2,1,0:T(8...) while((s32[]{:T(128)}, f32[16,128,256]{2,0,1:T(8,128)S(1)}, ...), condition=%wide.region_1.2_spmd.clone, body=%wide.region_0.1_spmd.clone.sunk | while | flops 235931184 | bytes 12063343 | solution.py:43
  157.7 2.8 gather_fusion
  160.5 1.5 fusion.36
  162.0 3.4 select_add_fusion.2
  165.4 2.8 gather_fusion
  168.2 1.5 fusion.36
  169.7 3.4 select_add_fusion.2
  173.2 2.8 gather_fusion
  176.0 1.5 fusion.36
  177.4 3.4 select_add_fusion.2
  180.9 2.8 gather_fusion
  183.7 1.5 fusion.36
  185.2 3.4 select_add_fusion.2
  188.6 2.8 gather_fusion
  191.4 1.5 fusion.36
  192.9 3.4 select_add_fusion.2
  196.3 2.6 copy.10
  198.9 0.0 all-reduce.2.cloned.1.call-start
  198.9 101.1 %reduce-scatter.2.cloned.1.call-done = f32[128,256]{1,0:T(8,128)} async-done(((f32[2048,256]{1,0:T(8,128)}), f32[128,256]{1,0:T(8,128)}) %reduce-scatter.2.cloned.1.call-update) | async-done | bytes 131088 | tf_op jit(solution)/shard_map/reduce_scatter | solution.py:45
  300.0 1.8 fusion.18
  301.9 1.7 convolution_convert_fusion
  303.6 872.7 %all-reduce.2.cloned.1.call-done = f32[256,256]{0,1:T(8,128)} async-done(((f32[256,256]{0,1:T(8,128)}), f32[256,256]{0,1:T(8,128)}) %all-reduce.2.cloned.1.call-update) | async-done | bytes 262160 | tf_op jit(solution)/shard_map/psum | solution.py:57
  1176.3 1.8 copy.11
  (28 shorter events, 0.2 us)
Async XLA Ops:
  7.2 294.7 %copy-start = (bf16[256,256]{1,0:T(8,128)(2,1)S(1)}, bf16[256,256]{1,0:T(8,128)(2,1)}, u32[]{:S(2)}) copy-start(bf16[256,256]{1,0:T(8,128)(2,1)} %param.11) | copy-start | bytes 393220
  7.2 150.5 %all-gather.2.cloned.1.call-start = ((), (), s32[]{:S(2)}) async-start(), calls=%async_computation.1 | async-start | bytes 4259840 | tf_op jit(solution)/shard_map/all_gather | solution.py:10
  7.9 292.1 %reduce-scatter.2.cloned.1.call-start = ((), (), s32[]{:S(2)}) async-start(), calls=%async_computation.2 | async-start | bytes 2228224 | tf_op jit(solution)/shard_map/reduce_scatter | solution.py:45
  198.8 101.2 %copy-start.1 = (bf16[128,256]{1,0:T(8,128)(2,1)S(1)}, bf16[128,256]{1,0:T(8,128)(2,1)}, u32[]{:S(2)}) copy-start(bf16[128,256]{1,0:T(8,128)(2,1)} %param.10) | copy-start | bytes 196612
  198.9 977.5 %all-reduce.2.cloned.1.call-start = ((), (), s32[]{:S(2)}) async-start(), calls=%async_computation.3 | async-start | bytes 524288 | tf_op jit(solution)/shard_map/psum | solution.py:57
Sparse Core Ops, SparseCore 0:
  10.7 146.9 all-gather.1
  199.0 101.0 reduce-scatter.1
  307.0 869.2 all-reduce.1
where the time goes:
time: 1190 us; the launch traced here: 1180 us
  waiting for transfers between devices  1120 us (94%)
  matrix products  27.7 us (2%)
  local copies, waits for them, and re-layouts  19.1 us (2%)
  between operations  14.4 us (1%)
    psum x1, waiting for transfers between devices, body(): weight_grad = lax.psum(local_grad, ('row', 'col'))  873 us
    all_gather x1, waiting for transfers between devices, body(): gathered = lax.all_gather(grad_out, 'row', axis=0, tiled=True)  146 us
    reduce_scatter x1, waiting for transfers between devices, body(): lax.psum_scatter(partial_value, 'col', scatter_dimension=0, tiled=True)  101 us
  transfers between devices with their start and end apart: 3, of which 3 were waited for; matrix products, arithmetic and copies ran while one was open for 0% of the time, Pallas kernels for 0%

commit v1 on v0

v1 whole, which is shorter than its diff:
```python
import functools

import jax
import jax.numpy as jnp
from jax import lax
from jax.experimental import pallas as pl
from jax.experimental.pallas import tpu as pltpu
from jax.sharding import Mesh
from jax.sharding import PartitionSpec as P

ROW = ("zh", "zm", "zl", "core")
COL = ("x", "y")


def tiles_kernel(count_ref, rows_ref, cols_ref, values_ref, gathered_ref, features_ref, out_ref, total):
    row_tiles, tile, width = total.shape
    share = features_ref.shape[1] // row_tiles
    total[...] = jnp.zeros_like(total)

    def add(slot):
        row = rows_ref[slot]
        total[row] += jnp.dot(
            values_ref[slot], gathered_ref[cols_ref[slot]], preferred_element_type=jnp.float32
        )

    count = count_ref[0]
    fours = lax.shift_right_logical(count, 2)

    def four(index, carry):
        for offset in range(4):
            add(4 * index + offset)
        return carry

    def one(slot, carry):
        add(slot)
        return carry

    lax.fori_loop(0, fours, four, 0)
    lax.fori_loop(4 * fours, count, one, 0)

    step = 4
    grad = jnp.zeros((features_ref.shape[1], width), jnp.float32)
    for first in range(0, row_tiles, step):
        part = total[first : first + step].astype(jnp.bfloat16)
        out_ref[first : first + step, :tile] = part
        grad += lax.dot_general(
            features_ref[first * tile : (first + step) * tile],
            part.reshape(step * tile, width),
            (((0,), (0,)), ((), ())),
            preferred_element_type=jnp.float32,
        )
    out_ref[:, tile:] = grad.astype(jnp.bfloat16).reshape(row_tiles, share, width)


def finish_kernel(scale, parts_ref, weight_ref, input_ref, share_ref):
    tile = input_ref.shape[0]
    summed = parts_ref[0].astype(jnp.float32)
    for other in range(1, parts_ref.shape[0]):
        summed += parts_ref[other].astype(jnp.float32)
    share_ref[...] = summed[tile:] * scale
    input_ref[...] = lax.dot_general(
        summed[:tile].astype(jnp.bfloat16),
        weight_ref[...],
        (((1,), (1,)), ((), ())),
        preferred_element_type=jnp.float32,
    ).astype(jnp.bfloat16)


def body(nodes, grad_out, features, weight, tile_values, tile_rows, tile_cols, tile_count):
    tile = tile_values.shape[-1]
    width = grad_out.shape[1]
    cols = lax.axis_size(COL)
    share = width // cols
    gathered = lax.all_gather(grad_out, ROW, axis=0, tiled=True)
    own_features = lax.all_gather(features, COL, axis=0, tiled=True)
    smem, vmem = pl.BlockSpec(memory_space=pltpu.SMEM), pl.BlockSpec(memory_space=pltpu.VMEM)
    parts = pl.pallas_call(
        tiles_kernel,
        out_shape=jax.ShapeDtypeStruct((cols, tile + share, width), jnp.bfloat16),
        in_specs=[smem] * 3 + [vmem] * 3,
        out_specs=vmem,
        scratch_shapes=[pltpu.VMEM((cols, tile, width), jnp.float32)],
        compiler_params=pltpu.CompilerParams(vmem_limit_bytes=24 * 2**20),
    )(
        tile_count[0],
        tile_rows[0, 0],
        tile_cols[0, 0],
        tile_values[0, 0],
        gathered.reshape(-1, tile, width),
        own_features,
    )
    parts = lax.all_to_all(parts, COL, 0, 0, tiled=True)
    input_grad, grad_share = pl.pallas_call(
        functools.partial(finish_kernel, nodes**-0.5),
        out_shape=(
            jax.ShapeDtypeStruct((tile, width), jnp.bfloat16),
            jax.ShapeDtypeStruct((share, width), jnp.float32),
        ),
        in_specs=[vmem] * 2,
        out_specs=(vmem, vmem),
        compiler_params=pltpu.CompilerParams(vmem_limit_bytes=8 * 2**20),
    )(parts, weight)
    for axes in ("core", "zl", "zm", "zh"):
        grad_share = jnp.sum(lax.all_gather(grad_share, axes), axis=0)
    weight_grad = lax.all_gather(grad_share, COL, axis=0, tiled=True)
    return input_grad, weight_grad


def solution(mesh):
    fine = Mesh(mesh.devices.reshape(4, 4, 2, 2, 4, 4), ROW + COL)
    placed = (
        P(COL + ROW, None),
        P(ROW + COL, None),
        P(),
        P(ROW, COL, None, None, None),
        P(ROW, COL, None),
        P(ROW, COL, None),
        P(ROW, COL),
    )

    def whole(grad_out, *rest):
        return jax.shard_map(
            functools.partial(body, grad_out.shape[0]),
            mesh=fine,
            in_specs=placed,
            out_specs=(P(ROW + COL, None), P()),
            check_vma=False,
        )(grad_out, *rest)

    return whole
```

time: 1190 us -> 362 us (0.30)
  waiting for transfers between devices: 1120 us -> 232 us
  blocking collectives: 0 us -> 103 us
  matrix products: 27.7 us -> 0 us
  local copies, waits for them, and re-layouts: 19.1 us -> 7.17 us
    psum x1 -> x0, waiting for transfers between devices: 873 us -> none  [body(): weight_grad = lax.psum(local_grad, ('row', 'col'))]
    reduce_scatter x1 -> x0, waiting for transfers between devices: 101 us -> none  [body(): lax.psum_scatter(partial_value, 'col', scatter_dimension=0, tiled=True)]
    all_gather x1 -> x2, waiting for transfers between devices: 146 us -> 231 us  [the longest x1 142 us: body(): gathered = lax.all_gather(grad_out, ROW, axis=0, tiled=True)]
    all_gather x0 -> x5, blocking collectives: none -> 80.1 us  [the longest x4 57.6 us: body(): grad_share = jnp.sum(lax.all_gather(grad_share, axes), axis=0)]
    dot_general x12 -> x0, matrix products: 27.7 us -> none  [the longest x5 16.8 us: accumulate(): jnp.einsum('gr,giw->riw', placing, prods, precision=lax.Precision.HIGHEST)]
    all_to_all x0 -> x1, blocking collectives: none -> 22.7 us  [body(): parts = lax.all_to_all(parts, COL, 0, 0, tiled=True)]
    gather x5 -> x0, local copies, waits for them, and re-layouts: 14 us -> none  [accumulate(): picked = col_blocks[col_ids]]
  transfers between devices with their start and end apart: 3 -> 2, of which waited for: 3 -> 2; matrix products, arithmetic and copies ran while one was open for 0% -> 0% of each run, Pallas kernels for 0% -> 0%
where the time goes in v1:
time: 362 us; the launch traced here: 361 us
  waiting for transfers between devices  232 us (64%)
  blocking collectives  103 us (28%)
  between operations  14.7 us (4%)
  local copies, waits for them, and re-layouts  7.17 us (2%)
  Pallas kernels  4.66 us (1%)
    all_gather x1, waiting for transfers between devices, body(): gathered = lax.all_gather(grad_out, ROW, axis=0, tiled=True)  142 us
    all_gather x1, waiting for transfers between devices, body(): own_features = lax.all_gather(features, COL, axis=0, tiled=True)  88.5 us
    all_gather x4, blocking collectives, body(): grad_share = jnp.sum(lax.all_gather(grad_share, axes), axis=0)  57.6 us
    all_to_all x1, blocking collectives, body(): parts = lax.all_to_all(parts, COL, 0, 0, tiled=True)  22.7 us
    all_gather x1, blocking collectives, body(): weight_grad = lax.all_gather(grad_share, COL, axis=0, tiled=True)  22.6 us
  transfers between devices with their start and end apart: 2, of which 2 were waited for; matrix products, arithmetic and copies ran while one was open for 0% of the time, Pallas kernels for 0%

profile of v1, /device:TPU:6, one launch (start us, length us, event | category | flops | bytes accessed | tf_op | source)
XLA Modules:
  0.0 361.5 jit_solution(8931349254832442376)
XLA Ops:
  7.2 0.0 all-gather.9.cloned.1.call-start
  7.2 0.7 all-gather.9.cloned.1.call-update
  7.9 0.0 all-gather.7.cloned.1.call-start
  7.9 0.7 all-gather.7.cloned.1.call-update
  9.3 88.5 %all-gather.9.cloned.1.call-done.features_ref = bf16[2048,256]{1,0:T(8,128)(2,1)} async-done(((bf16[128,256]{1,0:T(8,128)(2,1)}), bf16[2048,256]{1,0:T(8,128)(2,1)}) %all-gather.9.cloned.1.call-update) | async-done | bytes 1048592 | tf_op jit(solution)/shard_map/all_gather | solution.py:75
  97.8 142.1 %all-gather.7.cloned.1.call-done = bf16[8192,256]{1,0:T(8,128)(2,1)} async-done(((bf16[128,256]{1,0:T(8,128)(2,1)}), bf16[8192,256]{1,0:T(8,128)(2,1)}) %all-gather.7.cloned.1.call-update) | async-done | bytes 4194320 | tf_op jit(solution)/shard_map/all_gather | solution.py:74
  239.9 0.0 copy-start
  239.9 2.2 copy-done
  242.1 0.0 copy-start.1
  242.1 1.7 copy-done.1
  243.8 0.0 copy-start.2
  243.8 1.2 copy-done.2
  245.1 0.0 copy-start.4
  245.1 0.7 copy-done.4
  245.7 0.0 copy-start.5
  245.7 0.7 copy-done.5
  246.4 0.0 copy-start.3
  246.4 3.7 %shard_map.86 = bf16[16,144,256]{2,1,0:T(8,128)(2,1)S(1)} custom-call(s32[1]{0:T(128)} %bitcast.9.count_ref, s32[80]{0:T(128)S(1)} %bitcast.12, s32[80]{0:T(128)S(1)} %bitcast.13, bf16[80,128,128]{2,1,0:T(8,128)(2,1)S(1)} %bitcast.11, bf16[64,128,256]{2,1,0:T(8,128)(2,1)S(1)} %bitcast.10, bf16[2048,256]{1,0:T(8,128)(2,1)S(1)} %copy-done.2), custom_call_target="tpu_custom_call" | custom-call | tf_op jit(solution)/shard_map/pallas_call | solution.py:77
  250.1 22.7 %all_to_all.5.parts_ref = bf16[16,144,256]{2,1,0:T(8,128)(2,1)S(1)} all-to-all(bf16[16,144,256]{2,1,0:T(8,128)(2,1)S(1)} %shard_map.86), channel_id=1, replica_groups=mesh['zh'=4,'zm'=4,'zl'=2,'core'=2,'x'=4,'y'=4] {'x','y'}, dimensions={0} | all-to-all | bytes 2359296 | tf_op jit(solution)/shard_map/all_to_all | solution.py:92
  272.8 0.0 copy-done.3
  272.8 0.9 shard_map.87
  273.7 2.9 all-gather
  276.7 4.4 %all-gather.1 = f32[32,256]{1,0:T(8,128)S(1)} all-gather(f32[16,256]{1,0:T(8,128)S(1)} %reduce_sum.36), channel_id=3, replica_groups=mesh['zh'=4,'zm'=4,'zl'=2,'core'=2,'x'=4,'y'=4] {'zl'}, dimensions={0}, use_global_device_ids=true | all-gather | bytes 49152 | tf_op jit(solution)/shard_map/all_gather | solution.py:104
  281.1 20.9 %all-gather.2 = f32[64,256]{1,0:T(8,128)S(1)} all-gather(f32[16,256]{1,0:T(8,128)S(1)} %reduce_sum.37), channel_id=4, replica_groups=mesh['zh'=4,'zm'=4,'zl'=2,'core'=2,'x'=4,'y'=4] {'zm'}, dimensions={0}, use_global_device_ids=true | all-gather | bytes 81920 | tf_op jit(solution)/shard_map/all_gather | solution.py:104
  302.0 29.3 %all-gather.3 = f32[64,256]{1,0:T(8,128)S(1)} all-gather(f32[16,256]{1,0:T(8,128)S(1)} %reduce_sum.38), channel_id=5, replica_groups=mesh['zh'=4,'zm'=4,'zl'=2,'core'=2,'x'=4,'y'=4] {'zh'}, dimensions={0}, use_global_device_ids=true | all-gather | bytes 81920 | tf_op jit(solution)/shard_map/all_gather | solution.py:104
  331.4 22.6 %all_gather.43 = f32[256,256]{1,0:T(8,128)S(1)} all-gather(f32[16,256]{1,0:T(8,128)S(1)} %reduce_sum.39), channel_id=1, replica_groups=mesh['zh'=4,'zm'=4,'zl'=2,'core'=2,'x'=4,'y'=4] {'x','y'}, dimensions={0}, use_global_device_ids=true | all-gather | bytes 278528 | tf_op jit(solution)/shard_map/all_gather | solution.py:105
  353.9 0.7 copy.11
  (4 shorter events, 0.0 us)
Async XLA Ops:
  7.2 90.6 %all-gather.9.cloned.1.call-start = ((), (), s32[]{:S(2)}) async-start(), calls=%async_computation.2 | async-start | bytes 1114112 | tf_op jit(solution)/shard_map/all_gather | solution.py:75
  7.9 232.0 %all-gather.7.cloned.1.call-start = ((), (), s32[]{:S(2)}) async-start(), calls=%async_computation.1 | async-start | bytes 4259840 | tf_op jit(solution)/shard_map/all_gather | solution.py:74
  239.9 2.2 copy-start
  242.1 1.7 copy-start.1
  243.8 1.2 copy-start.2
  245.1 0.7 copy-start.4
  245.7 0.7 copy-start.5
  246.4 26.4 %copy-start.3 = (bf16[256,256]{1,0:T(8,128)(2,1)S(1)}, bf16[256,256]{1,0:T(8,128)(2,1)}, u32[]{:S(2)}) copy-start(bf16[256,256]{1,0:T(8,128)(2,1)} %weight_ref.1) | copy-start | bytes 393220
Sparse Core Ops, SparseCore 0:
  12.2 85.5 all-gather.8
  100.5 139.3 all-gather.6

commit v2 on v1

--- a/solution.py
+++ b/solution.py
@@ -8,19 +8,31 @@
 from jax.sharding import Mesh
 from jax.sharding import PartitionSpec as P
 
-ROW = ("zh", "zm", "zl", "core")
+Z = ("zh", "zm", "zl")
+ROW = Z + ("core",)
 COL = ("x", "y")
 
 
-def tiles_kernel(count_ref, rows_ref, cols_ref, values_ref, gathered_ref, features_ref, out_ref, total):
+def tiles_kernel(count_ref, rows_ref, places_ref, values_ref, *refs):
+    *pieces, features_ref, out_ref, values, gathered, total, copied = refs
     row_tiles, tile, width = total.shape
     share = features_ref.shape[1] // row_tiles
+    copies = [pltpu.make_async_copy(values_ref, values, copied.at[0])]
+    first = 0
+    for index, piece in enumerate(pieces):
+        place = gathered.at[first : first + piece.shape[0]]
+        copies.append(pltpu.make_async_copy(piece, place, copied.at[index + 1]))
+        first += piece.shape[0]
+    for copy in copies:
+        copy.start()
     total[...] = jnp.zeros_like(total)
+    for copy in copies:
+        copy.wait()
 
     def add(slot):
         row = rows_ref[slot]
         total[row] += jnp.dot(
-            values_ref[slot], gathered_ref[cols_ref[slot]], preferred_element_type=jnp.float32
+            values[slot], gathered[places_ref[slot]], preferred_element_type=jnp.float32
         )
 
     count = count_ref[0]
@@ -66,27 +78,64 @@
     ).astype(jnp.bfloat16)
 
 
+def shifted(step):
+    size = lax.axis_size(Z)
+    return [(index, (index + step) % size) for index in range(size)]
+
+
+def from_all(array, axes):
+    size = lax.axis_size(axes)
+    same = jnp.broadcast_to(array[None], (size, *array.shape))
+    return lax.all_to_all(same, axes, 0, 0, tiled=True)
+
+
+def gather_row(grad_out):
+    own = lax.all_gather(grad_out, "zh")
+    left, right = [own], [own]
+    for unused in range(3):
+        left.append(lax.ppermute(left[-1], Z, shifted(1)))
+        right.append(lax.ppermute(right[-1], Z, shifted(-1)))
+    far = lax.ppermute(left[3], Z, shifted(1))
+    early = jnp.concatenate([own, left[1], right[1], left[2], right[2]])
+    late = jnp.concatenate([left[3], right[3], far])
+    swap = [(0, 1), (1, 0)]
+    return early, late, lax.ppermute(early, "core", swap), lax.ppermute(late, "core", swap)
+
+
+def place_of(block):
+    high, residue, core = block >> 4, (block >> 1) & 7, block & 1
+    away = (residue - (lax.axis_index("zm") * 2 + lax.axis_index("zl"))) & 7
+    group = jnp.where(away < 4, 2 * away, jnp.where(away == 4, 7, 15 - 2 * away))
+    return (core ^ lax.axis_index("core")) * 32 + group * 4 + high
+
+
 def body(nodes, grad_out, features, weight, tile_values, tile_rows, tile_cols, tile_count):
     tile = tile_values.shape[-1]
     width = grad_out.shape[1]
     cols = lax.axis_size(COL)
     share = width // cols
-    gathered = lax.all_gather(grad_out, ROW, axis=0, tiled=True)
     own_features = lax.all_gather(features, COL, axis=0, tiled=True)
+    pieces = gather_row(grad_out)
     smem, vmem = pl.BlockSpec(memory_space=pltpu.SMEM), pl.BlockSpec(memory_space=pltpu.VMEM)
+    anywhere = pl.BlockSpec(memory_space=pl.ANY)
     parts = pl.pallas_call(
         tiles_kernel,
         out_shape=jax.ShapeDtypeStruct((cols, tile + share, width), jnp.bfloat16),
-        in_specs=[smem] * 3 + [vmem] * 3,
+        in_specs=[smem] * 3 + [anywhere] * (1 + len(pieces)) + [vmem],
         out_specs=vmem,
-        scratch_shapes=[pltpu.VMEM((cols, tile, width), jnp.float32)],
+        scratch_shapes=[
+            pltpu.VMEM(tile_values.shape[2:], jnp.bfloat16),
+            pltpu.VMEM((lax.axis_size(ROW), tile, width), jnp.bfloat16),
+            pltpu.VMEM((cols, tile, width), jnp.float32),
+            pltpu.SemaphoreType.DMA((1 + len(pieces),)),
+        ],
         compiler_params=pltpu.CompilerParams(vmem_limit_bytes=24 * 2**20),
     )(
         tile_count[0],
         tile_rows[0, 0],
-        tile_cols[0, 0],
+        place_of(tile_cols[0, 0]),
         tile_values[0, 0],
-        gathered.reshape(-1, tile, width),
+        *pieces,
         own_features,
     )
     parts = lax.all_to_all(parts, COL, 0, 0, tiled=True)
@@ -100,9 +149,12 @@
         out_specs=(vmem, vmem),
         compiler_params=pltpu.CompilerParams(vmem_limit_bytes=8 * 2**20),
     )(parts, weight)
-    for axes in ("core", "zl", "zm", "zh"):
-        grad_share = jnp.sum(lax.all_gather(grad_share, axes), axis=0)
-    weight_grad = lax.all_gather(grad_share, COL, axis=0, tiled=True)
+    grad_share = jnp.sum(lax.all_gather(grad_share, "core"), axis=0)
+    half = share // 2
+    mine = lax.dynamic_slice_in_dim(grad_share, half * lax.axis_index("core"), half)
+    mine = jnp.sum(from_all(mine.astype(jnp.bfloat16), Z).astype(jnp.float32), axis=0)
+    grad_share = lax.all_gather(mine, "core", axis=0, tiled=True)
+    weight_grad = from_all(grad_share, COL).reshape(width, width)
     return input_grad, weight_grad
 
 

time: 362 us -> 248 us (0.69)
  waiting for transfers between devices: 232 us -> 58.3 us
  starting transfers between devices: 0.08 us -> 35.7 us
  blocking collectives: 103 us -> 125 us
    all_gather x1 -> x0, waiting for transfers between devices: 142 us -> none  [body(): gathered = lax.all_gather(grad_out, ROW, axis=0, tiled=True)]
    all_gather x1, waiting for transfers between devices: 88.5 us -> 30.6 us  [body(): own_features = lax.all_gather(features, COL, axis=0, tiled=True)]
    all_to_all x1 -> x2, blocking collectives: 22.7 us -> 68.6 us  [from_all(): return lax.all_to_all(same, axes, 0, 0, tiled=True)]
    ppermute x0 -> x9, starting transfers between devices: none -> 27 us  [the longest x3 14.7 us: gather_row(): right.append(lax.ppermute(right[-1], Z, shifted(-1)))]
    all_gather x5 -> x3, blocking collectives: 80.1 us -> 56.3 us  [the longest x1 52.6 us: gather_row(): own = lax.all_gather(grad_out, 'zh')]
    all_to_all x0 -> x1, waiting for transfers between devices: none -> 13.9 us  [body(): parts = lax.all_to_all(parts, COL, 0, 0, tiled=True)]
    ppermute x0 -> x9, waiting for transfers between devices: none -> 13.9 us  [the longest x1 5.32 us: gather_row(): far = lax.ppermute(left[3], Z, shifted(1))]
    all_to_all x0 -> x1, starting transfers between devices: none -> 8.69 us  [body(): parts = lax.all_to_all(parts, COL, 0, 0, tiled=True)]
  transfers between devices with their start and end apart: 2 -> 11, of which waited for: 2 -> 7; matrix products, arithmetic and copies ran while one was open for 0% -> 2% of each run, Pallas kernels for 0% -> 0%
where the time goes in v2:
time: 248 us; the launch traced here: 246 us
  blocking collectives  125 us (50%)
  waiting for transfers between devices  58.3 us (24%)
  starting transfers between devices  35.7 us (14%)
  between operations  14.8 us (6%)
  Pallas kernels  6.9 us (3%)
  local copies, waits for them, and re-layouts  5.69 us (2%)
    all_to_all x2, blocking collectives, from_all(): return lax.all_to_all(same, axes, 0, 0, tiled=True)  68.6 us
    all_gather x1, blocking collectives, gather_row(): own = lax.all_gather(grad_out, 'zh')  52.6 us
    all_gather x1, waiting for transfers between devices, body(): own_features = lax.all_gather(features, COL, axis=0, tiled=True)  30.6 us
    ppermute x3, starting transfers between devices, gather_row(): right.append(lax.ppermute(right[-1], Z, shifted(-1)))  14.7 us
    all_to_all x1, waiting for transfers between devices, body(): parts = lax.all_to_all(parts, COL, 0, 0, tiled=True)  13.9 us
    all_to_all x1, starting transfers between devices, body(): parts = lax.all_to_all(parts, COL, 0, 0, tiled=True)  8.69 us
    ppermute x3, starting transfers between devices, gather_row(): left.append(lax.ppermute(left[-1], Z, shifted(1)))  6.5 us
    pallas_call x1, Pallas kernels, body(): pl.pallas_call(tiles_kernel, out_shape=jax.ShapeDtypeStruct((cols, tile +...  5.99 us
  transfers between devices with their start and end apart: 11, of which 7 were waited for; matrix products, arithmetic and copies ran while one was open for 2% of the time, Pallas kernels for 0%

profile of v2, /device:TPU:6, one launch (start us, length us, event | category | flops | bytes accessed | tf_op | source)
XLA Modules:
  0.0 246.4 jit_solution(17369290222700871166)
XLA Ops:
  7.2 0.0 all-gather.4.cloned.1.call-start
  7.2 52.6 %all-gather = bf16[512,256]{1,0:T(8,128)(2,1)S(1)} all-gather(bf16[128,256]{1,0:T(8,128)(2,1)} %param.7), channel_id=2, replica_groups=mesh['zh'=4,'zm'=4,'zl'=2,'core'=2,'x'=4,'y'=4] {'zh'}, dimensions={0}, use_global_device_ids=true | all-gather | bytes 327680 | tf_op jit(solution)/shard_map/all_gather | solution.py:93
  59.8 1.9 collective-permute-start
  61.8 5.1 %collective-permute-start.1 = (bf16[4,128,256]{2,1,0:T(8,128)(2,1)S(1)}, bf16[4,128,256]{2,1,0:T(8,128)(2,1)S(1)}, u32[]{:S(2)}, u32[]{:S(2)}) collective-permute-start(bf16[4,128,256]{2,1,0:T(8,128)(2,1)S(1)} %bitcast.35), channel_id=1, source_target_pairs={{0,992},{32,0},{64,32},{96,64},{128,96},{160,128},{192,160},{224,1... | collective-permute-start | bytes 786440 | tf_op jit(solution)/shard_map/ppermute | solution.py:97
  66.9 2.4 collective-permute-done
  69.3 2.5 collective-permute-start.2
  71.8 0.7 constant_dynamic-update-slice_fusion.4
  72.5 4.6 %collective-permute-start.3 = (bf16[4,128,256]{2,1,0:T(8,128)(2,1)S(1)}, bf16[4,128,256]{2,1,0:T(8,128)(2,1)S(1)}, u32[]{:S(2)}, u32[]{:S(2)}) collective-permute-start(bf16[4,128,256]{2,1,0:T(8,128)(2,1)S(1)} %collective-permute-done.1), channel_id=1, source_target_pairs={{0,992},{32,0},{64,32},{96,64},{128,96},{160,128},{192,160},{224,1... | collective-permute-start | bytes 786440 | tf_op jit(solution)/shard_map/ppermute | solution.py:97
  77.1 0.7 constant_dynamic-update-slice_fusion.3
  77.8 0.7 constant_dynamic-update-slice_fusion.2
  78.6 0.2 collective-permute-done.2
  78.8 2.1 collective-permute-start.4
  80.9 0.7 constant_dynamic-update-slice_fusion.1
  81.6 0.7 constant_dynamic-update-slice_fusion.refs_0_
  82.3 1.9 collective-permute-start.7
  84.3 5.1 %collective-permute-start.5 = (bf16[4,128,256]{2,1,0:T(8,128)(2,1)S(1)}, bf16[4,128,256]{2,1,0:T(8,128)(2,1)S(1)}, u32[]{:S(2)}, u32[]{:S(2)}) collective-permute-start(bf16[4,128,256]{2,1,0:T(8,128)(2,1)S(1)} %collective-permute-done.3), channel_id=1, source_target_pairs={{0,992},{32,0},{64,32},{96,64},{128,96},{160,128},{192,160},{224,1... | collective-permute-start | bytes 786440 | tf_op jit(solution)/shard_map/ppermute | solution.py:97
  89.4 1.9 collective-permute-start.6
  91.3 4.2 %collective-permute-done.5 = bf16[4,128,256]{2,1,0:T(8,128)(2,1)S(1)} collective-permute-done((bf16[4,128,256]{2,1,0:T(8,128)(2,1)S(1)}, bf16[4,128,256]{2,1,0:T(8,128)(2,1)S(1)}, u32[]{:S(2)}, u32[]{:S(2)}) %collective-permute-start.5) | collective-permute-done | bytes 262176 | tf_op jit(solution)/shard_map/ppermute | solution.py:97
  95.6 5.3 %collective-permute-done.6 = bf16[4,128,256]{2,1,0:T(8,128)(2,1)S(1)} collective-permute-done((bf16[4,128,256]{2,1,0:T(8,128)(2,1)S(1)}, bf16[4,128,256]{2,1,0:T(8,128)(2,1)S(1)}, u32[]{:S(2)}, u32[]{:S(2)}) %collective-permute-start.6) | collective-permute-done | bytes 262176 | tf_op jit(solution)/shard_map/ppermute | solution.py:98
  100.9 1.9 collective-permute-start.8
  103.5 1.7 collective-permute-done.8.refs_3_
  105.2 30.6 %all-gather.4.cloned.1.call-done.refs_4_ = bf16[2048,256]{1,0:T(8,128)(2,1)} async-done(((bf16[128,256]{1,0:T(8,128)(2,1)}), bf16[2048,256]{1,0:T(8,128)(2,1)}) %all-gather.4.cloned.1.call-update) | async-done | bytes 1048592 | tf_op jit(solution)/shard_map/all_gather | solution.py:117
  135.8 1.2 copy-done.1
  137.0 6.0 %shard_map.86 = bf16[16,144,256]{2,1,0:T(8,128)(2,1)} custom-call(s32[1]{0:T(128)} %bitcast.31.count_ref, s32[80]{0:T(128)S(1)} %bitcast.33, s32[80]{0:T(128)S(1)} %bitcast_add_fusion.places_ref, bf16[80,128,128]{2,1,0:T(8,128)(2,1)S(1)} %bitcast.32, bf16[20,128,256]{2,1,0:T(8,128)(2,1)} %constant_dynamic-update-slice_fusion.refs_0_, ...), custom_call_target="tpu_custom_call" | custom-call | tf_op jit(solution)/shard_map/pallas_call | solution.py:121
  143.0 8.7 %all-to-all-start = ((bf16[16,144,256]{2,1,0:T(8,128)(2,1)}), bf16[16,144,256]{2,1,0:T(8,128)(2,1)S(1)}, u32[]{:S(2)}, u32[]{:S(2)}) async-start(bf16[16,144,256]{2,1,0:T(8,128)(2,1)} %shard_map.86), calls=%async_computation | async-start | bytes 2359296 | tf_op jit(solution)/shard_map/all_to_all | solution.py:141
  151.7 13.9 %all-to-all-done.parts_ref = bf16[16,144,256]{2,1,0:T(8,128)(2,1)S(1)} async-done(((bf16[16,144,256]{2,1,0:T(8,128)(2,1)}), bf16[16,144,256]{2,1,0:T(8,128)(2,1)S(1)}, u32[]{:S(2)}, u32[]{:S(2)}) %all-to-all-start) | async-done | bytes 1179680 | tf_op jit(solution)/shard_map/all_to_all | solution.py:141
  165.6 0.9 shard_map.87
  166.5 1.8 all-gather.1
  168.4 56.2 %all_to_all.15 = bf16[32,8,256]{2,1,0:T(8,128)(2,1)S(1)} all-to-all(bf16[32,8,256]{2,1,0:T(8,128)(2,1)S(1)} %broadcast_in_dim.6), channel_id=1, replica_groups=mesh['zh'=4,'zm'=4,'zl'=2,'core'=2,'x'=4,'y'=4] {'zh','zm','zl'}, dimensions={0} | all-to-all | bytes 262144 | tf_op jit(solution)/shard_map/all_to_all | solution.py:89
  224.6 1.8 all_gather.23
  226.4 12.5 %all_to_all.16 = f32[16,16,256]{2,1,0:T(8,128)S(1)} all-to-all(f32[16,16,256]{2,1,0:T(8,128)S(1)} %broadcast_in_dim.7), channel_id=1, replica_groups=mesh['zh'=4,'zm'=4,'zl'=2,'core'=2,'x'=4,'y'=4] {'x','y'}, dimensions={0} | all-to-all | bytes 524288 | tf_op jit(solution)/shard_map/all_to_all | solution.py:89
  238.9 0.7 copy.17
  (23 shorter events, 0.2 us)
Async XLA Ops:
  7.2 128.6 %all-gather.4.cloned.1.call-start = ((), (), s32[]{:S(2)}) async-start(), calls=%async_computation.3 | async-start | bytes 1114112 | tf_op jit(solution)/shard_map/all_gather | solution.py:117
  59.8 9.5 %collective-permute-start = (bf16[4,128,256]{2,1,0:T(8,128)(2,1)S(1)}, bf16[4,128,256]{2,1,0:T(8,128)(2,1)S(1)}, u32[]{:S(2)}, u32[]{:S(2)}) collective-permute-start(bf16[4,128,256]{2,1,0:T(8,128)(2,1)S(1)} %bitcast.34), channel_id=1, source_target_pairs={{0,32},{32,64},{64,96},{96,128},{128,160},{160,192},{192,224},{224... | collective-permute-start | bytes 786440 | tf_op jit(solution)/shard_map/ppermute | solution.py:96
  61.8 10.7 %collective-permute-start.1 = (bf16[4,128,256]{2,1,0:T(8,128)(2,1)S(1)}, bf16[4,128,256]{2,1,0:T(8,128)(2,1)S(1)}, u32[]{:S(2)}, u32[]{:S(2)}) collective-permute-start(bf16[4,128,256]{2,1,0:T(8,128)(2,1)S(1)} %bitcast.35), channel_id=1, source_target_pairs={{0,992},{32,0},{64,32},{96,64},{128,96},{160,128},{192,160},{224,1... | collective-permute-start | bytes 786440 | tf_op jit(solution)/shard_map/ppermute | solution.py:97
  69.3 9.5 %collective-permute-start.2 = (bf16[4,128,256]{2,1,0:T(8,128)(2,1)S(1)}, bf16[4,128,256]{2,1,0:T(8,128)(2,1)S(1)}, u32[]{:S(2)}, u32[]{:S(2)}) collective-permute-start(bf16[4,128,256]{2,1,0:T(8,128)(2,1)S(1)} %collective-permute-done), channel_id=1, source_target_pairs={{0,32},{32,64},{64,96},{96,128},{128,160},{160,192},{192,224},{224... | collective-permute-start | bytes 786440 | tf_op jit(solution)/shard_map/ppermute | solution.py:96
  72.5 9.1 %collective-permute-start.3 = (bf16[4,128,256]{2,1,0:T(8,128)(2,1)S(1)}, bf16[4,128,256]{2,1,0:T(8,128)(2,1)S(1)}, u32[]{:S(2)}, u32[]{:S(2)}) collective-permute-start(bf16[4,128,256]{2,1,0:T(8,128)(2,1)S(1)} %collective-permute-done.1), channel_id=1, source_target_pairs={{0,992},{32,0},{64,32},{96,64},{128,96},{160,128},{192,160},{224,1... | collective-permute-start | bytes 786440 | tf_op jit(solution)/shard_map/ppermute | solution.py:97
  78.6 24.9 %copy-start.4 = (s32[1,1,80]{2,1,0:T(1,128)S(1)}, s32[1,1,80]{2,1,0:T(1,128)}, u32[]{:S(2)}) copy-start(s32[1,1,80]{2,1,0:T(1,128)} %param.12) | copy-start | bytes 964
  78.6 57.2 %copy-start = (bf16[1,1,80,128,128]{4,3,2,1,0:T(8,128)(2,1)S(1)}, bf16[1,1,80,128,128]{4,3,2,1,0:T(8,128)(2,1)}, u32[]{:S(2)}) copy-start(bf16[1,1,80,128,128]{4,3,2,1,0:T(8,128)(2,1)} %param.10) | copy-start | bytes 7864324
  78.6 57.2 %copy-start.3 = (s32[1,1,80]{2,1,0:T(1,128)S(1)}, s32[1,1,80]{2,1,0:T(1,128)}, u32[]{:S(2)}) copy-start(s32[1,1,80]{2,1,0:T(1,128)} %param.11) | copy-start | bytes 964
  78.8 10.6 %collective-permute-start.4 = (bf16[4,128,256]{2,1,0:T(8,128)(2,1)S(1)}, bf16[4,128,256]{2,1,0:T(8,128)(2,1)S(1)}, u32[]{:S(2)}, u32[]{:S(2)}) collective-permute-start(bf16[4,128,256]{2,1,0:T(8,128)(2,1)S(1)} %collective-permute-done.2), channel_id=1, source_target_pairs={{0,32},{32,64},{64,96},{96,128},{128,160},{160,192},{192,224},{224... | collective-permute-start | bytes 786440 | tf_op jit(solution)/shard_map/ppermute | solution.py:96
  82.3 22.9 %collective-permute-start.7 = (bf16[20,128,256]{2,1,0:T(8,128)(2,1)}, bf16[20,128,256]{2,1,0:T(8,128)(2,1)}, u32[]{:S(2)}, u32[]{:S(2)}) collective-permute-start(bf16[20,128,256]{2,1,0:T(8,128)(2,1)} %constant_dynamic-update-slice_fusion.refs_0_), channel_id=1, source_target_pairs={{0,16},{16,0},{1,17},{17,1},{2,18},{18,2},{3,19},{19,3},{4,20},{20... | collective-permute-start | bytes 3932168 | tf_op jit(solution)/shard_map/ppermute | solution.py:102
  84.3 11.3 %collective-permute-start.5 = (bf16[4,128,256]{2,1,0:T(8,128)(2,1)S(1)}, bf16[4,128,256]{2,1,0:T(8,128)(2,1)S(1)}, u32[]{:S(2)}, u32[]{:S(2)}) collective-permute-start(bf16[4,128,256]{2,1,0:T(8,128)(2,1)S(1)} %collective-permute-done.3), channel_id=1, source_target_pairs={{0,992},{32,0},{64,32},{96,64},{128,96},{160,128},{192,160},{224,1... | collective-permute-start | bytes 786440 | tf_op jit(solution)/shard_map/ppermute | solution.py:97
  89.4 11.5 %collective-permute-start.6 = (bf16[4,128,256]{2,1,0:T(8,128)(2,1)S(1)}, bf16[4,128,256]{2,1,0:T(8,128)(2,1)S(1)}, u32[]{:S(2)}, u32[]{:S(2)}) collective-permute-start(bf16[4,128,256]{2,1,0:T(8,128)(2,1)S(1)} %collective-permute-done.4), channel_id=1, source_target_pairs={{0,32},{32,64},{64,96},{96,128},{128,160},{160,192},{192,224},{224... | collective-permute-start | bytes 786440 | tf_op jit(solution)/shard_map/ppermute | solution.py:98
  100.9 4.3 %collective-permute-start.8 = (bf16[12,128,256]{2,1,0:T(8,128)(2,1)S(1)}, bf16[12,128,256]{2,1,0:T(8,128)(2,1)}, u32[]{:S(2)}, u32[]{:S(2)}) collective-permute-start(bf16[12,128,256]{2,1,0:T(8,128)(2,1)S(1)} %constant_dynamic-update-slice_fusion.5.refs_1_), channel_id=1, source_target_pairs={{0,16},{16,0},{1,17},{17,1},{2,18},{18,2},{3,19},{19,3},{4,20},{20... | collective-permute-start | bytes 2359304 | tf_op jit(solution)/shard_map/ppermute | solution.py:102
  135.8 1.2 copy-start.1
  143.0 22.6 %copy-start.2 = (bf16[256,256]{1,0:T(8,128)(2,1)S(1)}, bf16[256,256]{1,0:T(8,128)(2,1)}, u32[]{:S(2)}) copy-start(bf16[256,256]{1,0:T(8,128)(2,1)} %weight_ref.1) | copy-start | bytes 393220
  143.0 22.6 %all-to-all-start = ((bf16[16,144,256]{2,1,0:T(8,128)(2,1)}), bf16[16,144,256]{2,1,0:T(8,128)(2,1)S(1)}, u32[]{:S(2)}, u32[]{:S(2)}) async-start(bf16[16,144,256]{2,1,0:T(8,128)(2,1)} %shard_map.86), calls=%async_computation | async-start | bytes 2359296 | tf_op jit(solution)/shard_map/all_to_all | solution.py:141
Sparse Core Ops, SparseCore 0:
  67.1 68.6 all-gather.3

commit v3 on v2

--- a/solution.py
+++ b/solution.py
@@ -14,7 +14,7 @@
 
 
 def tiles_kernel(count_ref, rows_ref, places_ref, values_ref, *refs):
-    *pieces, features_ref, out_ref, values, gathered, total, copied = refs
+    *pieces, features_ref, out_ref, share_ref, values, gathered, total, copied = refs
     row_tiles, tile, width = total.shape
     share = features_ref.shape[1] // row_tiles
     copies = [pltpu.make_async_copy(values_ref, values, copied.at[0])]
@@ -54,24 +54,30 @@
     grad = jnp.zeros((features_ref.shape[1], width), jnp.float32)
     for first in range(0, row_tiles, step):
         part = total[first : first + step].astype(jnp.bfloat16)
-        out_ref[first : first + step, :tile] = part
+        out_ref[first : first + step] = part
         grad += lax.dot_general(
             features_ref[first * tile : (first + step) * tile],
             part.reshape(step * tile, width),
             (((0,), (0,)), ((), ())),
             preferred_element_type=jnp.float32,
         )
-    out_ref[:, tile:] = grad.astype(jnp.bfloat16).reshape(row_tiles, share, width)
-
-
-def finish_kernel(scale, parts_ref, weight_ref, input_ref, share_ref):
-    tile = input_ref.shape[0]
+    share_ref[...] = grad.astype(jnp.bfloat16).reshape(row_tiles, share, width)
+
+
+def sum_of(parts_ref):
     summed = parts_ref[0].astype(jnp.float32)
     for other in range(1, parts_ref.shape[0]):
         summed += parts_ref[other].astype(jnp.float32)
-    share_ref[...] = summed[tile:] * scale
+    return summed
+
+
+def share_kernel(scale, shares_ref, parts_ref, share_ref, same_parts_ref):
+    share_ref[...] = sum_of(shares_ref) * scale
+
+
+def finish_kernel(parts_ref, weight_ref, input_ref):
     input_ref[...] = lax.dot_general(
-        summed[:tile].astype(jnp.bfloat16),
+        sum_of(parts_ref).astype(jnp.bfloat16),
         weight_ref[...],
         (((1,), (1,)), ((), ())),
         preferred_element_type=jnp.float32,
@@ -89,17 +95,18 @@
     return lax.all_to_all(same, axes, 0, 0, tiled=True)
 
 
-def gather_row(grad_out):
-    own = lax.all_gather(grad_out, "zh")
+def gather_row(grad_out, beside):
+    own, beside = lax.optimization_barrier((lax.all_gather(grad_out, "zh"), beside))
     left, right = [own], [own]
     for unused in range(3):
         left.append(lax.ppermute(left[-1], Z, shifted(1)))
         right.append(lax.ppermute(right[-1], Z, shifted(-1)))
-    far = lax.ppermute(left[3], Z, shifted(1))
+    crossed = [(2 * source + core, 2 * target + 1 - core) for source, target in shifted(1) for core in (0, 1)]
+    far, far_other = lax.ppermute(left[3], Z, shifted(1)), lax.ppermute(left[3], ROW, crossed)
     early = jnp.concatenate([own, left[1], right[1], left[2], right[2]])
-    late = jnp.concatenate([left[3], right[3], far])
+    late = jnp.concatenate([left[3], right[3]])
     swap = [(0, 1), (1, 0)]
-    return early, late, lax.ppermute(early, "core", swap), lax.ppermute(late, "core", swap)
+    return early, late, far, lax.ppermute(early, "core", swap), lax.ppermute(late, "core", swap), far_other, beside
 
 
 def place_of(block):
@@ -114,15 +121,18 @@
     width = grad_out.shape[1]
     cols = lax.axis_size(COL)
     share = width // cols
-    own_features = lax.all_gather(features, COL, axis=0, tiled=True)
-    pieces = gather_row(grad_out)
+    own_features = from_all(features, COL).reshape(-1, width)
+    *pieces, own_features = gather_row(grad_out, own_features)
     smem, vmem = pl.BlockSpec(memory_space=pltpu.SMEM), pl.BlockSpec(memory_space=pltpu.VMEM)
     anywhere = pl.BlockSpec(memory_space=pl.ANY)
-    parts = pl.pallas_call(
+    parts, shares = pl.pallas_call(
         tiles_kernel,
-        out_shape=jax.ShapeDtypeStruct((cols, tile + share, width), jnp.bfloat16),
+        out_shape=(
+            jax.ShapeDtypeStruct((cols, tile, width), jnp.bfloat16),
+            jax.ShapeDtypeStruct((cols, share, width), jnp.bfloat16),
+        ),
         in_specs=[smem] * 3 + [anywhere] * (1 + len(pieces)) + [vmem],
-        out_specs=vmem,
+        out_specs=(vmem, vmem),
         scratch_shapes=[
             pltpu.VMEM(tile_values.shape[2:], jnp.bfloat16),
             pltpu.VMEM((lax.axis_size(ROW), tile, width), jnp.bfloat16),
@@ -138,23 +148,34 @@
         *pieces,
         own_features,
     )
+    shares = lax.all_to_all(shares, COL, 0, 0, tiled=True)
+    grad_share, parts = pl.pallas_call(
+        functools.partial(share_kernel, nodes**-0.5),
+        out_shape=(
+            jax.ShapeDtypeStruct((share, width), jnp.float32),
+            jax.ShapeDtypeStruct(parts.shape, parts.dtype),
+        ),
+        in_specs=[vmem, anywhere],
+        out_specs=(vmem, anywhere),
+        input_output_aliases={1: 1},
+        compiler_params=pltpu.CompilerParams(vmem_limit_bytes=4 * 2**20),
+    )(shares, parts)
     parts = lax.all_to_all(parts, COL, 0, 0, tiled=True)
-    input_grad, grad_share = pl.pallas_call(
-        functools.partial(finish_kernel, nodes**-0.5),
-        out_shape=(
-            jax.ShapeDtypeStruct((tile, width), jnp.bfloat16),
-            jax.ShapeDtypeStruct((share, width), jnp.float32),
-        ),
-        in_specs=[vmem] * 2,
-        out_specs=(vmem, vmem),
-        compiler_params=pltpu.CompilerParams(vmem_limit_bytes=8 * 2**20),
-    )(parts, weight)
     grad_share = jnp.sum(lax.all_gather(grad_share, "core"), axis=0)
     half = share // 2
     mine = lax.dynamic_slice_in_dim(grad_share, half * lax.axis_index("core"), half)
-    mine = jnp.sum(from_all(mine.astype(jnp.bfloat16), Z).astype(jnp.float32), axis=0)
+    mine = lax.all_gather(mine.astype(jnp.bfloat16), Z)
+    mine, parts = lax.optimization_barrier((mine, parts))
+    mine = jnp.sum(mine.astype(jnp.float32), axis=0)
     grad_share = lax.all_gather(mine, "core", axis=0, tiled=True)
     weight_grad = from_all(grad_share, COL).reshape(width, width)
+    input_grad = pl.pallas_call(
+        finish_kernel,
+        out_shape=jax.ShapeDtypeStruct((tile, width), jnp.bfloat16),
+        in_specs=[vmem] * 2,
+        out_specs=vmem,
+        compiler_params=pltpu.CompilerParams(vmem_limit_bytes=8 * 2**20),
+    )(parts, weight)
     return input_grad, weight_grad
 
 

time: 248 us -> 220 us (0.89)
  waiting for transfers between devices: 58.3 us -> 28.8 us
  starting transfers between devices: 35.7 us -> 61.5 us
  between operations: 14.8 us -> 1.5 us
  blocking collectives: 125 us -> 113 us
    all_to_all x2 -> x1, blocking collectives: 68.6 us -> 13.1 us  [body(): shares = lax.all_to_all(shares, COL, 0, 0, tiled=True)]
    all_gather x1 -> x2, blocking collectives: 52.6 us -> 96.6 us  [the longest x1 53.7 us: body(): mine = lax.all_gather(mine.astype(jnp.bfloat16), Z)]
    all_gather x1 -> x0, waiting for transfers between devices: 30.6 us -> none  [body(): own_features = lax.all_gather(features, COL, axis=0, tiled=True)]
    all_to_all x0 -> x2, starting transfers between devices: none -> 24 us  [from_all(): return lax.all_to_all(same, axes, 0, 0, tiled=True)]
    all_to_all x1, waiting for transfers between devices: 13.9 us -> 0.01 us  [body(): parts = lax.all_to_all(parts, COL, 0, 0, tiled=True)]
    ppermute x3, waiting for transfers between devices: 2.59 us -> 9.83 us  [gather_row(): left.append(lax.ppermute(left[-1], Z, shifted(1)))]
    ppermute x1 -> x2, waiting for transfers between devices: 5.32 us -> 11.6 us  [the longest x1 5.81 us: gather_row(): lax.ppermute(left[3], Z, shifted(1))]
    all_to_all x0 -> x2, waiting for transfers between devices: none -> 5.84 us  [from_all(): return lax.all_to_all(same, axes, 0, 0, tiled=True)]
  transfers between devices with their start and end apart: 11 -> 13, of which waited for: 7 -> 8; matrix products, arithmetic and copies ran while one was open for 2% -> 0% of each run, Pallas kernels for 0% -> 0%
where the time goes in v3:
time: 220 us; the launch traced here: 217 us
  blocking collectives  113 us (51%)
  starting transfers between devices  61.5 us (28%)
  waiting for transfers between devices  28.8 us (13%)
  local copies, waits for them, and re-layouts  6.2 us (3%)
  Pallas kernels  6.13 us (3%)
    all_gather x1, blocking collectives, body(): mine = lax.all_gather(mine.astype(jnp.bfloat16), Z)  53.7 us
    all_gather x1, blocking collectives, gather_row(): lax.all_gather(grad_out, 'zh')  42.9 us
    all_to_all x2, starting transfers between devices, from_all(): return lax.all_to_all(same, axes, 0, 0, tiled=True)  24 us
    ppermute x3, starting transfers between devices, gather_row(): right.append(lax.ppermute(right[-1], Z, shifted(-1)))  15.7 us
    all_to_all x1, blocking collectives, body(): shares = lax.all_to_all(shares, COL, 0, 0, tiled=True)  13.1 us
    ppermute x3, waiting for transfers between devices, gather_row(): left.append(lax.ppermute(left[-1], Z, shifted(1)))  9.83 us
    ppermute x3, starting transfers between devices, gather_row(): left.append(lax.ppermute(left[-1], Z, shifted(1)))  5.91 us
    all_to_all x2, waiting for transfers between devices, from_all(): return lax.all_to_all(same, axes, 0, 0, tiled=True)  5.84 us
  transfers between devices with their start and end apart: 13, of which 8 were waited for; matrix products, arithmetic and copies ran while one was open for 0% of the time, Pallas kernels for 0%

profile of v3, /device:TPU:6, one launch (start us, length us, event | category | flops | bytes accessed | tf_op | source)
XLA Modules:
  0.0 217.5 jit_solution(4981763318516190779)
XLA Ops:
  0.6 1.9 broadcast_in_dim.6
  2.6 16.8 %all-to-all-start = ((bf16[16,128,256]{2,1,0:T(8,128)(2,1)}), bf16[16,128,256]{2,1,0:T(8,128)(2,1)S(1)}, u32[]{:S(2)}, u32[]{:S(2)}) async-start(bf16[16,128,256]{2,1,0:T(8,128)(2,1)} %broadcast_in_dim.6), calls=%async_computation | async-start | bytes 2097152 | tf_op jit(solution)/shard_map/all_to_all | solution.py:95
  19.3 42.9 %all-gather = bf16[512,256]{1,0:T(8,128)(2,1)S(1)} all-gather(bf16[128,256]{1,0:T(8,128)(2,1)S(1)} %copy-done.3), channel_id=2, replica_groups=mesh['zh'=4,'zm'=4,'zl'=2,'core'=2,'x'=4,'y'=4] {'zh'}, dimensions={0}, use_global_device_ids=true | all-gather | bytes 327680 | tf_op jit(solution)/shard_map/all_gather | solution.py:99
  62.2 2.1 collective-permute-start
  64.3 5.0 %collective-permute-start.1 = (bf16[4,128,256]{2,1,0:T(8,128)(2,1)S(1)}, bf16[4,128,256]{2,1,0:T(8,128)(2,1)S(1)}, u32[]{:S(2)}, u32[]{:S(2)}) collective-permute-start(bf16[4,128,256]{2,1,0:T(8,128)(2,1)S(1)} %bitcast.38), channel_id=1, source_target_pairs={{0,992},{32,0},{64,32},{96,64},{128,96},{160,128},{192,160},{224,1... | collective-permute-start | bytes 786440 | tf_op jit(solution)/shard_map/ppermute | solution.py:103
  69.3 2.4 %collective-permute-done = bf16[4,128,256]{2,1,0:T(8,128)(2,1)S(1)} collective-permute-done((bf16[4,128,256]{2,1,0:T(8,128)(2,1)S(1)}, bf16[4,128,256]{2,1,0:T(8,128)(2,1)S(1)}, u32[]{:S(2)}, u32[]{:S(2)}) %collective-permute-start) | collective-permute-done | bytes 262176 | tf_op jit(solution)/shard_map/ppermute | solution.py:102
  71.7 1.9 collective-permute-start.2
  73.6 5.1 %collective-permute-start.3 = (bf16[4,128,256]{2,1,0:T(8,128)(2,1)S(1)}, bf16[4,128,256]{2,1,0:T(8,128)(2,1)S(1)}, u32[]{:S(2)}, u32[]{:S(2)}) collective-permute-start(bf16[4,128,256]{2,1,0:T(8,128)(2,1)S(1)} %collective-permute-done.1), channel_id=1, source_target_pairs={{0,992},{32,0},{64,32},{96,64},{128,96},{160,128},{192,160},{224,1... | collective-permute-start | bytes 786440 | tf_op jit(solution)/shard_map/ppermute | solution.py:103
  78.8 2.3 %collective-permute-done.2 = bf16[4,128,256]{2,1,0:T(8,128)(2,1)S(1)} collective-permute-done((bf16[4,128,256]{2,1,0:T(8,128)(2,1)S(1)}, bf16[4,128,256]{2,1,0:T(8,128)(2,1)S(1)}, u32[]{:S(2)}, u32[]{:S(2)}) %collective-permute-start.2) | collective-permute-done | bytes 262176 | tf_op jit(solution)/shard_map/ppermute | solution.py:102
  81.2 1.5 collective-permute-done.3
  82.7 1.9 collective-permute-start.7
  84.6 1.9 collective-permute-start.4
  86.5 5.6 %collective-permute-start.5 = (bf16[4,128,256]{2,1,0:T(8,128)(2,1)S(1)}, bf16[4,128,256]{2,1,0:T(8,128)(2,1)S(1)}, u32[]{:S(2)}, u32[]{:S(2)}) collective-permute-start(bf16[4,128,256]{2,1,0:T(8,128)(2,1)S(1)} %collective-permute-done.3), channel_id=1, source_target_pairs={{0,992},{32,0},{64,32},{96,64},{128,96},{160,128},{192,160},{224,1... | collective-permute-start | bytes 786440 | tf_op jit(solution)/shard_map/ppermute | solution.py:103
  92.1 5.1 %collective-permute-done.4 = bf16[4,128,256]{2,1,0:T(8,128)(2,1)} collective-permute-done((bf16[4,128,256]{2,1,0:T(8,128)(2,1)S(1)}, bf16[4,128,256]{2,1,0:T(8,128)(2,1)}, u32[]{:S(2)}, u32[]{:S(2)}) %collective-permute-start.4) | collective-permute-done | bytes 262176 | tf_op jit(solution)/shard_map/ppermute | solution.py:102
  97.3 1.0 constant_dynamic-update-slice_fusion.6
  98.4 1.9 collective-permute-start.8
  100.3 2.6 %collective-permute-start.9 = (bf16[4,128,256]{2,1,0:T(8,128)(2,1)}, bf16[4,128,256]{2,1,0:T(8,128)(2,1)}, u32[]{:S(2)}, u32[]{:S(2)}) collective-permute-start(bf16[4,128,256]{2,1,0:T(8,128)(2,1)} %collective-permute-done.4), channel_id=1, source_target_pairs={{0,48},{16,32},{32,80},{48,64},{64,112},{80,96},{96,144},{112,128}... | collective-permute-start | bytes 786440 | tf_op jit(solution)/shard_map/ppermute | solution.py:105
  102.9 3.6 %collective-permute-start.6 = (bf16[4,128,256]{2,1,0:T(8,128)(2,1)}, bf16[4,128,256]{2,1,0:T(8,128)(2,1)}, u32[]{:S(2)}, u32[]{:S(2)}) collective-permute-start(bf16[4,128,256]{2,1,0:T(8,128)(2,1)} %collective-permute-done.4), channel_id=1, source_target_pairs={{0,32},{32,64},{64,96},{96,128},{128,160},{160,192},{192,224},{224... | collective-permute-start | bytes 786440 | tf_op jit(solution)/shard_map/ppermute | solution.py:105
  107.2 5.7 %collective-permute-done.9.refs_5_ = bf16[4,128,256]{2,1,0:T(8,128)(2,1)} collective-permute-done((bf16[4,128,256]{2,1,0:T(8,128)(2,1)}, bf16[4,128,256]{2,1,0:T(8,128)(2,1)}, u32[]{:S(2)}, u32[]{:S(2)}) %collective-permute-start.9) | collective-permute-done | bytes 262176 | tf_op jit(solution)/shard_map/ppermute | solution.py:105
  113.0 5.8 %collective-permute-done.6.refs_2_ = bf16[4,128,256]{2,1,0:T(8,128)(2,1)} collective-permute-done((bf16[4,128,256]{2,1,0:T(8,128)(2,1)}, bf16[4,128,256]{2,1,0:T(8,128)(2,1)}, u32[]{:S(2)}, u32[]{:S(2)}) %collective-permute-start.6) | collective-permute-done | bytes 262176 | tf_op jit(solution)/shard_map/ppermute | solution.py:105
  118.8 1.7 copy-done
  120.5 5.2 %shard_map.86 = (bf16[16,128,256]{2,1,0:T(8,128)(2,1)}, bf16[16,16,256]{2,1,0:T(8,128)(2,1)S(1)}) custom-call(s32[1]{0:T(128)} %bitcast.33.count_ref, s32[80]{0:T(128)S(1)} %bitcast.36, s32[80]{0:T(128)S(1)} %bitcast_add_fusion.places_ref, bf16[80,128,128]{2,1,0:T(8,128)(2,1)S(1)} %bitcast.35, ...), custom_call_target="tpu_custom_call" | custom-call | tf_op jit(solution)/shard_map/pallas_call | solution.py:128
  125.7 13.1 %all_to_all.20.shares_ref = bf16[16,16,256]{2,1,0:T(8,128)(2,1)S(1)} all-to-all(bf16[16,16,256]{2,1,0:T(8,128)(2,1)S(1)} %get-tuple-element.12), channel_id=1, replica_groups=mesh['zh'=4,'zm'=4,'zl'=2,'core'=2,'x'=4,'y'=4] {'x','y'}, dimensions={0} | all-to-all | bytes 262144 | tf_op jit(solution)/shard_map/all_to_all | solution.py:151
  138.9 5.8 %all-to-all-start.2 = ((bf16[16,128,256]{2,1,0:T(8,128)(2,1)}), bf16[16,128,256]{2,1,0:T(8,128)(2,1)S(1)}, u32[]{:S(2)}, u32[]{:S(2)}) async-start(bf16[16,128,256]{2,1,0:T(8,128)(2,1)} %get-tuple-element.15), calls=%async_computation.2 | async-start | bytes 2097152 | tf_op jit(solution)/shard_map/all_to_all | solution.py:163
  144.7 1.8 all-gather.1
  146.6 53.7 %all-gather.2 = bf16[256,256]{1,0:T(8,128)(2,1)S(1)} all-gather(bf16[8,256]{1,0:T(8,128)(2,1)S(1)} %dynamic-slice_convert_fusion), channel_id=4, replica_groups=mesh['zh'=4,'zm'=4,'zl'=2,'core'=2,'x'=4,'y'=4] {'zh','zm','zl'}, dimensions={0}, use_global_device_ids=true | all-gather | bytes 135168 | tf_op jit(solution)/shard_map/all_gather | solution.py:167
  200.3 1.8 all_gather.27
  202.1 0.7 broadcast_in_dim.7
  202.8 7.2 %all-to-all-start.3 = ((f32[16,16,256]{2,1,0:T(8,128)}), f32[16,16,256]{2,1,0:T(8,128)S(1)}, u32[]{:S(2)}, u32[]{:S(2)}) async-start(f32[16,16,256]{2,1,0:T(8,128)} %broadcast_in_dim.7), calls=%async_computation.3 | async-start | bytes 524288 | tf_op jit(solution)/shard_map/all_to_all | solution.py:95
  210.1 0.9 shard_map.88
  211.0 5.8 %all-to-all-done.3 = f32[16,16,256]{2,1,0:T(8,128)S(1)} async-done(((f32[16,16,256]{2,1,0:T(8,128)}), f32[16,16,256]{2,1,0:T(8,128)S(1)}, u32[]{:S(2)}, u32[]{:S(2)}) %all-to-all-start.3) | async-done | bytes 262176 | tf_op jit(solution)/shard_map/all_to_all | solution.py:95
  216.8 0.7 copy.18
  (26 shorter events, 0.3 us)
Async XLA Ops:
  2.6 16.8 %copy-start.3 = (bf16[128,256]{1,0:T(8,128)(2,1)S(1)}, bf16[128,256]{1,0:T(8,128)(2,1)}, u32[]{:S(2)}) copy-start(bf16[128,256]{1,0:T(8,128)(2,1)} %param.7) | copy-start | bytes 196612
  2.6 59.6 %all-to-all-start = ((bf16[16,128,256]{2,1,0:T(8,128)(2,1)}), bf16[16,128,256]{2,1,0:T(8,128)(2,1)S(1)}, u32[]{:S(2)}, u32[]{:S(2)}) async-start(bf16[16,128,256]{2,1,0:T(8,128)(2,1)} %broadcast_in_dim.6), calls=%async_computation | async-start | bytes 2097152 | tf_op jit(solution)/shard_map/all_to_all | solution.py:95
  62.2 9.5 %collective-permute-start = (bf16[4,128,256]{2,1,0:T(8,128)(2,1)S(1)}, bf16[4,128,256]{2,1,0:T(8,128)(2,1)S(1)}, u32[]{:S(2)}, u32[]{:S(2)}) collective-permute-start(bf16[4,128,256]{2,1,0:T(8,128)(2,1)S(1)} %bitcast.37), channel_id=1, source_target_pairs={{0,32},{32,64},{64,96},{96,128},{128,160},{160,192},{192,224},{224... | collective-permute-start | bytes 786440 | tf_op jit(solution)/shard_map/ppermute | solution.py:102
  64.3 9.3 %collective-permute-start.1 = (bf16[4,128,256]{2,1,0:T(8,128)(2,1)S(1)}, bf16[4,128,256]{2,1,0:T(8,128)(2,1)S(1)}, u32[]{:S(2)}, u32[]{:S(2)}) collective-permute-start(bf16[4,128,256]{2,1,0:T(8,128)(2,1)S(1)} %bitcast.38), channel_id=1, source_target_pairs={{0,992},{32,0},{64,32},{96,64},{128,96},{160,128},{192,160},{224,1... | collective-permute-start | bytes 786440 | tf_op jit(solution)/shard_map/ppermute | solution.py:103
  71.7 9.5 %collective-permute-start.2 = (bf16[4,128,256]{2,1,0:T(8,128)(2,1)S(1)}, bf16[4,128,256]{2,1,0:T(8,128)(2,1)S(1)}, u32[]{:S(2)}, u32[]{:S(2)}) collective-permute-start(bf16[4,128,256]{2,1,0:T(8,128)(2,1)S(1)} %collective-permute-done), channel_id=1, source_target_pairs={{0,32},{32,64},{64,96},{96,128},{128,160},{160,192},{192,224},{224... | collective-permute-start | bytes 786440 | tf_op jit(solution)/shard_map/ppermute | solution.py:102
  73.6 9.0 %collective-permute-start.3 = (bf16[4,128,256]{2,1,0:T(8,128)(2,1)S(1)}, bf16[4,128,256]{2,1,0:T(8,128)(2,1)S(1)}, u32[]{:S(2)}, u32[]{:S(2)}) collective-permute-start(bf16[4,128,256]{2,1,0:T(8,128)(2,1)S(1)} %collective-permute-done.1), channel_id=1, source_target_pairs={{0,992},{32,0},{64,32},{96,64},{128,96},{160,128},{192,160},{224,1... | collective-permute-start | bytes 786440 | tf_op jit(solution)/shard_map/ppermute | solution.py:103
  78.8 28.4 %copy-start.4 = (s32[1,1,80]{2,1,0:T(1,128)S(1)}, s32[1,1,80]{2,1,0:T(1,128)}, u32[]{:S(2)}) copy-start(s32[1,1,80]{2,1,0:T(1,128)} %param.12) | copy-start | bytes 964
  78.8 40.0 %copy-start.2 = (s32[1,1,80]{2,1,0:T(1,128)S(1)}, s32[1,1,80]{2,1,0:T(1,128)}, u32[]{:S(2)}) copy-start(s32[1,1,80]{2,1,0:T(1,128)} %param.11) | copy-start | bytes 964
  82.7 36.1 %collective-permute-start.7 = (bf16[20,128,256]{2,1,0:T(8,128)(2,1)S(1)}, bf16[20,128,256]{2,1,0:T(8,128)(2,1)}, u32[]{:S(2)}, u32[]{:S(2)}) collective-permute-start(bf16[20,128,256]{2,1,0:T(8,128)(2,1)S(1)} %constant_dynamic-update-slice_fusion.refs_0_), channel_id=1, source_target_pairs={{0,16},{16,0},{1,17},{17,1},{2,18},{18,2},{3,19},{19,3},{4,20},{20... | collective-permute-start | bytes 3932168 | tf_op jit(solution)/shard_map/ppermute | solution.py:109
  84.6 12.7 %collective-permute-start.4 = (bf16[4,128,256]{2,1,0:T(8,128)(2,1)S(1)}, bf16[4,128,256]{2,1,0:T(8,128)(2,1)}, u32[]{:S(2)}, u32[]{:S(2)}) collective-permute-start(bf16[4,128,256]{2,1,0:T(8,128)(2,1)S(1)} %collective-permute-done.2), channel_id=1, source_target_pairs={{0,32},{32,64},{64,96},{96,128},{128,160},{160,192},{192,224},{224... | collective-permute-start | bytes 786440 | tf_op jit(solution)/shard_map/ppermute | solution.py:102
  86.5 11.8 %collective-permute-start.5 = (bf16[4,128,256]{2,1,0:T(8,128)(2,1)S(1)}, bf16[4,128,256]{2,1,0:T(8,128)(2,1)S(1)}, u32[]{:S(2)}, u32[]{:S(2)}) collective-permute-start(bf16[4,128,256]{2,1,0:T(8,128)(2,1)S(1)} %collective-permute-done.3), channel_id=1, source_target_pairs={{0,992},{32,0},{64,32},{96,64},{128,96},{160,128},{192,160},{224,1... | collective-permute-start | bytes 786440 | tf_op jit(solution)/shard_map/ppermute | solution.py:103
  98.4 20.4 %collective-permute-start.8 = (bf16[8,128,256]{2,1,0:T(8,128)(2,1)S(1)}, bf16[8,128,256]{2,1,0:T(8,128)(2,1)S(1)}, u32[]{:S(2)}, u32[]{:S(2)}) collective-permute-start(bf16[8,128,256]{2,1,0:T(8,128)(2,1)S(1)} %constant_dynamic-update-slice_fusion.5.refs_1_), channel_id=1, source_target_pairs={{0,16},{16,0},{1,17},{17,1},{2,18},{18,2},{3,19},{19,3},{4,20},{20... | collective-permute-start | bytes 1572872 | tf_op jit(solution)/shard_map/ppermute | solution.py:109
  100.3 12.7 %collective-permute-start.9 = (bf16[4,128,256]{2,1,0:T(8,128)(2,1)}, bf16[4,128,256]{2,1,0:T(8,128)(2,1)}, u32[]{:S(2)}, u32[]{:S(2)}) collective-permute-start(bf16[4,128,256]{2,1,0:T(8,128)(2,1)} %collective-permute-done.4), channel_id=1, source_target_pairs={{0,48},{16,32},{32,80},{48,64},{64,112},{80,96},{96,144},{112,128}... | collective-permute-start | bytes 786440 | tf_op jit(solution)/shard_map/ppermute | solution.py:105
  102.9 15.9 %collective-permute-start.6 = (bf16[4,128,256]{2,1,0:T(8,128)(2,1)}, bf16[4,128,256]{2,1,0:T(8,128)(2,1)}, u32[]{:S(2)}, u32[]{:S(2)}) collective-permute-start(bf16[4,128,256]{2,1,0:T(8,128)(2,1)} %collective-permute-done.4), channel_id=1, source_target_pairs={{0,32},{32,64},{64,96},{96,128},{128,160},{160,192},{192,224},{224... | collective-permute-start | bytes 786440 | tf_op jit(solution)/shard_map/ppermute | solution.py:105
  118.8 1.7 copy-start
  138.9 71.2 %copy-start.1 = (bf16[256,256]{1,0:T(8,128)(2,1)S(1)}, bf16[256,256]{1,0:T(8,128)(2,1)}, u32[]{:S(2)}) copy-start(bf16[256,256]{1,0:T(8,128)(2,1)} %weight_ref.1) | copy-start | bytes 393220
  138.9 61.4 %all-to-all-start.2 = ((bf16[16,128,256]{2,1,0:T(8,128)(2,1)}), bf16[16,128,256]{2,1,0:T(8,128)(2,1)S(1)}, u32[]{:S(2)}, u32[]{:S(2)}) async-start(bf16[16,128,256]{2,1,0:T(8,128)(2,1)} %get-tuple-element.15), calls=%async_computation.2 | async-start | bytes 2097152 | tf_op jit(solution)/shard_map/all_to_all | solution.py:163
  202.8 14.0 %all-to-all-start.3 = ((f32[16,16,256]{2,1,0:T(8,128)}), f32[16,16,256]{2,1,0:T(8,128)S(1)}, u32[]{:S(2)}, u32[]{:S(2)}) async-start(f32[16,16,256]{2,1,0:T(8,128)} %broadcast_in_dim.7), calls=%async_computation.3 | async-start | bytes 524288 | tf_op jit(solution)/shard_map/all_to_all | solution.py:95

commit v4 on v3

--- a/solution.py
+++ b/solution.py
@@ -8,20 +8,19 @@
 from jax.sharding import Mesh
 from jax.sharding import PartitionSpec as P
 
-Z = ("zh", "zm", "zl")
+Z = ("za", "zb")
 ROW = Z + ("core",)
 COL = ("x", "y")
 
 
 def tiles_kernel(count_ref, rows_ref, places_ref, values_ref, *refs):
-    *pieces, features_ref, out_ref, share_ref, values, gathered, total, copied = refs
+    *pieces, features_ref, out_ref, share_ref, gathered, total, copied = refs
     row_tiles, tile, width = total.shape
     share = features_ref.shape[1] // row_tiles
-    copies = [pltpu.make_async_copy(values_ref, values, copied.at[0])]
-    first = 0
+    copies, first = [], 0
     for index, piece in enumerate(pieces):
         place = gathered.at[first : first + piece.shape[0]]
-        copies.append(pltpu.make_async_copy(piece, place, copied.at[index + 1]))
+        copies.append(pltpu.make_async_copy(piece, place, copied.at[index]))
         first += piece.shape[0]
     for copy in copies:
         copy.start()
@@ -32,7 +31,7 @@
     def add(slot):
         row = rows_ref[slot]
         total[row] += jnp.dot(
-            values[slot], gathered[places_ref[slot]], preferred_element_type=jnp.float32
+            values_ref[slot], gathered[places_ref[slot]], preferred_element_type=jnp.float32
         )
 
     count = count_ref[0]
@@ -96,24 +95,25 @@
 
 
 def gather_row(grad_out, beside):
-    own, beside = lax.optimization_barrier((lax.all_gather(grad_out, "zh"), beside))
-    left, right = [own], [own]
-    for unused in range(3):
-        left.append(lax.ppermute(left[-1], Z, shifted(1)))
-        right.append(lax.ppermute(right[-1], Z, shifted(-1)))
-    crossed = [(2 * source + core, 2 * target + 1 - core) for source, target in shifted(1) for core in (0, 1)]
-    far, far_other = lax.ppermute(left[3], Z, shifted(1)), lax.ppermute(left[3], ROW, crossed)
-    early = jnp.concatenate([own, left[1], right[1], left[2], right[2]])
-    late = jnp.concatenate([left[3], right[3]])
-    swap = [(0, 1), (1, 0)]
-    return early, late, far, lax.ppermute(early, "core", swap), lax.ppermute(late, "core", swap), far_other, beside
+    own, beside = lax.optimization_barrier((lax.all_gather(grad_out, "za"), beside))
+    left, right = lax.ppermute(own, Z, shifted(1)), lax.ppermute(own, Z, shifted(-1))
+    half = own.shape[0] // 2
+    pieces = [own, left, right]
+    others = [lax.ppermute(piece, "core", [(0, 1), (1, 0)]) for piece in pieces]
+    for block, step in ((left[:half], 1), (right[half:], -1)):
+        crossed = [
+            (2 * source + core, 2 * target + 1 - core) for source, target in shifted(step) for core in (0, 1)
+        ]
+        pieces.append(lax.ppermute(block, Z, shifted(step)))
+        others.append(lax.ppermute(block, ROW, crossed))
+    return *pieces, *others, beside
 
 
 def place_of(block):
-    high, residue, core = block >> 4, (block >> 1) & 7, block & 1
-    away = (residue - (lax.axis_index("zm") * 2 + lax.axis_index("zl"))) & 7
-    group = jnp.where(away < 4, 2 * away, jnp.where(away == 4, 7, 15 - 2 * away))
-    return (core ^ lax.axis_index("core")) * 32 + group * 4 + high
+    high, residue, core = block >> 3, (block >> 1) & 3, block & 1
+    away = (residue - lax.axis_index("zb")) & 3
+    group = jnp.where(away == 3, 1, jnp.where(away == 0, 0, away + 1))
+    return (core ^ lax.axis_index("core")) * 32 + group * 8 + high
 
 
 def body(nodes, grad_out, features, weight, tile_values, tile_rows, tile_cols, tile_count):
@@ -131,13 +131,12 @@
             jax.ShapeDtypeStruct((cols, tile, width), jnp.bfloat16),
             jax.ShapeDtypeStruct((cols, share, width), jnp.bfloat16),
         ),
-        in_specs=[smem] * 3 + [anywhere] * (1 + len(pieces)) + [vmem],
+        in_specs=[smem] * 3 + [vmem] + [anywhere] * len(pieces) + [vmem],
         out_specs=(vmem, vmem),
         scratch_shapes=[
-            pltpu.VMEM(tile_values.shape[2:], jnp.bfloat16),
             pltpu.VMEM((lax.axis_size(ROW), tile, width), jnp.bfloat16),
             pltpu.VMEM((cols, tile, width), jnp.float32),
-            pltpu.SemaphoreType.DMA((1 + len(pieces),)),
+            pltpu.SemaphoreType.DMA((len(pieces),)),
         ],
         compiler_params=pltpu.CompilerParams(vmem_limit_bytes=24 * 2**20),
     )(
@@ -180,7 +179,7 @@
 
 
 def solution(mesh):
-    fine = Mesh(mesh.devices.reshape(4, 4, 2, 2, 4, 4), ROW + COL)
+    fine = Mesh(mesh.devices.reshape(8, 4, 2, 4, 4), ROW + COL)
     placed = (
         P(COL + ROW, None),
         P(ROW + COL, None),

time: 220 us -> 209 us (0.950)
  waiting for transfers between devices: 28.8 us -> 20.6 us
  starting transfers between devices: 61.5 us -> 53.7 us
  blocking collectives: 113 us -> 118 us
    ppermute x10 -> x9, waiting for transfers between devices: 23 us -> 14.8 us  [the longest x2 7.64 us: gather_row(): pieces.append(lax.ppermute(block, Z, shifted(step)))]
    ppermute x10 -> x9, starting transfers between devices: 31.7 us -> 24.1 us  [the longest x3 8.61 us: gather_row(): others = [lax.ppermute(piece, 'core', [(0, 1), (1, 0)]) for piece in pieces]]
    all_gather x1, blocking collectives: 42.9 us -> 47.4 us  [gather_row(): lax.all_gather(grad_out, 'za')]
  transfers between devices with their start and end apart: 13 -> 12, of which waited for: 8 -> 5; matrix products, arithmetic and copies ran while one was open for 0% -> 1% of each run, Pallas kernels for 0% -> 0%
where the time goes in v4:
time: 209 us; the launch traced here: 207 us
  blocking collectives  118 us (56%)
  starting transfers between devices  53.7 us (26%)
  waiting for transfers between devices  20.6 us (10%)
  Pallas kernels  6.59 us (3%)
  local copies, waits for them, and re-layouts  6.57 us (3%)
    all_gather x1, blocking collectives, body(): mine = lax.all_gather(mine.astype(jnp.bfloat16), Z)  53.5 us
    all_gather x1, blocking collectives, gather_row(): lax.all_gather(grad_out, 'za')  47.4 us
    all_to_all x2, starting transfers between devices, from_all(): return lax.all_to_all(same, axes, 0, 0, tiled=True)  23.9 us
    all_to_all x1, blocking collectives, body(): shares = lax.all_to_all(shares, COL, 0, 0, tiled=True)  13.1 us
    ppermute x3, starting transfers between devices, gather_row(): others = [lax.ppermute(piece, 'core', [(0, 1), (1, 0)]) for piece in pieces]  8.61 us
    ppermute x2, waiting for transfers between devices, gather_row(): pieces.append(lax.ppermute(block, Z, shifted(step)))  7.64 us
    all_to_all x2, waiting for transfers between devices, from_all(): return lax.all_to_all(same, axes, 0, 0, tiled=True)  5.84 us
    all_to_all x1, starting transfers between devices, body(): parts = lax.all_to_all(parts, COL, 0, 0, tiled=True)  5.75 us
  transfers between devices with their start and end apart: 12, of which 5 were waited for; matrix products, arithmetic and copies ran while one was open for 1% of the time, Pallas kernels for 0%

profile of v4, /device:TPU:6, one launch (start us, length us, event | category | flops | bytes accessed | tf_op | source)
XLA Modules:
  0.0 206.7 jit_solution(14513641840107878277)
XLA Ops:
  0.7 1.9 broadcast_in_dim.7
  2.6 16.6 %all-to-all-start = ((bf16[16,128,256]{2,1,0:T(8,128)(2,1)}), bf16[16,128,256]{2,1,0:T(8,128)(2,1)S(1)}, u32[]{:S(2)}, u32[]{:S(2)}) async-start(bf16[16,128,256]{2,1,0:T(8,128)(2,1)} %broadcast_in_dim.7), calls=%async_computation | async-start | bytes 2097152 | tf_op jit(solution)/shard_map/all_to_all | solution.py:94
  19.3 47.4 %all-gather = bf16[1024,256]{1,0:T(8,128)(2,1)S(1)} all-gather(bf16[128,256]{1,0:T(8,128)(2,1)S(1)} %copy-done.3), channel_id=2, replica_groups=mesh['za'=8,'zb'=4,'core'=2,'x'=4,'y'=4] {'za'}, dimensions={0}, use_global_device_ids=true | all-gather | bytes 589824 | tf_op jit(solution)/shard_map/all_gather | solution.py:98
  66.6 3.4 %collective-permute-start.1 = (bf16[8,128,256]{2,1,0:T(8,128)(2,1)S(1)}, bf16[8,128,256]{2,1,0:T(8,128)(2,1)S(1)}, u32[]{:S(2)}, u32[]{:S(2)}) collective-permute-start(bf16[8,128,256]{2,1,0:T(8,128)(2,1)S(1)} %bitcast.13), channel_id=1, source_target_pairs={{0,992},{32,0},{64,32},{96,64},{128,96},{160,128},{192,160},{224,1... | collective-permute-start | bytes 1572872 | tf_op jit(solution)/shard_map/ppermute | solution.py:99
  70.1 2.4 %collective-permute-start = (bf16[8,128,256]{2,1,0:T(8,128)(2,1)S(1)}, bf16[8,128,256]{2,1,0:T(8,128)(2,1)S(1)}, u32[]{:S(2)}, u32[]{:S(2)}) collective-permute-start(bf16[8,128,256]{2,1,0:T(8,128)(2,1)S(1)} %bitcast.14), channel_id=1, source_target_pairs={{0,32},{32,64},{64,96},{96,128},{128,160},{160,192},{192,224},{224... | collective-permute-start | bytes 1572872 | tf_op jit(solution)/shard_map/ppermute | solution.py:99
  72.5 1.9 collective-permute-start.4
  74.4 3.3 %collective-permute-done.1.refs_2_ = bf16[8,128,256]{2,1,0:T(8,128)(2,1)S(1)} collective-permute-done((bf16[8,128,256]{2,1,0:T(8,128)(2,1)S(1)}, bf16[8,128,256]{2,1,0:T(8,128)(2,1)S(1)}, u32[]{:S(2)}, u32[]{:S(2)}) %collective-permute-start.1) | collective-permute-done | bytes 524320 | tf_op jit(solution)/shard_map/ppermute | solution.py:99
  77.7 0.7 slice.9
  78.4 1.9 collective-permute-start.8
  80.3 4.8 %collective-permute-start.6 = (bf16[8,128,256]{2,1,0:T(8,128)(2,1)S(1)}, bf16[8,128,256]{2,1,0:T(8,128)(2,1)}, u32[]{:S(2)}, u32[]{:S(2)}) collective-permute-start(bf16[8,128,256]{2,1,0:T(8,128)(2,1)S(1)} %collective-permute-done.1.refs_2_), channel_id=1, source_target_pairs={{0,16},{16,0},{1,17},{17,1},{2,18},{18,2},{3,19},{19,3},{4,20},{20... | collective-permute-start | bytes 1572872 | tf_op jit(solution)/shard_map/ppermute | solution.py:102
  85.1 1.9 collective-permute-start.5
  87.1 2.3 %collective-permute-start.3 = (bf16[4,128,256]{2,1,0:T(8,128)(2,1)}, bf16[4,128,256]{2,1,0:T(8,128)(2,1)}, u32[]{:S(2)}, u32[]{:S(2)}) collective-permute-start(bf16[4,128,256]{2,1,0:T(8,128)(2,1)} %slice.9), channel_id=1, source_target_pairs={{0,992},{32,0},{64,32},{96,64},{128,96},{160,128},{192,160},{224,1... | collective-permute-start | bytes 786440 | tf_op jit(solution)/shard_map/ppermute | solution.py:107
  89.4 0.7 slice.8
  90.1 3.4 %collective-permute-start.7 = (bf16[4,128,256]{2,1,0:T(8,128)(2,1)}, bf16[4,128,256]{2,1,0:T(8,128)(2,1)}, u32[]{:S(2)}, u32[]{:S(2)}) collective-permute-start(bf16[4,128,256]{2,1,0:T(8,128)(2,1)} %slice.8), channel_id=1, source_target_pairs={{0,48},{16,32},{32,80},{48,64},{64,112},{80,96},{96,144},{112,128}... | collective-permute-start | bytes 786440 | tf_op jit(solution)/shard_map/ppermute | solution.py:108
  93.5 2.1 %collective-permute-start.2 = (bf16[4,128,256]{2,1,0:T(8,128)(2,1)}, bf16[4,128,256]{2,1,0:T(8,128)(2,1)}, u32[]{:S(2)}, u32[]{:S(2)}) collective-permute-start(bf16[4,128,256]{2,1,0:T(8,128)(2,1)} %slice.8), channel_id=1, source_target_pairs={{0,32},{32,64},{64,96},{96,128},{128,160},{160,192},{192,224},{224... | collective-permute-start | bytes 786440 | tf_op jit(solution)/shard_map/ppermute | solution.py:107
  96.3 1.7 collective-permute-done.3.refs_4_
  98.0 3.8 %collective-permute-done.7.refs_8_ = bf16[4,128,256]{2,1,0:T(8,128)(2,1)} collective-permute-done((bf16[4,128,256]{2,1,0:T(8,128)(2,1)}, bf16[4,128,256]{2,1,0:T(8,128)(2,1)}, u32[]{:S(2)}, u32[]{:S(2)}) %collective-permute-start.7) | collective-permute-done | bytes 262176 | tf_op jit(solution)/shard_map/ppermute | solution.py:108
  101.8 5.9 %collective-permute-done.2.refs_3_ = bf16[4,128,256]{2,1,0:T(8,128)(2,1)} collective-permute-done((bf16[4,128,256]{2,1,0:T(8,128)(2,1)}, bf16[4,128,256]{2,1,0:T(8,128)(2,1)}, u32[]{:S(2)}, u32[]{:S(2)}) %collective-permute-start.2) | collective-permute-done | bytes 262176 | tf_op jit(solution)/shard_map/ppermute | solution.py:107
  107.7 0.0 copy-start
  107.8 1.7 copy-done
  109.5 5.7 %shard_map.86 = (bf16[16,128,256]{2,1,0:T(8,128)(2,1)}, bf16[16,16,256]{2,1,0:T(8,128)(2,1)S(1)}) custom-call(s32[1]{0:T(128)} %bitcast.10.count_ref, s32[80]{0:T(128)S(1)} %bitcast.17, s32[80]{0:T(128)S(1)} %add_bitcast_fusion.places_ref, bf16[80,128,128]{2,1,0:T(8,128)(2,1)S(1)} %bitcast.12, bf16[8,128,256]{2,1,0:T(8,128)(2,1)S(1)} %bitcast.16, ...), custom_call_target="tpu_custom_call" | custom-call | tf_op jit(solution)/shard_map/pallas_call | solution.py:128
  115.2 0.0 copy-start.1
  115.2 13.1 %all_to_all.20.shares_ref = bf16[16,16,256]{2,1,0:T(8,128)(2,1)S(1)} all-to-all(bf16[16,16,256]{2,1,0:T(8,128)(2,1)S(1)} %get-tuple-element.12), channel_id=1, replica_groups=mesh['za'=8,'zb'=4,'core'=2,'x'=4,'y'=4] {'x','y'}, dimensions={0} | all-to-all | bytes 262144 | tf_op jit(solution)/shard_map/all_to_all | solution.py:150
  128.3 5.8 %all-to-all-start.2 = ((bf16[16,128,256]{2,1,0:T(8,128)(2,1)}), bf16[16,128,256]{2,1,0:T(8,128)(2,1)S(1)}, u32[]{:S(2)}, u32[]{:S(2)}) async-start(bf16[16,128,256]{2,1,0:T(8,128)(2,1)} %get-tuple-element.15), calls=%async_computation.2 | async-start | bytes 2097152 | tf_op jit(solution)/shard_map/all_to_all | solution.py:162
  134.1 1.8 all-gather.1
  135.9 53.5 %all-gather.2 = bf16[256,256]{1,0:T(8,128)(2,1)S(1)} all-gather(bf16[8,256]{1,0:T(8,128)(2,1)S(1)} %dynamic-slice_convert_fusion), channel_id=4, replica_groups=mesh['za'=8,'zb'=4,'core'=2,'x'=4,'y'=4] {'za','zb'}, dimensions={0}, use_global_device_ids=true | all-gather | bytes 135168 | tf_op jit(solution)/shard_map/all_gather | solution.py:166
  189.5 1.8 all_gather.27
  191.3 0.7 broadcast_in_dim.8
  192.1 7.2 %all-to-all-start.3 = ((f32[16,16,256]{2,1,0:T(8,128)}), f32[16,16,256]{2,1,0:T(8,128)S(1)}, u32[]{:S(2)}, u32[]{:S(2)}) async-start(f32[16,16,256]{2,1,0:T(8,128)} %broadcast_in_dim.8), calls=%async_computation.3 | async-start | bytes 524288 | tf_op jit(solution)/shard_map/all_to_all | solution.py:94
  199.3 0.9 shard_map.88
  200.2 5.8 %all-to-all-done.3 = f32[16,16,256]{2,1,0:T(8,128)S(1)} async-done(((f32[16,16,256]{2,1,0:T(8,128)}), f32[16,16,256]{2,1,0:T(8,128)S(1)}, u32[]{:S(2)}, u32[]{:S(2)}) %all-to-all-start.3) | async-done | bytes 262176 | tf_op jit(solution)/shard_map/all_to_all | solution.py:94
  206.0 0.7 copy.13
  (19 shorter events, 0.1 us)
Async XLA Ops:
  0.6 18.6 %copy-start.3 = (bf16[128,256]{1,0:T(8,128)(2,1)S(1)}, bf16[128,256]{1,0:T(8,128)(2,1)}, u32[]{:S(2)}) copy-start(bf16[128,256]{1,0:T(8,128)(2,1)} %param.7) | copy-start | bytes 196612
  0.6 95.6 %copy-start.4 = (s32[1,1,80]{2,1,0:T(1,128)S(1)}, s32[1,1,80]{2,1,0:T(1,128)}, u32[]{:S(2)}) copy-start(s32[1,1,80]{2,1,0:T(1,128)} %param.12) | copy-start | bytes 964
  0.7 107.1 %copy-start.2 = (s32[1,1,80]{2,1,0:T(1,128)S(1)}, s32[1,1,80]{2,1,0:T(1,128)}, u32[]{:S(2)}) copy-start(s32[1,1,80]{2,1,0:T(1,128)} %param.11) | copy-start | bytes 964
  2.6 64.0 %all-to-all-start = ((bf16[16,128,256]{2,1,0:T(8,128)(2,1)}), bf16[16,128,256]{2,1,0:T(8,128)(2,1)S(1)}, u32[]{:S(2)}, u32[]{:S(2)}) async-start(bf16[16,128,256]{2,1,0:T(8,128)(2,1)} %broadcast_in_dim.7), calls=%async_computation | async-start | bytes 2097152 | tf_op jit(solution)/shard_map/all_to_all | solution.py:94
  66.6 11.1 %collective-permute-start.1 = (bf16[8,128,256]{2,1,0:T(8,128)(2,1)S(1)}, bf16[8,128,256]{2,1,0:T(8,128)(2,1)S(1)}, u32[]{:S(2)}, u32[]{:S(2)}) collective-permute-start(bf16[8,128,256]{2,1,0:T(8,128)(2,1)S(1)} %bitcast.13), channel_id=1, source_target_pairs={{0,992},{32,0},{64,32},{96,64},{128,96},{160,128},{192,160},{224,1... | collective-permute-start | bytes 1572872 | tf_op jit(solution)/shard_map/ppermute | solution.py:99
  70.1 15.0 %collective-permute-start = (bf16[8,128,256]{2,1,0:T(8,128)(2,1)S(1)}, bf16[8,128,256]{2,1,0:T(8,128)(2,1)S(1)}, u32[]{:S(2)}, u32[]{:S(2)}) collective-permute-start(bf16[8,128,256]{2,1,0:T(8,128)(2,1)S(1)} %bitcast.14), channel_id=1, source_target_pairs={{0,32},{32,64},{64,96},{96,128},{128,160},{160,192},{192,224},{224... | collective-permute-start | bytes 1572872 | tf_op jit(solution)/shard_map/ppermute | solution.py:99
  72.5 17.6 %collective-permute-start.4 = (bf16[8,128,256]{2,1,0:T(8,128)(2,1)S(1)}, bf16[8,128,256]{2,1,0:T(8,128)(2,1)S(1)}, u32[]{:S(2)}, u32[]{:S(2)}) collective-permute-start(bf16[8,128,256]{2,1,0:T(8,128)(2,1)S(1)} %bitcast.15), channel_id=1, source_target_pairs={{0,16},{16,0},{1,17},{17,1},{2,18},{18,2},{3,19},{19,3},{4,20},{20... | collective-permute-start | bytes 1572872 | tf_op jit(solution)/shard_map/ppermute | solution.py:102
  78.4 15.0 %collective-permute-start.8 = (bf16[4,128,256]{2,1,0:T(8,128)(2,1)}, bf16[4,128,256]{2,1,0:T(8,128)(2,1)S(1)}, u32[]{:S(2)}, u32[]{:S(2)}) collective-permute-start(bf16[4,128,256]{2,1,0:T(8,128)(2,1)} %slice.9), channel_id=1, source_target_pairs={{0,1008},{16,992},{32,16},{48,0},{64,48},{80,32},{96,80},{112,64},... | collective-permute-start | bytes 786440 | tf_op jit(solution)/shard_map/ppermute | solution.py:108
  80.3 27.4 %collective-permute-start.6 = (bf16[8,128,256]{2,1,0:T(8,128)(2,1)S(1)}, bf16[8,128,256]{2,1,0:T(8,128)(2,1)}, u32[]{:S(2)}, u32[]{:S(2)}) collective-permute-start(bf16[8,128,256]{2,1,0:T(8,128)(2,1)S(1)} %collective-permute-done.1.refs_2_), channel_id=1, source_target_pairs={{0,16},{16,0},{1,17},{17,1},{2,18},{18,2},{3,19},{19,3},{4,20},{20... | collective-permute-start | bytes 1572872 | tf_op jit(solution)/shard_map/ppermute | solution.py:102
  85.1 22.6 %collective-permute-start.5 = (bf16[8,128,256]{2,1,0:T(8,128)(2,1)S(1)}, bf16[8,128,256]{2,1,0:T(8,128)(2,1)}, u32[]{:S(2)}, u32[]{:S(2)}) collective-permute-start(bf16[8,128,256]{2,1,0:T(8,128)(2,1)S(1)} %collective-permute-done.refs_1_), channel_id=1, source_target_pairs={{0,16},{16,0},{1,17},{17,1},{2,18},{18,2},{3,19},{19,3},{4,20},{20... | collective-permute-start | bytes 1572872 | tf_op jit(solution)/shard_map/ppermute | solution.py:102
  87.1 10.9 %collective-permute-start.3 = (bf16[4,128,256]{2,1,0:T(8,128)(2,1)}, bf16[4,128,256]{2,1,0:T(8,128)(2,1)}, u32[]{:S(2)}, u32[]{:S(2)}) collective-permute-start(bf16[4,128,256]{2,1,0:T(8,128)(2,1)} %slice.9), channel_id=1, source_target_pairs={{0,992},{32,0},{64,32},{96,64},{128,96},{160,128},{192,160},{224,1... | collective-permute-start | bytes 786440 | tf_op jit(solution)/shard_map/ppermute | solution.py:107
  90.1 11.7 %collective-permute-start.7 = (bf16[4,128,256]{2,1,0:T(8,128)(2,1)}, bf16[4,128,256]{2,1,0:T(8,128)(2,1)}, u32[]{:S(2)}, u32[]{:S(2)}) collective-permute-start(bf16[4,128,256]{2,1,0:T(8,128)(2,1)} %slice.8), channel_id=1, source_target_pairs={{0,48},{16,32},{32,80},{48,64},{64,112},{80,96},{96,144},{112,128}... | collective-permute-start | bytes 786440 | tf_op jit(solution)/shard_map/ppermute | solution.py:108
  93.5 14.3 %collective-permute-start.2 = (bf16[4,128,256]{2,1,0:T(8,128)(2,1)}, bf16[4,128,256]{2,1,0:T(8,128)(2,1)}, u32[]{:S(2)}, u32[]{:S(2)}) collective-permute-start(bf16[4,128,256]{2,1,0:T(8,128)(2,1)} %slice.8), channel_id=1, source_target_pairs={{0,32},{32,64},{64,96},{96,128},{128,160},{160,192},{192,224},{224... | collective-permute-start | bytes 786440 | tf_op jit(solution)/shard_map/ppermute | solution.py:107
  107.7 1.7 copy-start
  115.2 84.1 %copy-start.1 = (bf16[256,256]{1,0:T(8,128)(2,1)S(1)}, bf16[256,256]{1,0:T(8,128)(2,1)}, u32[]{:S(2)}) copy-start(bf16[256,256]{1,0:T(8,128)(2,1)} %weight_ref.1) | copy-start | bytes 393220
  128.3 61.1 %all-to-all-start.2 = ((bf16[16,128,256]{2,1,0:T(8,128)(2,1)}), bf16[16,128,256]{2,1,0:T(8,128)(2,1)S(1)}, u32[]{:S(2)}, u32[]{:S(2)}) async-start(bf16[16,128,256]{2,1,0:T(8,128)(2,1)} %get-tuple-element.15), calls=%async_computation.2 | async-start | bytes 2097152 | tf_op jit(solution)/shard_map/all_to_all | solution.py:162
  192.1 14.0 %all-to-all-start.3 = ((f32[16,16,256]{2,1,0:T(8,128)}), f32[16,16,256]{2,1,0:T(8,128)S(1)}, u32[]{:S(2)}, u32[]{:S(2)}) async-start(f32[16,16,256]{2,1,0:T(8,128)} %broadcast_in_dim.8), calls=%async_computation.3 | async-start | bytes 524288 | tf_op jit(solution)/shard_map/all_to_all | solution.py:94

commit v5 on v4

--- a/solution.py
+++ b/solution.py
@@ -70,7 +70,7 @@
     return summed
 
 
-def share_kernel(scale, shares_ref, parts_ref, share_ref, same_parts_ref):
+def share_kernel(scale, shares_ref, share_ref):
     share_ref[...] = sum_of(shares_ref) * scale
 
 
@@ -96,16 +96,11 @@
 
 def gather_row(grad_out, beside):
     own, beside = lax.optimization_barrier((lax.all_gather(grad_out, "za"), beside))
-    left, right = lax.ppermute(own, Z, shifted(1)), lax.ppermute(own, Z, shifted(-1))
     half = own.shape[0] // 2
-    pieces = [own, left, right]
+    pieces = [own]
+    for block, step in ((own, 1), (own, -1), (own[:half], 2), (own[half:], -2)):
+        pieces.append(lax.ppermute(block, Z, shifted(step)))
     others = [lax.ppermute(piece, "core", [(0, 1), (1, 0)]) for piece in pieces]
-    for block, step in ((left[:half], 1), (right[half:], -1)):
-        crossed = [
-            (2 * source + core, 2 * target + 1 - core) for source, target in shifted(step) for core in (0, 1)
-        ]
-        pieces.append(lax.ppermute(block, Z, shifted(step)))
-        others.append(lax.ppermute(block, ROW, crossed))
     return *pieces, *others, beside
 
 
@@ -148,22 +143,19 @@
         own_features,
     )
     shares = lax.all_to_all(shares, COL, 0, 0, tiled=True)
-    grad_share, parts = pl.pallas_call(
+    grad_share = pl.pallas_call(
         functools.partial(share_kernel, nodes**-0.5),
-        out_shape=(
-            jax.ShapeDtypeStruct((share, width), jnp.float32),
-            jax.ShapeDtypeStruct(parts.shape, parts.dtype),
-        ),
-        in_specs=[vmem, anywhere],
-        out_specs=(vmem, anywhere),
-        input_output_aliases={1: 1},
+        out_shape=jax.ShapeDtypeStruct((share, width), jnp.float32),
+        in_specs=[vmem],
+        out_specs=vmem,
         compiler_params=pltpu.CompilerParams(vmem_limit_bytes=4 * 2**20),
-    )(shares, parts)
+    )(shares)
+    grad_share = jnp.sum(from_all(grad_share, ("zb", "core")), axis=0)
+    half = share // 2
+    mine = lax.dynamic_slice_in_dim(grad_share, half * lax.axis_index("core"), half).astype(jnp.bfloat16)
+    mine, parts = lax.optimization_barrier((mine, parts))
     parts = lax.all_to_all(parts, COL, 0, 0, tiled=True)
-    grad_share = jnp.sum(lax.all_gather(grad_share, "core"), axis=0)
-    half = share // 2
-    mine = lax.dynamic_slice_in_dim(grad_share, half * lax.axis_index("core"), half)
-    mine = lax.all_gather(mine.astype(jnp.bfloat16), Z)
+    mine = lax.all_gather(mine, "za")
     mine, parts = lax.optimization_barrier((mine, parts))
     mine = jnp.sum(mine.astype(jnp.float32), axis=0)
     grad_share = lax.all_gather(mine, "core", axis=0, tiled=True)

time: 209 us -> 192 us (0.919)
  blocking collectives: 118 us -> 98.8 us
  starting transfers between devices: 53.7 us -> 60.6 us
  waiting for transfers between devices: 20.6 us -> 16.4 us
    all_gather x2 -> x1, blocking collectives: 55.4 us -> 36.9 us  [body(): mine = lax.all_gather(mine, 'za')]
    ppermute x4 -> x0, starting transfers between devices: 11.1 us -> none  [the longest x2 5.26 us: gather_row(): others.append(lax.ppermute(block, ROW, crossed))]
    all_to_all x2 -> x3, starting transfers between devices: 23.9 us -> 32.2 us  [from_all(): return lax.all_to_all(same, axes, 0, 0, tiled=True)]
    ppermute x2 -> x4, starting transfers between devices: 4.4 us -> 12.6 us  [gather_row(): pieces.append(lax.ppermute(block, Z, shifted(step)))]
    ppermute x4 -> x0, waiting for transfers between devices: 7.13 us -> none  [the longest x2 3.84 us: gather_row(): others.append(lax.ppermute(block, ROW, crossed))]
    all_to_all x2 -> x3, waiting for transfers between devices: 5.84 us -> 12.6 us  [from_all(): return lax.all_to_all(same, axes, 0, 0, tiled=True)]
    ppermute x2 -> x4, waiting for transfers between devices: 7.64 us -> 2.61 us  [gather_row(): pieces.append(lax.ppermute(block, Z, shifted(step)))]
    ppermute x3 -> x5, starting transfers between devices: 8.61 us -> 10.1 us  [gather_row(): others = [lax.ppermute(piece, 'core', [(0, 1), (1, 0)]) for piece in pieces]]
  transfers between devices with their start and end apart: 12 -> 13, of which waited for: 5 -> 5; matrix products, arithmetic and copies ran while one was open for 1% -> 0% of each run, Pallas kernels for 0% -> 0%
where the time goes in v5:
time: 192 us; the launch traced here: 190 us
  blocking collectives  98.8 us (51%)
  starting transfers between devices  60.6 us (32%)
  waiting for transfers between devices  16.4 us (9%)
  Pallas kernels  6.44 us (3%)
  local copies, waits for them, and re-layouts  5.85 us (3%)
    all_gather x1, blocking collectives, gather_row(): lax.all_gather(grad_out, 'za')  47.4 us
    all_gather x1, blocking collectives, body(): mine = lax.all_gather(mine, 'za')  36.9 us
    all_to_all x3, starting transfers between devices, from_all(): return lax.all_to_all(same, axes, 0, 0, tiled=True)  32.2 us
    all_to_all x1, blocking collectives, body(): shares = lax.all_to_all(shares, COL, 0, 0, tiled=True)  12.7 us
    all_to_all x3, waiting for transfers between devices, from_all(): return lax.all_to_all(same, axes, 0, 0, tiled=True)  12.6 us
    ppermute x4, starting transfers between devices, gather_row(): pieces.append(lax.ppermute(block, Z, shifted(step)))  12.6 us
    ppermute x5, starting transfers between devices, gather_row(): others = [lax.ppermute(piece, 'core', [(0, 1), (1, 0)]) for piece in pieces]  10.1 us
    all_to_all x1, starting transfers between devices, body(): parts = lax.all_to_all(parts, COL, 0, 0, tiled=True)  5.73 us
  transfers between devices with their start and end apart: 13, of which 5 were waited for; matrix products, arithmetic and copies ran while one was open for 0% of the time, Pallas kernels for 0%

profile of v5, /device:TPU:6, one launch (start us, length us, event | category | flops | bytes accessed | tf_op | source)
XLA Modules:
  0.0 189.6 jit_solution(4550029499426896437)
XLA Ops:
  0.7 2.0 %broadcast_in_dim.9 = bf16[16,128,256]{2,1,0:T(8,128)(2,1)} broadcast(bf16[128,256]{1,0:T(8,128)(2,1)} %param.8), dimensions={1,2} | broadcast | bytes 1114112 | tf_op jit(solution)/shard_map/broadcast_in_dim | solution.py:93
  2.6 16.6 %all-to-all-start = ((bf16[16,128,256]{2,1,0:T(8,128)(2,1)}), bf16[16,128,256]{2,1,0:T(8,128)(2,1)S(1)}, u32[]{:S(2)}, u32[]{:S(2)}) async-start(bf16[16,128,256]{2,1,0:T(8,128)(2,1)} %broadcast_in_dim.9), calls=%async_computation | async-start | bytes 2097152 | tf_op jit(solution)/shard_map/all_to_all | solution.py:94
  19.3 47.4 %all-gather = bf16[1024,256]{1,0:T(8,128)(2,1)S(1)} all-gather(bf16[128,256]{1,0:T(8,128)(2,1)S(1)} %copy-done.3), channel_id=2, replica_groups=mesh['za'=8,'zb'=4,'core'=2,'x'=4,'y'=4] {'za'}, dimensions={0}, use_global_device_ids=true | all-gather | bytes 589824 | tf_op jit(solution)/shard_map/all_gather | solution.py:98
  66.7 3.4 %collective-permute-start.1 = (bf16[8,128,256]{2,1,0:T(8,128)(2,1)S(1)}, bf16[8,128,256]{2,1,0:T(8,128)(2,1)S(1)}, u32[]{:S(2)}, u32[]{:S(2)}) collective-permute-start(bf16[8,128,256]{2,1,0:T(8,128)(2,1)S(1)} %bitcast.10), channel_id=1, source_target_pairs={{0,992},{32,0},{64,32},{96,64},{128,96},{160,128},{192,160},{224,1... | collective-permute-start | bytes 1572872 | tf_op jit(solution)/shard_map/ppermute | solution.py:102
  70.1 2.4 %collective-permute-start = (bf16[8,128,256]{2,1,0:T(8,128)(2,1)S(1)}, bf16[8,128,256]{2,1,0:T(8,128)(2,1)S(1)}, u32[]{:S(2)}, u32[]{:S(2)}) collective-permute-start(bf16[8,128,256]{2,1,0:T(8,128)(2,1)S(1)} %bitcast.11), channel_id=1, source_target_pairs={{0,32},{32,64},{64,96},{96,128},{128,160},{160,192},{192,224},{224... | collective-permute-start | bytes 1572872 | tf_op jit(solution)/shard_map/ppermute | solution.py:102
  72.5 1.9 %collective-permute-start.4 = (bf16[8,128,256]{2,1,0:T(8,128)(2,1)S(1)}, bf16[8,128,256]{2,1,0:T(8,128)(2,1)S(1)}, u32[]{:S(2)}, u32[]{:S(2)}) collective-permute-start(bf16[8,128,256]{2,1,0:T(8,128)(2,1)S(1)} %bitcast.12), channel_id=1, source_target_pairs={{0,16},{16,0},{1,17},{17,1},{2,18},{18,2},{3,19},{19,3},{4,20},{20... | collective-permute-start | bytes 1572872 | tf_op jit(solution)/shard_map/ppermute | solution.py:103
  74.5 2.9 %collective-permute-start.3 = (bf16[4,128,256]{2,1,0:T(8,128)(2,1)S(1)}, bf16[4,128,256]{2,1,0:T(8,128)(2,1)S(1)}, u32[]{:S(2)}, u32[]{:S(2)}) collective-permute-start(bf16[4,128,256]{2,1,0:T(8,128)(2,1)S(1)} %get-tuple-element.18), channel_id=1, source_target_pairs={{0,960},{32,992},{64,0},{96,32},{128,64},{160,96},{192,128},{224,1... | collective-permute-start | bytes 786440 | tf_op jit(solution)/shard_map/ppermute | solution.py:102
  77.4 3.8 %collective-permute-start.2 = (bf16[4,128,256]{2,1,0:T(8,128)(2,1)S(1)}, bf16[4,128,256]{2,1,0:T(8,128)(2,1)}, u32[]{:S(2)}, u32[]{:S(2)}) collective-permute-start(bf16[4,128,256]{2,1,0:T(8,128)(2,1)S(1)} %get-tuple-element.19), channel_id=1, source_target_pairs={{0,64},{32,96},{64,128},{96,160},{128,192},{160,224},{192,256},{22... | collective-permute-start | bytes 786440 | tf_op jit(solution)/shard_map/ppermute | solution.py:102
  81.2 1.9 %collective-permute-start.6 = (bf16[8,128,256]{2,1,0:T(8,128)(2,1)S(1)}, bf16[8,128,256]{2,1,0:T(8,128)(2,1)}, u32[]{:S(2)}, u32[]{:S(2)}) collective-permute-start(bf16[8,128,256]{2,1,0:T(8,128)(2,1)S(1)} %collective-permute-done.1.refs_2_), channel_id=1, source_target_pairs={{0,16},{16,0},{1,17},{17,1},{2,18},{18,2},{3,19},{19,3},{4,20},{20... | collective-permute-start | bytes 1572872 | tf_op jit(solution)/shard_map/ppermute | solution.py:103
  83.2 2.4 %collective-permute-start.5 = (bf16[8,128,256]{2,1,0:T(8,128)(2,1)S(1)}, bf16[8,128,256]{2,1,0:T(8,128)(2,1)}, u32[]{:S(2)}, u32[]{:S(2)}) collective-permute-start(bf16[8,128,256]{2,1,0:T(8,128)(2,1)S(1)} %collective-permute-done.refs_1_), channel_id=1, source_target_pairs={{0,16},{16,0},{1,17},{17,1},{2,18},{18,2},{3,19},{19,3},{4,20},{20... | collective-permute-start | bytes 1572872 | tf_op jit(solution)/shard_map/ppermute | solution.py:103
  85.6 1.9 collective-permute-done.3.refs_4_
  87.5 1.9 %collective-permute-start.8 = (bf16[4,128,256]{2,1,0:T(8,128)(2,1)S(1)}, bf16[4,128,256]{2,1,0:T(8,128)(2,1)}, u32[]{:S(2)}, u32[]{:S(2)}) collective-permute-start(bf16[4,128,256]{2,1,0:T(8,128)(2,1)S(1)} %collective-permute-done.3.refs_4_), channel_id=1, source_target_pairs={{0,16},{16,0},{1,17},{17,1},{2,18},{18,2},{3,19},{19,3},{4,20},{20... | collective-permute-start | bytes 786440 | tf_op jit(solution)/shard_map/ppermute | solution.py:103
  89.4 0.7 collective-permute-done.2.refs_3_
  90.1 1.9 %collective-permute-start.7 = (bf16[4,128,256]{2,1,0:T(8,128)(2,1)}, bf16[4,128,256]{2,1,0:T(8,128)(2,1)}, u32[]{:S(2)}, u32[]{:S(2)}) collective-permute-start(bf16[4,128,256]{2,1,0:T(8,128)(2,1)} %collective-permute-done.2.refs_3_), channel_id=1, source_target_pairs={{0,16},{16,0},{1,17},{17,1},{2,18},{18,2},{3,19},{19,3},{4,20},{20... | collective-permute-start | bytes 786440 | tf_op jit(solution)/shard_map/ppermute | solution.py:103
  92.7 0.0 collective-permute-done.8.refs_9_
  92.7 1.2 collective-permute-done.7.refs_8_
  93.9 0.0 copy-start
  93.9 1.7 copy-done
  95.6 5.5 %shard_map.86 = (bf16[16,128,256]{2,1,0:T(8,128)(2,1)}, bf16[16,16,256]{2,1,0:T(8,128)(2,1)S(1)}) custom-call(s32[1]{0:T(128)} %bitcast.9.count_ref, s32[80]{0:T(128)S(1)} %bitcast.17, s32[80]{0:T(128)S(1)} %add_bitcast_fusion.places_ref, bf16[80,128,128]{2,1,0:T(8,128)(2,1)S(1)} %bitcast.16, bf16[8,128,256]{2,1,0:T(8,128)(2,1)S(1)} %bitcast.14, ...), custom_call_target="tpu_custom_call" | custom-call | tf_op jit(solution)/shard_map/pallas_call | solution.py:123
  101.2 0.0 copy-start.1
  101.2 12.7 %all_to_all.25.shares_ref = bf16[16,16,256]{2,1,0:T(8,128)(2,1)S(1)} all-to-all(bf16[16,16,256]{2,1,0:T(8,128)(2,1)S(1)} %get-tuple-element.12), channel_id=1, replica_groups=mesh['za'=8,'zb'=4,'core'=2,'x'=4,'y'=4] {'x','y'}, dimensions={0} | all-to-all | bytes 262144 | tf_op jit(solution)/shard_map/all_to_all | solution.py:145
  113.9 0.7 broadcast_in_dim.10
  114.6 8.4 %all-to-all-start.2 = ((f32[8,16,256]{2,1,0:T(8,128)}), f32[8,16,256]{2,1,0:T(8,128)S(1)}, u32[]{:S(2)}, u32[]{:S(2)}) async-start(f32[8,16,256]{2,1,0:T(8,128)} %broadcast_in_dim.10), calls=%async_computation.2 | async-start | bytes 262144 | tf_op jit(solution)/shard_map/all_to_all | solution.py:94
  123.0 6.8 %all-to-all-done.2 = f32[8,16,256]{2,1,0:T(8,128)S(1)} async-done(((f32[8,16,256]{2,1,0:T(8,128)}), f32[8,16,256]{2,1,0:T(8,128)S(1)}, u32[]{:S(2)}, u32[]{:S(2)}) %all-to-all-start.2) | async-done | bytes 131104 | tf_op jit(solution)/shard_map/all_to_all | solution.py:94
  129.8 5.7 %all-to-all-start.3 = ((bf16[16,128,256]{2,1,0:T(8,128)(2,1)}), bf16[16,128,256]{2,1,0:T(8,128)(2,1)S(1)}, u32[]{:S(2)}, u32[]{:S(2)}) async-start(bf16[16,128,256]{2,1,0:T(8,128)(2,1)} %get-tuple-element.15), calls=%async_computation.3 | async-start | bytes 2097152 | tf_op jit(solution)/shard_map/all_to_all | solution.py:157
  135.6 36.9 %all-gather.1 = bf16[64,256]{1,0:T(8,128)(2,1)S(1)} all-gather(bf16[8,256]{1,0:T(8,128)(2,1)S(1)} %dynamic-slice_convert_fusion), channel_id=3, replica_groups=mesh['za'=8,'zb'=4,'core'=2,'x'=4,'y'=4] {'za'}, dimensions={0}, use_global_device_ids=true | all-gather | bytes 36864 | tf_op jit(solution)/shard_map/all_gather | solution.py:158
  172.4 1.8 all_gather.19
  174.3 0.7 broadcast_in_dim.11
  175.0 7.1 %all-to-all-start.4 = ((f32[16,16,256]{2,1,0:T(8,128)}), f32[16,16,256]{2,1,0:T(8,128)S(1)}, u32[]{:S(2)}, u32[]{:S(2)}) async-start(f32[16,16,256]{2,1,0:T(8,128)} %broadcast_in_dim.11), calls=%async_computation.4 | async-start | bytes 524288 | tf_op jit(solution)/shard_map/all_to_all | solution.py:94
  182.1 0.9 shard_map.88
  183.1 5.8 %all-to-all-done.4 = f32[16,16,256]{2,1,0:T(8,128)S(1)} async-done(((f32[16,16,256]{2,1,0:T(8,128)}), f32[16,16,256]{2,1,0:T(8,128)S(1)}, u32[]{:S(2)}, u32[]{:S(2)}) %all-to-all-start.4) | async-done | bytes 262176 | tf_op jit(solution)/shard_map/all_to_all | solution.py:94
  188.9 0.7 copy.11
  (20 shorter events, 0.1 us)
Async XLA Ops:
  0.6 18.6 %copy-start.3 = (bf16[128,256]{1,0:T(8,128)(2,1)S(1)}, bf16[128,256]{1,0:T(8,128)(2,1)}, u32[]{:S(2)}) copy-start(bf16[128,256]{1,0:T(8,128)(2,1)} %param.7) | copy-start | bytes 196612
  0.6 92.1 %copy-start.4 = (s32[1,1,80]{2,1,0:T(1,128)S(1)}, s32[1,1,80]{2,1,0:T(1,128)}, u32[]{:S(2)}) copy-start(s32[1,1,80]{2,1,0:T(1,128)} %param.12) | copy-start | bytes 964
  0.7 93.2 %copy-start.2 = (s32[1,1,80]{2,1,0:T(1,128)S(1)}, s32[1,1,80]{2,1,0:T(1,128)}, u32[]{:S(2)}) copy-start(s32[1,1,80]{2,1,0:T(1,128)} %param.11) | copy-start | bytes 964
  2.6 64.0 %all-to-all-start = ((bf16[16,128,256]{2,1,0:T(8,128)(2,1)}), bf16[16,128,256]{2,1,0:T(8,128)(2,1)S(1)}, u32[]{:S(2)}, u32[]{:S(2)}) async-start(bf16[16,128,256]{2,1,0:T(8,128)(2,1)} %broadcast_in_dim.9), calls=%async_computation | async-start | bytes 2097152 | tf_op jit(solution)/shard_map/all_to_all | solution.py:94
  66.7 14.6 %collective-permute-start.1 = (bf16[8,128,256]{2,1,0:T(8,128)(2,1)S(1)}, bf16[8,128,256]{2,1,0:T(8,128)(2,1)S(1)}, u32[]{:S(2)}, u32[]{:S(2)}) collective-permute-start(bf16[8,128,256]{2,1,0:T(8,128)(2,1)S(1)} %bitcast.10), channel_id=1, source_target_pairs={{0,992},{32,0},{64,32},{96,64},{128,96},{160,128},{192,160},{224,1... | collective-permute-start | bytes 1572872 | tf_op jit(solution)/shard_map/ppermute | solution.py:102
  70.1 13.1 %collective-permute-start = (bf16[8,128,256]{2,1,0:T(8,128)(2,1)S(1)}, bf16[8,128,256]{2,1,0:T(8,128)(2,1)S(1)}, u32[]{:S(2)}, u32[]{:S(2)}) collective-permute-start(bf16[8,128,256]{2,1,0:T(8,128)(2,1)S(1)} %bitcast.11), channel_id=1, source_target_pairs={{0,32},{32,64},{64,96},{96,128},{128,160},{160,192},{192,224},{224... | collective-permute-start | bytes 1572872 | tf_op jit(solution)/shard_map/ppermute | solution.py:102
  72.5 21.4 %collective-permute-start.4 = (bf16[8,128,256]{2,1,0:T(8,128)(2,1)S(1)}, bf16[8,128,256]{2,1,0:T(8,128)(2,1)S(1)}, u32[]{:S(2)}, u32[]{:S(2)}) collective-permute-start(bf16[8,128,256]{2,1,0:T(8,128)(2,1)S(1)} %bitcast.12), channel_id=1, source_target_pairs={{0,16},{16,0},{1,17},{17,1},{2,18},{18,2},{3,19},{19,3},{4,20},{20... | collective-permute-start | bytes 1572872 | tf_op jit(solution)/shard_map/ppermute | solution.py:103
  74.5 13.0 %collective-permute-start.3 = (bf16[4,128,256]{2,1,0:T(8,128)(2,1)S(1)}, bf16[4,128,256]{2,1,0:T(8,128)(2,1)S(1)}, u32[]{:S(2)}, u32[]{:S(2)}) collective-permute-start(bf16[4,128,256]{2,1,0:T(8,128)(2,1)S(1)} %get-tuple-element.18), channel_id=1, source_target_pairs={{0,960},{32,992},{64,0},{96,32},{128,64},{160,96},{192,128},{224,1... | collective-permute-start | bytes 786440 | tf_op jit(solution)/shard_map/ppermute | solution.py:102
  77.4 12.7 %collective-permute-start.2 = (bf16[4,128,256]{2,1,0:T(8,128)(2,1)S(1)}, bf16[4,128,256]{2,1,0:T(8,128)(2,1)}, u32[]{:S(2)}, u32[]{:S(2)}) collective-permute-start(bf16[4,128,256]{2,1,0:T(8,128)(2,1)S(1)} %get-tuple-element.19), channel_id=1, source_target_pairs={{0,64},{32,96},{64,128},{96,160},{128,192},{160,224},{192,256},{22... | collective-permute-start | bytes 786440 | tf_op jit(solution)/shard_map/ppermute | solution.py:102
  81.2 12.6 %collective-permute-start.6 = (bf16[8,128,256]{2,1,0:T(8,128)(2,1)S(1)}, bf16[8,128,256]{2,1,0:T(8,128)(2,1)}, u32[]{:S(2)}, u32[]{:S(2)}) collective-permute-start(bf16[8,128,256]{2,1,0:T(8,128)(2,1)S(1)} %collective-permute-done.1.refs_2_), channel_id=1, source_target_pairs={{0,16},{16,0},{1,17},{17,1},{2,18},{18,2},{3,19},{19,3},{4,20},{20... | collective-permute-start | bytes 1572872 | tf_op jit(solution)/shard_map/ppermute | solution.py:103
  83.2 10.7 %collective-permute-start.5 = (bf16[8,128,256]{2,1,0:T(8,128)(2,1)S(1)}, bf16[8,128,256]{2,1,0:T(8,128)(2,1)}, u32[]{:S(2)}, u32[]{:S(2)}) collective-permute-start(bf16[8,128,256]{2,1,0:T(8,128)(2,1)S(1)} %collective-permute-done.refs_1_), channel_id=1, source_target_pairs={{0,16},{16,0},{1,17},{17,1},{2,18},{18,2},{3,19},{19,3},{4,20},{20... | collective-permute-start | bytes 1572872 | tf_op jit(solution)/shard_map/ppermute | solution.py:103
  87.5 5.2 %collective-permute-start.8 = (bf16[4,128,256]{2,1,0:T(8,128)(2,1)S(1)}, bf16[4,128,256]{2,1,0:T(8,128)(2,1)}, u32[]{:S(2)}, u32[]{:S(2)}) collective-permute-start(bf16[4,128,256]{2,1,0:T(8,128)(2,1)S(1)} %collective-permute-done.3.refs_4_), channel_id=1, source_target_pairs={{0,16},{16,0},{1,17},{17,1},{2,18},{18,2},{3,19},{19,3},{4,20},{20... | collective-permute-start | bytes 786440 | tf_op jit(solution)/shard_map/ppermute | solution.py:103
  90.1 3.8 %collective-permute-start.7 = (bf16[4,128,256]{2,1,0:T(8,128)(2,1)}, bf16[4,128,256]{2,1,0:T(8,128)(2,1)}, u32[]{:S(2)}, u32[]{:S(2)}) collective-permute-start(bf16[4,128,256]{2,1,0:T(8,128)(2,1)} %collective-permute-done.2.refs_3_), channel_id=1, source_target_pairs={{0,16},{16,0},{1,17},{17,1},{2,18},{18,2},{3,19},{19,3},{4,20},{20... | collective-permute-start | bytes 786440 | tf_op jit(solution)/shard_map/ppermute | solution.py:103
  93.9 1.7 copy-start
  101.2 81.0 %copy-start.1 = (bf16[256,256]{1,0:T(8,128)(2,1)S(1)}, bf16[256,256]{1,0:T(8,128)(2,1)}, u32[]{:S(2)}) copy-start(bf16[256,256]{1,0:T(8,128)(2,1)} %weight_ref.1) | copy-start | bytes 393220
  114.6 15.2 %all-to-all-start.2 = ((f32[8,16,256]{2,1,0:T(8,128)}), f32[8,16,256]{2,1,0:T(8,128)S(1)}, u32[]{:S(2)}, u32[]{:S(2)}) async-start(f32[8,16,256]{2,1,0:T(8,128)} %broadcast_in_dim.10), calls=%async_computation.2 | async-start | bytes 262144 | tf_op jit(solution)/shard_map/all_to_all | solution.py:94
  129.8 42.6 %all-to-all-start.3 = ((bf16[16,128,256]{2,1,0:T(8,128)(2,1)}), bf16[16,128,256]{2,1,0:T(8,128)(2,1)S(1)}, u32[]{:S(2)}, u32[]{:S(2)}) async-start(bf16[16,128,256]{2,1,0:T(8,128)(2,1)} %get-tuple-element.15), calls=%async_computation.3 | async-start | bytes 2097152 | tf_op jit(solution)/shard_map/all_to_all | solution.py:157
  175.0 13.9 %all-to-all-start.4 = ((f32[16,16,256]{2,1,0:T(8,128)}), f32[16,16,256]{2,1,0:T(8,128)S(1)}, u32[]{:S(2)}, u32[]{:S(2)}) async-start(f32[16,16,256]{2,1,0:T(8,128)} %broadcast_in_dim.11), calls=%async_computation.4 | async-start | bytes 524288 | tf_op jit(solution)/shard_map/all_to_all | solution.py:94

commit v6 on v5

--- a/solution.py
+++ b/solution.py
@@ -100,7 +100,9 @@
     pieces = [own]
     for block, step in ((own, 1), (own, -1), (own[:half], 2), (own[half:], -2)):
         pieces.append(lax.ppermute(block, Z, shifted(step)))
-    others = [lax.ppermute(piece, "core", [(0, 1), (1, 0)]) for piece in pieces]
+    swap = [(0, 1), (1, 0)]
+    first, unused = lax.optimization_barrier((own, pieces[2]))
+    others = [lax.ppermute(piece, "core", swap) for piece in (first, *pieces[1:])]
     return *pieces, *others, beside
 
 
@@ -151,15 +153,11 @@
         compiler_params=pltpu.CompilerParams(vmem_limit_bytes=4 * 2**20),
     )(shares)
     grad_share = jnp.sum(from_all(grad_share, ("zb", "core")), axis=0)
-    half = share // 2
-    mine = lax.dynamic_slice_in_dim(grad_share, half * lax.axis_index("core"), half).astype(jnp.bfloat16)
-    mine, parts = lax.optimization_barrier((mine, parts))
+    grad_share, parts = lax.optimization_barrier((grad_share, parts))
     parts = lax.all_to_all(parts, COL, 0, 0, tiled=True)
-    mine = lax.all_gather(mine, "za")
-    mine, parts = lax.optimization_barrier((mine, parts))
-    mine = jnp.sum(mine.astype(jnp.float32), axis=0)
-    grad_share = lax.all_gather(mine, "core", axis=0, tiled=True)
-    weight_grad = from_all(grad_share, COL).reshape(width, width)
+    grad_share, parts = lax.optimization_barrier((lax.all_gather(grad_share, "za"), parts))
+    grad_share = jnp.sum(grad_share, axis=0).astype(jnp.bfloat16)
+    weight_grad = from_all(grad_share, COL).reshape(width, width).astype(jnp.float32)
     input_grad = pl.pallas_call(
         finish_kernel,
         out_shape=jax.ShapeDtypeStruct((tile, width), jnp.bfloat16),

time: 192 us -> 188 us (0.979)
  blocking collectives: 98.8 us -> 107 us
  starting transfers between devices: 60.6 us -> 52.7 us
  waiting for transfers between devices: 16.4 us -> 13.1 us
    all_to_all x0 -> x1, blocking collectives: none -> 10.8 us  [from_all(): return lax.all_to_all(same, axes, 0, 0, tiled=True)]
    all_to_all x3 -> x2, starting transfers between devices: 32.2 us -> 23.9 us  [from_all(): return lax.all_to_all(same, axes, 0, 0, tiled=True)]
    all_to_all x3 -> x2, waiting for transfers between devices: 12.6 us -> 4.96 us  [from_all(): return lax.all_to_all(same, axes, 0, 0, tiled=True)]
    ppermute x4, waiting for transfers between devices: 2.61 us -> 6.94 us  [gather_row(): pieces.append(lax.ppermute(block, Z, shifted(step)))]
    all_gather x2 -> x1, blocking collectives: 38.7 us -> 36.8 us  [body(): lax.all_gather(grad_share, 'za')]
  transfers between devices with their start and end apart: 13 -> 12, of which waited for: 5 -> 4; matrix products, arithmetic and copies ran while one was open for 0% -> 0% of each run, Pallas kernels for 0% -> 0%
where the time goes in v6:
time: 188 us; the launch traced here: 186 us
  blocking collectives  107 us (57%)
  starting transfers between devices  52.7 us (28%)
  waiting for transfers between devices  13.1 us (7%)
  Pallas kernels  6.52 us (3%)
  local copies, waits for them, and re-layouts  4.42 us (2%)
    all_gather x1, blocking collectives, gather_row(): lax.all_gather(grad_out, 'za')  47.4 us
    all_gather x1, blocking collectives, body(): lax.all_gather(grad_share, 'za')  36.8 us
    all_to_all x2, starting transfers between devices, from_all(): return lax.all_to_all(same, axes, 0, 0, tiled=True)  23.9 us
    ppermute x4, starting transfers between devices, gather_row(): pieces.append(lax.ppermute(block, Z, shifted(step)))  12.6 us
    all_to_all x1, blocking collectives, body(): shares = lax.all_to_all(shares, COL, 0, 0, tiled=True)  12.2 us
    all_to_all x1, blocking collectives, from_all(): return lax.all_to_all(same, axes, 0, 0, tiled=True)  10.8 us
    ppermute x5, starting transfers between devices, gather_row(): lax.ppermute(piece, 'core', swap)  10.6 us
    ppermute x4, waiting for transfers between devices, gather_row(): pieces.append(lax.ppermute(block, Z, shifted(step)))  6.94 us
  transfers between devices with their start and end apart: 12, of which 4 were waited for; matrix products, arithmetic and copies ran while one was open for 0% of the time, Pallas kernels for 0%

profile of v6, /device:TPU:6, one launch (start us, length us, event | category | flops | bytes accessed | tf_op | source)
XLA Modules:
  0.0 186.1 jit_solution(3246023111135067284)
XLA Ops:
  0.7 1.9 %broadcast_in_dim.9 = bf16[16,128,256]{2,1,0:T(8,128)(2,1)} broadcast(bf16[128,256]{1,0:T(8,128)(2,1)} %param.8), dimensions={1,2} | broadcast | bytes 1114112 | tf_op jit(solution)/shard_map/broadcast_in_dim | solution.py:93
  2.6 16.6 %all-to-all-start = ((bf16[16,128,256]{2,1,0:T(8,128)(2,1)}), bf16[16,128,256]{2,1,0:T(8,128)(2,1)S(1)}, u32[]{:S(2)}, u32[]{:S(2)}) async-start(bf16[16,128,256]{2,1,0:T(8,128)(2,1)} %broadcast_in_dim.9), calls=%async_computation | async-start | bytes 2097152 | tf_op jit(solution)/shard_map/all_to_all | solution.py:94
  19.3 47.4 %all-gather = bf16[1024,256]{1,0:T(8,128)(2,1)S(1)} all-gather(bf16[128,256]{1,0:T(8,128)(2,1)S(1)} %copy-done.3), channel_id=2, replica_groups=mesh['za'=8,'zb'=4,'core'=2,'x'=4,'y'=4] {'za'}, dimensions={0}, use_global_device_ids=true | all-gather | bytes 589824 | tf_op jit(solution)/shard_map/all_gather | solution.py:98
  66.6 3.4 %collective-permute-start.1 = (bf16[8,128,256]{2,1,0:T(8,128)(2,1)S(1)}, bf16[8,128,256]{2,1,0:T(8,128)(2,1)S(1)}, u32[]{:S(2)}, u32[]{:S(2)}) collective-permute-start(bf16[8,128,256]{2,1,0:T(8,128)(2,1)S(1)} %bitcast.12), channel_id=1, source_target_pairs={{0,992},{32,0},{64,32},{96,64},{128,96},{160,128},{192,160},{224,1... | collective-permute-start | bytes 1572872 | tf_op jit(solution)/shard_map/ppermute | solution.py:102
  70.1 2.4 %collective-permute-start = (bf16[8,128,256]{2,1,0:T(8,128)(2,1)S(1)}, bf16[8,128,256]{2,1,0:T(8,128)(2,1)S(1)}, u32[]{:S(2)}, u32[]{:S(2)}) collective-permute-start(bf16[8,128,256]{2,1,0:T(8,128)(2,1)S(1)} %bitcast.13), channel_id=1, source_target_pairs={{0,32},{32,64},{64,96},{96,128},{128,160},{160,192},{192,224},{224... | collective-permute-start | bytes 1572872 | tf_op jit(solution)/shard_map/ppermute | solution.py:102
  72.5 2.9 %collective-permute-start.3 = (bf16[4,128,256]{2,1,0:T(8,128)(2,1)S(1)}, bf16[4,128,256]{2,1,0:T(8,128)(2,1)S(1)}, u32[]{:S(2)}, u32[]{:S(2)}) collective-permute-start(bf16[4,128,256]{2,1,0:T(8,128)(2,1)S(1)} %get-tuple-element.20), channel_id=1, source_target_pairs={{0,960},{32,992},{64,0},{96,32},{128,64},{160,96},{192,128},{224,1... | collective-permute-start | bytes 786440 | tf_op jit(solution)/shard_map/ppermute | solution.py:102
  75.5 3.8 %collective-permute-start.2 = (bf16[4,128,256]{2,1,0:T(8,128)(2,1)S(1)}, bf16[4,128,256]{2,1,0:T(8,128)(2,1)}, u32[]{:S(2)}, u32[]{:S(2)}) collective-permute-start(bf16[4,128,256]{2,1,0:T(8,128)(2,1)S(1)} %get-tuple-element.21), channel_id=1, source_target_pairs={{0,64},{32,96},{64,128},{96,160},{128,192},{160,224},{192,256},{22... | collective-permute-start | bytes 786440 | tf_op jit(solution)/shard_map/ppermute | solution.py:102
  79.3 4.0 %collective-permute-done.1.refs_2_ = bf16[8,128,256]{2,1,0:T(8,128)(2,1)S(1)} collective-permute-done((bf16[8,128,256]{2,1,0:T(8,128)(2,1)S(1)}, bf16[8,128,256]{2,1,0:T(8,128)(2,1)S(1)}, u32[]{:S(2)}, u32[]{:S(2)}) %collective-permute-start.1) | collective-permute-done | bytes 524320 | tf_op jit(solution)/shard_map/ppermute | solution.py:102
  83.3 1.9 %collective-permute-start.4 = (bf16[8,128,256]{2,1,0:T(8,128)(2,1)S(1)}, bf16[8,128,256]{2,1,0:T(8,128)(2,1)S(1)}, u32[]{:S(2)}, u32[]{:S(2)}) collective-permute-start(bf16[8,128,256]{2,1,0:T(8,128)(2,1)S(1)} %bitcast.15), channel_id=1, source_target_pairs={{0,16},{16,0},{1,17},{17,1},{2,18},{18,2},{3,19},{19,3},{4,20},{20... | collective-permute-start | bytes 1572872 | tf_op jit(solution)/shard_map/ppermute | solution.py:105
  85.2 2.4 %collective-permute-start.6 = (bf16[8,128,256]{2,1,0:T(8,128)(2,1)S(1)}, bf16[8,128,256]{2,1,0:T(8,128)(2,1)}, u32[]{:S(2)}, u32[]{:S(2)}) collective-permute-start(bf16[8,128,256]{2,1,0:T(8,128)(2,1)S(1)} %collective-permute-done.1.refs_2_), channel_id=1, source_target_pairs={{0,16},{16,0},{1,17},{17,1},{2,18},{18,2},{3,19},{19,3},{4,20},{20... | collective-permute-start | bytes 1572872 | tf_op jit(solution)/shard_map/ppermute | solution.py:105
  87.7 2.9 %collective-permute-done.refs_1_ = bf16[8,128,256]{2,1,0:T(8,128)(2,1)S(1)} collective-permute-done((bf16[8,128,256]{2,1,0:T(8,128)(2,1)S(1)}, bf16[8,128,256]{2,1,0:T(8,128)(2,1)S(1)}, u32[]{:S(2)}, u32[]{:S(2)}) %collective-permute-start) | collective-permute-done | bytes 524320 | tf_op jit(solution)/shard_map/ppermute | solution.py:102
  90.6 1.9 %collective-permute-start.5 = (bf16[8,128,256]{2,1,0:T(8,128)(2,1)S(1)}, bf16[8,128,256]{2,1,0:T(8,128)(2,1)}, u32[]{:S(2)}, u32[]{:S(2)}) collective-permute-start(bf16[8,128,256]{2,1,0:T(8,128)(2,1)S(1)} %collective-permute-done.refs_1_), channel_id=1, source_target_pairs={{0,16},{16,0},{1,17},{17,1},{2,18},{18,2},{3,19},{19,3},{4,20},{20... | collective-permute-start | bytes 1572872 | tf_op jit(solution)/shard_map/ppermute | solution.py:105
  92.5 2.4 %collective-permute-start.8 = (bf16[4,128,256]{2,1,0:T(8,128)(2,1)S(1)}, bf16[4,128,256]{2,1,0:T(8,128)(2,1)}, u32[]{:S(2)}, u32[]{:S(2)}) collective-permute-start(bf16[4,128,256]{2,1,0:T(8,128)(2,1)S(1)} %collective-permute-done.3.refs_4_), channel_id=1, source_target_pairs={{0,16},{16,0},{1,17},{17,1},{2,18},{18,2},{3,19},{19,3},{4,20},{20... | collective-permute-start | bytes 786440 | tf_op jit(solution)/shard_map/ppermute | solution.py:105
  94.9 0.0 collective-permute-done.2.refs_3_
  94.9 1.9 %collective-permute-start.7 = (bf16[4,128,256]{2,1,0:T(8,128)(2,1)}, bf16[4,128,256]{2,1,0:T(8,128)(2,1)}, u32[]{:S(2)}, u32[]{:S(2)}) collective-permute-start(bf16[4,128,256]{2,1,0:T(8,128)(2,1)} %collective-permute-done.2.refs_3_), channel_id=1, source_target_pairs={{0,16},{16,0},{1,17},{17,1},{2,18},{18,2},{3,19},{19,3},{4,20},{20... | collective-permute-start | bytes 786440 | tf_op jit(solution)/shard_map/ppermute | solution.py:105
  97.5 1.2 collective-permute-done.7.refs_8_
  98.7 0.0 collective-permute-done.4.refs_5_
  98.7 0.0 collective-permute-done.6.refs_7_
  98.7 0.0 collective-permute-done.5.refs_6_
  98.7 0.0 copy-start
  98.7 1.7 copy-done
  100.5 5.6 %shard_map.86 = (bf16[16,128,256]{2,1,0:T(8,128)(2,1)}, bf16[16,16,256]{2,1,0:T(8,128)(2,1)S(1)}) custom-call(s32[1]{0:T(128)} %bitcast.11.count_ref, s32[80]{0:T(128)S(1)} %bitcast.19, s32[80]{0:T(128)S(1)} %add_bitcast_fusion.places_ref, bf16[80,128,128]{2,1,0:T(8,128)(2,1)S(1)} %bitcast.18, bf16[8,128,256]{2,1,0:T(8,128)(2,1)S(1)} %bitcast.16, ...), custom_call_target="tpu_custom_call" | custom-call | tf_op jit(solution)/shard_map/pallas_call | solution.py:125
  106.1 0.0 copy-start.1
  106.1 12.2 %all_to_all.25.shares_ref = bf16[16,16,256]{2,1,0:T(8,128)(2,1)S(1)} all-to-all(bf16[16,16,256]{2,1,0:T(8,128)(2,1)S(1)} %get-tuple-element.14), channel_id=1, replica_groups=mesh['za'=8,'zb'=4,'core'=2,'x'=4,'y'=4] {'x','y'}, dimensions={0} | all-to-all | bytes 262144 | tf_op jit(solution)/shard_map/all_to_all | solution.py:147
  118.4 10.8 %all_to_all.26 = f32[8,16,256]{2,1,0:T(8,128)S(1)} all-to-all(f32[8,16,256]{2,1,0:T(8,128)S(1)} %broadcast_in_dim.10), channel_id=1, replica_groups=mesh['za'=8,'zb'=4,'core'=2,'x'=4,'y'=4] {'zb','core'}, dimensions={0} | all-to-all | bytes 262144 | tf_op jit(solution)/shard_map/all_to_all | solution.py:94
  129.2 5.6 %all-to-all-start.3 = ((bf16[16,128,256]{2,1,0:T(8,128)(2,1)}), bf16[16,128,256]{2,1,0:T(8,128)(2,1)S(1)}, u32[]{:S(2)}, u32[]{:S(2)}) async-start(bf16[16,128,256]{2,1,0:T(8,128)(2,1)} %get-tuple-element.17), calls=%async_computation.3 | async-start | bytes 2097152 | tf_op jit(solution)/shard_map/all_to_all | solution.py:157
  134.8 36.8 %all-gather.1 = f32[128,256]{1,0:T(8,128)S(1)} all-gather(f32[16,256]{1,0:T(8,128)S(1)} %reduce_sum.18), channel_id=3, replica_groups=mesh['za'=8,'zb'=4,'core'=2,'x'=4,'y'=4] {'za'}, dimensions={0}, use_global_device_ids=true | all-gather | bytes 147456 | tf_op jit(solution)/shard_map/all_gather | solution.py:158
  171.6 0.7 broadcast_in_dim.11
  172.2 7.3 %all-to-all-start.4 = ((bf16[16,16,256]{2,1,0:T(8,128)(2,1)}), bf16[16,16,256]{2,1,0:T(8,128)(2,1)S(1)}, u32[]{:S(2)}, u32[]{:S(2)}) async-start(bf16[16,16,256]{2,1,0:T(8,128)(2,1)} %broadcast_in_dim.11), calls=%async_computation.4 | async-start | bytes 262144 | tf_op jit(solution)/shard_map/all_to_all | solution.py:94
  179.5 0.9 shard_map.88
  180.4 5.0 %all-to-all-done.4 = bf16[16,16,256]{2,1,0:T(8,128)(2,1)S(1)} async-done(((bf16[16,16,256]{2,1,0:T(8,128)(2,1)}), bf16[16,16,256]{2,1,0:T(8,128)(2,1)S(1)}, u32[]{:S(2)}, u32[]{:S(2)}) %all-to-all-start.4) | async-done | bytes 131104 | tf_op jit(solution)/shard_map/all_to_all | solution.py:94
  185.4 0.7 bitcast_convert_fusion
  (17 shorter events, 0.1 us)
Async XLA Ops:
  0.6 18.6 %copy-start.3 = (bf16[128,256]{1,0:T(8,128)(2,1)S(1)}, bf16[128,256]{1,0:T(8,128)(2,1)}, u32[]{:S(2)}) copy-start(bf16[128,256]{1,0:T(8,128)(2,1)} %param.7) | copy-start | bytes 196612
  0.6 96.9 %copy-start.4 = (s32[1,1,80]{2,1,0:T(1,128)S(1)}, s32[1,1,80]{2,1,0:T(1,128)}, u32[]{:S(2)}) copy-start(s32[1,1,80]{2,1,0:T(1,128)} %param.12) | copy-start | bytes 964
  0.7 98.1 %copy-start.2 = (s32[1,1,80]{2,1,0:T(1,128)S(1)}, s32[1,1,80]{2,1,0:T(1,128)}, u32[]{:S(2)}) copy-start(s32[1,1,80]{2,1,0:T(1,128)} %param.11) | copy-start | bytes 964
  2.6 64.0 %all-to-all-start = ((bf16[16,128,256]{2,1,0:T(8,128)(2,1)}), bf16[16,128,256]{2,1,0:T(8,128)(2,1)S(1)}, u32[]{:S(2)}, u32[]{:S(2)}) async-start(bf16[16,128,256]{2,1,0:T(8,128)(2,1)} %broadcast_in_dim.9), calls=%async_computation | async-start | bytes 2097152 | tf_op jit(solution)/shard_map/all_to_all | solution.py:94
  66.6 16.7 %collective-permute-start.1 = (bf16[8,128,256]{2,1,0:T(8,128)(2,1)S(1)}, bf16[8,128,256]{2,1,0:T(8,128)(2,1)S(1)}, u32[]{:S(2)}, u32[]{:S(2)}) collective-permute-start(bf16[8,128,256]{2,1,0:T(8,128)(2,1)S(1)} %bitcast.12), channel_id=1, source_target_pairs={{0,992},{32,0},{64,32},{96,64},{128,96},{160,128},{192,160},{224,1... | collective-permute-start | bytes 1572872 | tf_op jit(solution)/shard_map/ppermute | solution.py:102
  70.1 20.5 %collective-permute-start = (bf16[8,128,256]{2,1,0:T(8,128)(2,1)S(1)}, bf16[8,128,256]{2,1,0:T(8,128)(2,1)S(1)}, u32[]{:S(2)}, u32[]{:S(2)}) collective-permute-start(bf16[8,128,256]{2,1,0:T(8,128)(2,1)S(1)} %bitcast.13), channel_id=1, source_target_pairs={{0,32},{32,64},{64,96},{96,128},{128,160},{160,192},{192,224},{224... | collective-permute-start | bytes 1572872 | tf_op jit(solution)/shard_map/ppermute | solution.py:102
  72.5 20.0 %collective-permute-start.3 = (bf16[4,128,256]{2,1,0:T(8,128)(2,1)S(1)}, bf16[4,128,256]{2,1,0:T(8,128)(2,1)S(1)}, u32[]{:S(2)}, u32[]{:S(2)}) collective-permute-start(bf16[4,128,256]{2,1,0:T(8,128)(2,1)S(1)} %get-tuple-element.20), channel_id=1, source_target_pairs={{0,960},{32,992},{64,0},{96,32},{128,64},{160,96},{192,128},{224,1... | collective-permute-start | bytes 786440 | tf_op jit(solution)/shard_map/ppermute | solution.py:102
  75.5 19.5 %collective-permute-start.2 = (bf16[4,128,256]{2,1,0:T(8,128)(2,1)S(1)}, bf16[4,128,256]{2,1,0:T(8,128)(2,1)}, u32[]{:S(2)}, u32[]{:S(2)}) collective-permute-start(bf16[4,128,256]{2,1,0:T(8,128)(2,1)S(1)} %get-tuple-element.21), channel_id=1, source_target_pairs={{0,64},{32,96},{64,128},{96,160},{128,192},{160,224},{192,256},{22... | collective-permute-start | bytes 786440 | tf_op jit(solution)/shard_map/ppermute | solution.py:102
  83.3 15.4 %collective-permute-start.4 = (bf16[8,128,256]{2,1,0:T(8,128)(2,1)S(1)}, bf16[8,128,256]{2,1,0:T(8,128)(2,1)S(1)}, u32[]{:S(2)}, u32[]{:S(2)}) collective-permute-start(bf16[8,128,256]{2,1,0:T(8,128)(2,1)S(1)} %bitcast.15), channel_id=1, source_target_pairs={{0,16},{16,0},{1,17},{17,1},{2,18},{18,2},{3,19},{19,3},{4,20},{20... | collective-permute-start | bytes 1572872 | tf_op jit(solution)/shard_map/ppermute | solution.py:105
  85.2 13.5 %collective-permute-start.6 = (bf16[8,128,256]{2,1,0:T(8,128)(2,1)S(1)}, bf16[8,128,256]{2,1,0:T(8,128)(2,1)}, u32[]{:S(2)}, u32[]{:S(2)}) collective-permute-start(bf16[8,128,256]{2,1,0:T(8,128)(2,1)S(1)} %collective-permute-done.1.refs_2_), channel_id=1, source_target_pairs={{0,16},{16,0},{1,17},{17,1},{2,18},{18,2},{3,19},{19,3},{4,20},{20... | collective-permute-start | bytes 1572872 | tf_op jit(solution)/shard_map/ppermute | solution.py:105
  90.6 8.1 %collective-permute-start.5 = (bf16[8,128,256]{2,1,0:T(8,128)(2,1)S(1)}, bf16[8,128,256]{2,1,0:T(8,128)(2,1)}, u32[]{:S(2)}, u32[]{:S(2)}) collective-permute-start(bf16[8,128,256]{2,1,0:T(8,128)(2,1)S(1)} %collective-permute-done.refs_1_), channel_id=1, source_target_pairs={{0,16},{16,0},{1,17},{17,1},{2,18},{18,2},{3,19},{19,3},{4,20},{20... | collective-permute-start | bytes 1572872 | tf_op jit(solution)/shard_map/ppermute | solution.py:105
  92.5 5.0 %collective-permute-start.8 = (bf16[4,128,256]{2,1,0:T(8,128)(2,1)S(1)}, bf16[4,128,256]{2,1,0:T(8,128)(2,1)}, u32[]{:S(2)}, u32[]{:S(2)}) collective-permute-start(bf16[4,128,256]{2,1,0:T(8,128)(2,1)S(1)} %collective-permute-done.3.refs_4_), channel_id=1, source_target_pairs={{0,16},{16,0},{1,17},{17,1},{2,18},{18,2},{3,19},{19,3},{4,20},{20... | collective-permute-start | bytes 786440 | tf_op jit(solution)/shard_map/ppermute | solution.py:105
  94.9 3.8 %collective-permute-start.7 = (bf16[4,128,256]{2,1,0:T(8,128)(2,1)}, bf16[4,128,256]{2,1,0:T(8,128)(2,1)}, u32[]{:S(2)}, u32[]{:S(2)}) collective-permute-start(bf16[4,128,256]{2,1,0:T(8,128)(2,1)} %collective-permute-done.2.refs_3_), channel_id=1, source_target_pairs={{0,16},{16,0},{1,17},{17,1},{2,18},{18,2},{3,19},{19,3},{4,20},{20... | collective-permute-start | bytes 786440 | tf_op jit(solution)/shard_map/ppermute | solution.py:105
  98.7 1.7 copy-start
  106.1 73.5 %copy-start.1 = (bf16[256,256]{1,0:T(8,128)(2,1)S(1)}, bf16[256,256]{1,0:T(8,128)(2,1)}, u32[]{:S(2)}) copy-start(bf16[256,256]{1,0:T(8,128)(2,1)} %weight_ref.1) | copy-start | bytes 393220
  129.2 42.4 %all-to-all-start.3 = ((bf16[16,128,256]{2,1,0:T(8,128)(2,1)}), bf16[16,128,256]{2,1,0:T(8,128)(2,1)S(1)}, u32[]{:S(2)}, u32[]{:S(2)}) async-start(bf16[16,128,256]{2,1,0:T(8,128)(2,1)} %get-tuple-element.17), calls=%async_computation.3 | async-start | bytes 2097152 | tf_op jit(solution)/shard_map/all_to_all | solution.py:157
  172.2 13.2 %all-to-all-start.4 = ((bf16[16,16,256]{2,1,0:T(8,128)(2,1)}), bf16[16,16,256]{2,1,0:T(8,128)(2,1)S(1)}, u32[]{:S(2)}, u32[]{:S(2)}) async-start(bf16[16,16,256]{2,1,0:T(8,128)(2,1)} %broadcast_in_dim.11), calls=%async_computation.4 | async-start | bytes 262144 | tf_op jit(solution)/shard_map/all_to_all | solution.py:94

commit v7 on v6

--- a/solution.py
+++ b/solution.py
@@ -11,12 +11,12 @@
 Z = ("za", "zb")
 ROW = Z + ("core",)
 COL = ("x", "y")
+SHARE = ("core", "y")
 
 
 def tiles_kernel(count_ref, rows_ref, places_ref, values_ref, *refs):
     *pieces, features_ref, out_ref, share_ref, gathered, total, copied = refs
     row_tiles, tile, width = total.shape
-    share = features_ref.shape[1] // row_tiles
     copies, first = [], 0
     for index, piece in enumerate(pieces):
         place = gathered.at[first : first + piece.shape[0]]
@@ -60,7 +60,7 @@
             (((0,), (0,)), ((), ())),
             preferred_element_type=jnp.float32,
         )
-    share_ref[...] = grad.astype(jnp.bfloat16).reshape(row_tiles, share, width)
+    share_ref[...] = grad.astype(jnp.bfloat16).reshape(share_ref.shape)
 
 
 def sum_of(parts_ref):
@@ -97,12 +97,10 @@
 def gather_row(grad_out, beside):
     own, beside = lax.optimization_barrier((lax.all_gather(grad_out, "za"), beside))
     half = own.shape[0] // 2
-    pieces = [own]
-    for block, step in ((own, 1), (own, -1), (own[:half], 2), (own[half:], -2)):
-        pieces.append(lax.ppermute(block, Z, shifted(step)))
-    swap = [(0, 1), (1, 0)]
-    first, unused = lax.optimization_barrier((own, pieces[2]))
-    others = [lax.ppermute(piece, "core", swap) for piece in (first, *pieces[1:])]
+    left, right = lax.ppermute(own, Z, shifted(1)), lax.ppermute(own, Z, shifted(-1))
+    low, high = lax.ppermute(left[:half], Z, shifted(1)), lax.ppermute(right[half:], Z, shifted(-1))
+    pieces = [own, left, right, low, high]
+    others = [lax.ppermute(piece, "core", [(0, 1), (1, 0)]) for piece in pieces]
     return *pieces, *others, beside
 
 
@@ -117,7 +115,8 @@
     tile = tile_values.shape[-1]
     width = grad_out.shape[1]
     cols = lax.axis_size(COL)
-    share = width // cols
+    sharers = lax.axis_size(SHARE)
+    share = width // sharers
     own_features = from_all(features, COL).reshape(-1, width)
     *pieces, own_features = gather_row(grad_out, own_features)
     smem, vmem = pl.BlockSpec(memory_space=pltpu.SMEM), pl.BlockSpec(memory_space=pltpu.VMEM)
@@ -126,7 +125,7 @@
         tiles_kernel,
         out_shape=(
             jax.ShapeDtypeStruct((cols, tile, width), jnp.bfloat16),
-            jax.ShapeDtypeStruct((cols, share, width), jnp.bfloat16),
+            jax.ShapeDtypeStruct((sharers, share, width), jnp.bfloat16),
         ),
         in_specs=[smem] * 3 + [vmem] + [anywhere] * len(pieces) + [vmem],
         out_specs=(vmem, vmem),
@@ -144,7 +143,7 @@
         *pieces,
         own_features,
     )
-    shares = lax.all_to_all(shares, COL, 0, 0, tiled=True)
+    shares = lax.all_to_all(shares, SHARE, 0, 0, tiled=True)
     grad_share = pl.pallas_call(
         functools.partial(share_kernel, nodes**-0.5),
         out_shape=jax.ShapeDtypeStruct((share, width), jnp.float32),
@@ -152,12 +151,12 @@
         out_specs=vmem,
         compiler_params=pltpu.CompilerParams(vmem_limit_bytes=4 * 2**20),
     )(shares)
-    grad_share = jnp.sum(from_all(grad_share, ("zb", "core")), axis=0)
+    grad_share = jnp.sum(from_all(grad_share, ("zb", "x")), axis=0)
     grad_share, parts = lax.optimization_barrier((grad_share, parts))
     parts = lax.all_to_all(parts, COL, 0, 0, tiled=True)
     grad_share, parts = lax.optimization_barrier((lax.all_gather(grad_share, "za"), parts))
     grad_share = jnp.sum(grad_share, axis=0).astype(jnp.bfloat16)
-    weight_grad = from_all(grad_share, COL).reshape(width, width).astype(jnp.float32)
+    weight_grad = from_all(grad_share, SHARE).reshape(width, width).astype(jnp.float32)
     input_grad = pl.pallas_call(
         finish_kernel,
         out_shape=jax.ShapeDtypeStruct((tile, width), jnp.bfloat16),

time: 188 us -> 189 us (level)
  blocking collectives: 107 us -> 114 us
  starting transfers between devices: 52.7 us -> 49.2 us
  waiting for transfers between devices: 13.1 us -> 10.5 us
    all_to_all x1, blocking collectives: 10.8 us -> 18.6 us  [from_all(): return lax.all_to_all(same, axes, 0, 0, tiled=True)]
    all_to_all x2, starting transfers between devices: 23.9 us -> 20.9 us  [from_all(): return lax.all_to_all(same, axes, 0, 0, tiled=True)]
    ppermute x9, waiting for transfers between devices: 8.11 us -> 5.82 us  [the longest x1 3.29 us: gather_row(): lax.ppermute(own, Z, shifted(-1))]
where the time goes in v7:
time: 189 us; the launch traced here: 187 us
  blocking collectives  114 us (60%)
  starting transfers between devices  49.2 us (26%)
  waiting for transfers between devices  10.5 us (6%)
  Pallas kernels  5.71 us (3%)
  local copies, waits for them, and re-layouts  5.42 us (3%)
    all_gather x1, blocking collectives, gather_row(): lax.all_gather(grad_out, 'za')  47.4 us
    all_gather x1, blocking collectives, body(): lax.all_gather(grad_share, 'za')  36.9 us
    all_to_all x2, starting transfers between devices, from_all(): return lax.all_to_all(same, axes, 0, 0, tiled=True)  20.9 us
    all_to_all x1, blocking collectives, from_all(): return lax.all_to_all(same, axes, 0, 0, tiled=True)  18.6 us
    all_to_all x1, blocking collectives, body(): shares = lax.all_to_all(shares, SHARE, 0, 0, tiled=True)  11.2 us
    ppermute x5, starting transfers between devices, gather_row(): others = [lax.ppermute(piece, 'core', [(0, 1), (1, 0)]) for piece in pieces]  10.1 us
    all_to_all x1, starting transfers between devices, body(): parts = lax.all_to_all(parts, COL, 0, 0, tiled=True)  5.86 us
    pallas_call x1, Pallas kernels, body(): pl.pallas_call(tiles_kernel, out_shape=(jax.ShapeDtypeStruct((cols, tile,...  4.78 us
  transfers between devices with their start and end apart: 12, of which 4 were waited for; matrix products, arithmetic and copies ran while one was open for 0% of the time, Pallas kernels for 0%

profile of v7, /device:TPU:6, one launch (start us, length us, event | category | flops | bytes accessed | tf_op | source)
XLA Modules:
  0.0 187.2 jit_solution(1514139379281631959)
XLA Ops:
  0.7 1.9 %broadcast_in_dim.9 = bf16[16,128,256]{2,1,0:T(8,128)(2,1)} broadcast(bf16[128,256]{1,0:T(8,128)(2,1)} %param.8), dimensions={1,2} | broadcast | bytes 1114112 | tf_op jit(solution)/shard_map/broadcast_in_dim | solution.py:93
  2.6 16.6 %all-to-all-start = ((bf16[16,128,256]{2,1,0:T(8,128)(2,1)}), bf16[16,128,256]{2,1,0:T(8,128)(2,1)S(1)}, u32[]{:S(2)}, u32[]{:S(2)}) async-start(bf16[16,128,256]{2,1,0:T(8,128)(2,1)} %broadcast_in_dim.9), calls=%async_computation | async-start | bytes 2097152 | tf_op jit(solution)/shard_map/all_to_all | solution.py:94
  19.3 47.4 %all-gather = bf16[1024,256]{1,0:T(8,128)(2,1)S(1)} all-gather(bf16[128,256]{1,0:T(8,128)(2,1)S(1)} %copy-done.4), channel_id=2, replica_groups=mesh['za'=8,'zb'=4,'core'=2,'x'=4,'y'=4] {'za'}, dimensions={0}, use_global_device_ids=true | all-gather | bytes 589824 | tf_op jit(solution)/shard_map/all_gather | solution.py:98
  66.6 3.4 %collective-permute-start.1 = (bf16[8,128,256]{2,1,0:T(8,128)(2,1)S(1)}, bf16[8,128,256]{2,1,0:T(8,128)(2,1)S(1)}, u32[]{:S(2)}, u32[]{:S(2)}) collective-permute-start(bf16[8,128,256]{2,1,0:T(8,128)(2,1)S(1)} %bitcast.14), channel_id=1, source_target_pairs={{0,992},{32,0},{64,32},{96,64},{128,96},{160,128},{192,160},{224,1... | collective-permute-start | bytes 1572872 | tf_op jit(solution)/shard_map/ppermute | solution.py:100
  70.1 2.4 %collective-permute-start = (bf16[8,128,256]{2,1,0:T(8,128)(2,1)S(1)}, bf16[8,128,256]{2,1,0:T(8,128)(2,1)S(1)}, u32[]{:S(2)}, u32[]{:S(2)}) collective-permute-start(bf16[8,128,256]{2,1,0:T(8,128)(2,1)S(1)} %bitcast.15), channel_id=1, source_target_pairs={{0,32},{32,64},{64,96},{96,128},{128,160},{160,192},{192,224},{224... | collective-permute-start | bytes 1572872 | tf_op jit(solution)/shard_map/ppermute | solution.py:100
  72.5 1.9 %collective-permute-start.4 = (bf16[8,128,256]{2,1,0:T(8,128)(2,1)S(1)}, bf16[8,128,256]{2,1,0:T(8,128)(2,1)S(1)}, u32[]{:S(2)}, u32[]{:S(2)}) collective-permute-start(bf16[8,128,256]{2,1,0:T(8,128)(2,1)S(1)} %bitcast.16), channel_id=1, source_target_pairs={{0,16},{16,0},{1,17},{17,1},{2,18},{18,2},{3,19},{19,3},{4,20},{20... | collective-permute-start | bytes 1572872 | tf_op jit(solution)/shard_map/ppermute | solution.py:103
  74.4 3.3 %collective-permute-done.1.refs_2_ = bf16[8,128,256]{2,1,0:T(8,128)(2,1)S(1)} collective-permute-done((bf16[8,128,256]{2,1,0:T(8,128)(2,1)S(1)}, bf16[8,128,256]{2,1,0:T(8,128)(2,1)S(1)}, u32[]{:S(2)}, u32[]{:S(2)}) %collective-permute-start.1) | collective-permute-done | bytes 524320 | tf_op jit(solution)/shard_map/ppermute | solution.py:100
  77.7 4.7 %collective-permute-start.3 = (bf16[4,128,256]{2,1,0:T(8,128)(2,1)S(1)}, bf16[4,128,256]{2,1,0:T(8,128)(2,1)S(1)}, u32[]{:S(2)}, u32[]{:S(2)}) collective-permute-start(bf16[4,128,256]{2,1,0:T(8,128)(2,1)S(1)} %slice.9), channel_id=1, source_target_pairs={{0,992},{32,0},{64,32},{96,64},{128,96},{160,128},{192,160},{224,1... | collective-permute-start | bytes 786440 | tf_op jit(solution)/shard_map/ppermute | solution.py:101
  82.4 0.0 collective-permute-done.refs_1_
  82.4 1.9 %collective-permute-start.2 = (bf16[4,128,256]{2,1,0:T(8,128)(2,1)S(1)}, bf16[4,128,256]{2,1,0:T(8,128)(2,1)}, u32[]{:S(2)}, u32[]{:S(2)}) collective-permute-start(bf16[4,128,256]{2,1,0:T(8,128)(2,1)S(1)} %slice.8), channel_id=1, source_target_pairs={{0,32},{32,64},{64,96},{96,128},{128,160},{160,192},{192,224},{224... | collective-permute-start | bytes 786440 | tf_op jit(solution)/shard_map/ppermute | solution.py:101
  84.4 1.9 %collective-permute-start.6 = (bf16[8,128,256]{2,1,0:T(8,128)(2,1)S(1)}, bf16[8,128,256]{2,1,0:T(8,128)(2,1)}, u32[]{:S(2)}, u32[]{:S(2)}) collective-permute-start(bf16[8,128,256]{2,1,0:T(8,128)(2,1)S(1)} %collective-permute-done.1.refs_2_), channel_id=1, source_target_pairs={{0,16},{16,0},{1,17},{17,1},{2,18},{18,2},{3,19},{19,3},{4,20},{20... | collective-permute-start | bytes 1572872 | tf_op jit(solution)/shard_map/ppermute | solution.py:103
  86.3 2.4 %collective-permute-start.5 = (bf16[8,128,256]{2,1,0:T(8,128)(2,1)S(1)}, bf16[8,128,256]{2,1,0:T(8,128)(2,1)}, u32[]{:S(2)}, u32[]{:S(2)}) collective-permute-start(bf16[8,128,256]{2,1,0:T(8,128)(2,1)S(1)} %collective-permute-done.refs_1_), channel_id=1, source_target_pairs={{0,16},{16,0},{1,17},{17,1},{2,18},{18,2},{3,19},{19,3},{4,20},{20... | collective-permute-start | bytes 1572872 | tf_op jit(solution)/shard_map/ppermute | solution.py:103
  88.7 0.0 collective-permute-done.3.refs_4_
  88.7 1.9 %collective-permute-start.8 = (bf16[4,128,256]{2,1,0:T(8,128)(2,1)S(1)}, bf16[4,128,256]{2,1,0:T(8,128)(2,1)}, u32[]{:S(2)}, u32[]{:S(2)}) collective-permute-start(bf16[4,128,256]{2,1,0:T(8,128)(2,1)S(1)} %collective-permute-done.3.refs_4_), channel_id=1, source_target_pairs={{0,16},{16,0},{1,17},{17,1},{2,18},{18,2},{3,19},{19,3},{4,20},{20... | collective-permute-start | bytes 786440 | tf_op jit(solution)/shard_map/ppermute | solution.py:103
  90.7 1.4 collective-permute-done.2.refs_3_
  92.0 1.9 %collective-permute-start.7 = (bf16[4,128,256]{2,1,0:T(8,128)(2,1)}, bf16[4,128,256]{2,1,0:T(8,128)(2,1)}, u32[]{:S(2)}, u32[]{:S(2)}) collective-permute-start(bf16[4,128,256]{2,1,0:T(8,128)(2,1)} %collective-permute-done.2.refs_3_), channel_id=1, source_target_pairs={{0,16},{16,0},{1,17},{17,1},{2,18},{18,2},{3,19},{19,3},{4,20},{20... | collective-permute-start | bytes 786440 | tf_op jit(solution)/shard_map/ppermute | solution.py:103
  94.6 1.1 collective-permute-done.7.refs_8_
  95.8 0.0 collective-permute-done.6.refs_7_
  95.8 0.0 copy-start
  95.8 1.7 copy-done
  97.5 4.8 %shard_map.86 = (bf16[16,128,256]{2,1,0:T(8,128)(2,1)S(1)}, bf16[8,32,256]{2,1,0:T(8,128)(2,1)S(1)}) custom-call(s32[1]{0:T(128)} %bitcast.11.count_ref, s32[80]{0:T(128)S(1)} %bitcast.18, s32[80]{0:T(128)S(1)} %add_bitcast_fusion.places_ref, bf16[80,128,128]{2,1,0:T(8,128)(2,1)S(1)} %bitcast.13, bf16[8,128,256]{2,1,0:T(8,128)(2,1)S(1)} %bitcast.17, ...), custom_call_target="tpu_custom_call" | custom-call | tf_op jit(solution)/shard_map/pallas_call | solution.py:124
  102.3 1.0 copy-done.1
  103.3 11.2 %all_to_all.25.shares_ref = bf16[8,32,256]{2,1,0:T(8,128)(2,1)S(1)} all-to-all(bf16[8,32,256]{2,1,0:T(8,128)(2,1)S(1)} %get-tuple-element.12), channel_id=1, replica_groups=mesh['za'=8,'zb'=4,'core'=2,'x'=4,'y'=4] {'core','y'}, dimensions={0} | all-to-all | bytes 262144 | tf_op jit(solution)/shard_map/all_to_all | solution.py:146
  114.5 0.0 copy-start.2
  114.6 18.6 %all_to_all.26 = f32[16,32,256]{2,1,0:T(8,128)S(1)} all-to-all(f32[16,32,256]{2,1,0:T(8,128)S(1)} %broadcast_in_dim.10), channel_id=1, replica_groups=mesh['za'=8,'zb'=4,'core'=2,'x'=4,'y'=4] {'zb','x'}, dimensions={0} | all-to-all | bytes 1048576 | tf_op jit(solution)/shard_map/all_to_all | solution.py:94
  133.2 5.9 %all-to-all-start.3 = ((bf16[16,128,256]{2,1,0:T(8,128)(2,1)}), bf16[16,128,256]{2,1,0:T(8,128)(2,1)S(1)}, u32[]{:S(2)}, u32[]{:S(2)}) async-start(bf16[16,128,256]{2,1,0:T(8,128)(2,1)} %copy-done.1), calls=%async_computation.3 | async-start | bytes 2097152 | tf_op jit(solution)/shard_map/all_to_all | solution.py:156
  139.1 36.9 %all-gather.1 = f32[256,256]{1,0:T(8,128)S(1)} all-gather(f32[32,256]{1,0:T(8,128)S(1)} %reduce_sum.18), channel_id=3, replica_groups=mesh['za'=8,'zb'=4,'core'=2,'x'=4,'y'=4] {'za'}, dimensions={0}, use_global_device_ids=true | all-gather | bytes 294912 | tf_op jit(solution)/shard_map/all_gather | solution.py:157
  176.0 0.7 broadcast_in_dim.11
  176.7 4.2 %all-to-all-start.4 = ((bf16[8,32,256]{2,1,0:T(8,128)(2,1)}), bf16[8,32,256]{2,1,0:T(8,128)(2,1)S(1)}, u32[]{:S(2)}, u32[]{:S(2)}) async-start(bf16[8,32,256]{2,1,0:T(8,128)(2,1)} %broadcast_in_dim.11), calls=%async_computation.4 | async-start | bytes 262144 | tf_op jit(solution)/shard_map/all_to_all | solution.py:94
  180.9 0.9 shard_map.88
  181.8 4.6 %all-to-all-done.4 = bf16[8,32,256]{2,1,0:T(8,128)(2,1)S(1)} async-done(((bf16[8,32,256]{2,1,0:T(8,128)(2,1)}), bf16[8,32,256]{2,1,0:T(8,128)(2,1)S(1)}, u32[]{:S(2)}, u32[]{:S(2)}) %all-to-all-start.4) | async-done | bytes 131104 | tf_op jit(solution)/shard_map/all_to_all | solution.py:94
  186.5 0.7 bitcast_convert_fusion
  (20 shorter events, 0.2 us)
Async XLA Ops:
  0.6 18.6 %copy-start.4 = (bf16[128,256]{1,0:T(8,128)(2,1)S(1)}, bf16[128,256]{1,0:T(8,128)(2,1)}, u32[]{:S(2)}) copy-start(bf16[128,256]{1,0:T(8,128)(2,1)} %param.7) | copy-start | bytes 196612
  0.6 94.0 %copy-start.5 = (s32[1,1,80]{2,1,0:T(1,128)S(1)}, s32[1,1,80]{2,1,0:T(1,128)}, u32[]{:S(2)}) copy-start(s32[1,1,80]{2,1,0:T(1,128)} %param.12) | copy-start | bytes 964
  0.7 95.1 %copy-start.3 = (s32[1,1,80]{2,1,0:T(1,128)S(1)}, s32[1,1,80]{2,1,0:T(1,128)}, u32[]{:S(2)}) copy-start(s32[1,1,80]{2,1,0:T(1,128)} %param.11) | copy-start | bytes 964
  2.6 64.0 %all-to-all-start = ((bf16[16,128,256]{2,1,0:T(8,128)(2,1)}), bf16[16,128,256]{2,1,0:T(8,128)(2,1)S(1)}, u32[]{:S(2)}, u32[]{:S(2)}) async-start(bf16[16,128,256]{2,1,0:T(8,128)(2,1)} %broadcast_in_dim.9), calls=%async_computation | async-start | bytes 2097152 | tf_op jit(solution)/shard_map/all_to_all | solution.py:94
  66.6 11.1 %collective-permute-start.1 = (bf16[8,128,256]{2,1,0:T(8,128)(2,1)S(1)}, bf16[8,128,256]{2,1,0:T(8,128)(2,1)S(1)}, u32[]{:S(2)}, u32[]{:S(2)}) collective-permute-start(bf16[8,128,256]{2,1,0:T(8,128)(2,1)S(1)} %bitcast.14), channel_id=1, source_target_pairs={{0,992},{32,0},{64,32},{96,64},{128,96},{160,128},{192,160},{224,1... | collective-permute-start | bytes 1572872 | tf_op jit(solution)/shard_map/ppermute | solution.py:100
  70.1 12.3 %collective-permute-start = (bf16[8,128,256]{2,1,0:T(8,128)(2,1)S(1)}, bf16[8,128,256]{2,1,0:T(8,128)(2,1)S(1)}, u32[]{:S(2)}, u32[]{:S(2)}) collective-permute-start(bf16[8,128,256]{2,1,0:T(8,128)(2,1)S(1)} %bitcast.15), channel_id=1, source_target_pairs={{0,32},{32,64},{64,96},{96,128},{128,160},{160,192},{192,224},{224... | collective-permute-start | bytes 1572872 | tf_op jit(solution)/shard_map/ppermute | solution.py:100
  72.5 22.1 %collective-permute-start.4 = (bf16[8,128,256]{2,1,0:T(8,128)(2,1)S(1)}, bf16[8,128,256]{2,1,0:T(8,128)(2,1)S(1)}, u32[]{:S(2)}, u32[]{:S(2)}) collective-permute-start(bf16[8,128,256]{2,1,0:T(8,128)(2,1)S(1)} %bitcast.16), channel_id=1, source_target_pairs={{0,16},{16,0},{1,17},{17,1},{2,18},{18,2},{3,19},{19,3},{4,20},{20... | collective-permute-start | bytes 1572872 | tf_op jit(solution)/shard_map/ppermute | solution.py:103
  77.7 11.0 %collective-permute-start.3 = (bf16[4,128,256]{2,1,0:T(8,128)(2,1)S(1)}, bf16[4,128,256]{2,1,0:T(8,128)(2,1)S(1)}, u32[]{:S(2)}, u32[]{:S(2)}) collective-permute-start(bf16[4,128,256]{2,1,0:T(8,128)(2,1)S(1)} %slice.9), channel_id=1, source_target_pairs={{0,992},{32,0},{64,32},{96,64},{128,96},{160,128},{192,160},{224,1... | collective-permute-start | bytes 786440 | tf_op jit(solution)/shard_map/ppermute | solution.py:101
  82.4 9.6 %collective-permute-start.2 = (bf16[4,128,256]{2,1,0:T(8,128)(2,1)S(1)}, bf16[4,128,256]{2,1,0:T(8,128)(2,1)}, u32[]{:S(2)}, u32[]{:S(2)}) collective-permute-start(bf16[4,128,256]{2,1,0:T(8,128)(2,1)S(1)} %slice.8), channel_id=1, source_target_pairs={{0,32},{32,64},{64,96},{96,128},{128,160},{160,192},{192,224},{224... | collective-permute-start | bytes 786440 | tf_op jit(solution)/shard_map/ppermute | solution.py:101
  84.4 11.4 %collective-permute-start.6 = (bf16[8,128,256]{2,1,0:T(8,128)(2,1)S(1)}, bf16[8,128,256]{2,1,0:T(8,128)(2,1)}, u32[]{:S(2)}, u32[]{:S(2)}) collective-permute-start(bf16[8,128,256]{2,1,0:T(8,128)(2,1)S(1)} %collective-permute-done.1.refs_2_), channel_id=1, source_target_pairs={{0,16},{16,0},{1,17},{17,1},{2,18},{18,2},{3,19},{19,3},{4,20},{20... | collective-permute-start | bytes 1572872 | tf_op jit(solution)/shard_map/ppermute | solution.py:103
  86.3 9.5 %collective-permute-start.5 = (bf16[8,128,256]{2,1,0:T(8,128)(2,1)S(1)}, bf16[8,128,256]{2,1,0:T(8,128)(2,1)}, u32[]{:S(2)}, u32[]{:S(2)}) collective-permute-start(bf16[8,128,256]{2,1,0:T(8,128)(2,1)S(1)} %collective-permute-done.refs_1_), channel_id=1, source_target_pairs={{0,16},{16,0},{1,17},{17,1},{2,18},{18,2},{3,19},{19,3},{4,20},{20... | collective-permute-start | bytes 1572872 | tf_op jit(solution)/shard_map/ppermute | solution.py:103
  88.7 5.9 %collective-permute-start.8 = (bf16[4,128,256]{2,1,0:T(8,128)(2,1)S(1)}, bf16[4,128,256]{2,1,0:T(8,128)(2,1)}, u32[]{:S(2)}, u32[]{:S(2)}) collective-permute-start(bf16[4,128,256]{2,1,0:T(8,128)(2,1)S(1)} %collective-permute-done.3.refs_4_), channel_id=1, source_target_pairs={{0,16},{16,0},{1,17},{17,1},{2,18},{18,2},{3,19},{19,3},{4,20},{20... | collective-permute-start | bytes 786440 | tf_op jit(solution)/shard_map/ppermute | solution.py:103
  92.0 3.8 %collective-permute-start.7 = (bf16[4,128,256]{2,1,0:T(8,128)(2,1)}, bf16[4,128,256]{2,1,0:T(8,128)(2,1)}, u32[]{:S(2)}, u32[]{:S(2)}) collective-permute-start(bf16[4,128,256]{2,1,0:T(8,128)(2,1)} %collective-permute-done.2.refs_3_), channel_id=1, source_target_pairs={{0,16},{16,0},{1,17},{17,1},{2,18},{18,2},{3,19},{19,3},{4,20},{20... | collective-permute-start | bytes 786440 | tf_op jit(solution)/shard_map/ppermute | solution.py:103
  95.8 1.7 copy-start
  102.3 1.0 copy-start.1
  114.5 66.4 %copy-start.2 = (bf16[256,256]{1,0:T(8,128)(2,1)S(1)}, bf16[256,256]{1,0:T(8,128)(2,1)}, u32[]{:S(2)}) copy-start(bf16[256,256]{1,0:T(8,128)(2,1)} %weight_ref.1) | copy-start | bytes 393220
  133.2 42.8 %all-to-all-start.3 = ((bf16[16,128,256]{2,1,0:T(8,128)(2,1)}), bf16[16,128,256]{2,1,0:T(8,128)(2,1)S(1)}, u32[]{:S(2)}, u32[]{:S(2)}) async-start(bf16[16,128,256]{2,1,0:T(8,128)(2,1)} %copy-done.1), calls=%async_computation.3 | async-start | bytes 2097152 | tf_op jit(solution)/shard_map/all_to_all | solution.py:156
  176.7 9.8 %all-to-all-start.4 = ((bf16[8,32,256]{2,1,0:T(8,128)(2,1)}), bf16[8,32,256]{2,1,0:T(8,128)(2,1)S(1)}, u32[]{:S(2)}, u32[]{:S(2)}) async-start(bf16[8,32,256]{2,1,0:T(8,128)(2,1)} %broadcast_in_dim.11), calls=%async_computation.4 | async-start | bytes 262144 | tf_op jit(solution)/shard_map/all_to_all | solution.py:94

commit v8 on v6

--- a/solution.py
+++ b/solution.py
@@ -16,7 +16,6 @@
 def tiles_kernel(count_ref, rows_ref, places_ref, values_ref, *refs):
     *pieces, features_ref, out_ref, share_ref, gathered, total, copied = refs
     row_tiles, tile, width = total.shape
-    share = features_ref.shape[1] // row_tiles
     copies, first = [], 0
     for index, piece in enumerate(pieces):
         place = gathered.at[first : first + piece.shape[0]]
@@ -60,7 +59,7 @@
             (((0,), (0,)), ((), ())),
             preferred_element_type=jnp.float32,
         )
-    share_ref[...] = grad.astype(jnp.bfloat16).reshape(row_tiles, share, width)
+    share_ref[...] = grad.astype(jnp.bfloat16).reshape(share_ref.shape)
 
 
 def sum_of(parts_ref):
@@ -96,13 +95,9 @@
 
 def gather_row(grad_out, beside):
     own, beside = lax.optimization_barrier((lax.all_gather(grad_out, "za"), beside))
-    half = own.shape[0] // 2
-    pieces = [own]
-    for block, step in ((own, 1), (own, -1), (own[:half], 2), (own[half:], -2)):
-        pieces.append(lax.ppermute(block, Z, shifted(step)))
-    swap = [(0, 1), (1, 0)]
-    first, unused = lax.optimization_barrier((own, pieces[2]))
-    others = [lax.ppermute(piece, "core", swap) for piece in (first, *pieces[1:])]
+    left, right = lax.ppermute(own, Z, shifted(1)), lax.ppermute(own, Z, shifted(-1))
+    pieces = [own, left, right, lax.ppermute(right, Z, shifted(-1))]
+    others = [lax.ppermute(piece, "core", [(0, 1), (1, 0)]) for piece in pieces]
     return *pieces, *others, beside
 
 

time: 188 us -> 184 us (0.979)
  starting transfers between devices: 52.7 us -> 47.4 us
    ppermute x9 -> x7, starting transfers between devices: 23.1 us -> 17.7 us  [the longest x4 8.16 us: gather_row(): others = [lax.ppermute(piece, 'core', [(0, 1), (1, 0)]) for piece in pieces]]
    all_to_all x1, blocking collectives: 12.2 us -> 15.8 us  [body(): shares = lax.all_to_all(shares, COL, 0, 0, tiled=True)]
    ppermute x9 -> x7, waiting for transfers between devices: 8.11 us -> 9.24 us  [the longest x1 6.88 us: gather_row(): lax.ppermute(own, Z, shifted(-1))]
  transfers between devices with their start and end apart: 12 -> 10, of which waited for: 4 -> 4; matrix products, arithmetic and copies ran while one was open for 0% -> 0% of each run, Pallas kernels for 0% -> 0%
where the time goes in v8:
time: 184 us; the launch traced here: 183 us
  blocking collectives  108 us (59%)
  starting transfers between devices  47.4 us (26%)
  waiting for transfers between devices  14.2 us (8%)
  Pallas kernels  6.53 us (4%)
  local copies, waits for them, and re-layouts  4.38 us (2%)
    all_gather x1, blocking collectives, gather_row(): lax.all_gather(grad_out, 'za')  47.4 us
    all_gather x1, blocking collectives, body(): lax.all_gather(grad_share, 'za')  35.6 us
    all_to_all x2, starting transfers between devices, from_all(): return lax.all_to_all(same, axes, 0, 0, tiled=True)  24 us
    all_to_all x1, blocking collectives, body(): shares = lax.all_to_all(shares, COL, 0, 0, tiled=True)  15.8 us
    all_to_all x1, blocking collectives, from_all(): return lax.all_to_all(same, axes, 0, 0, tiled=True)  9.19 us
    ppermute x4, starting transfers between devices, gather_row(): others = [lax.ppermute(piece, 'core', [(0, 1), (1, 0)]) for piece in pieces]  8.16 us
    ppermute x1, waiting for transfers between devices, gather_row(): lax.ppermute(own, Z, shifted(-1))  6.88 us
    all_to_all x1, starting transfers between devices, body(): parts = lax.all_to_all(parts, COL, 0, 0, tiled=True)  5.74 us
  transfers between devices with their start and end apart: 10, of which 4 were waited for; matrix products, arithmetic and copies ran while one was open for 0% of the time, Pallas kernels for 0%

profile of v8, /device:TPU:6, one launch (start us, length us, event | category | flops | bytes accessed | tf_op | source)
XLA Modules:
  0.0 182.8 jit_solution(5044690360122010587)
XLA Ops:
  0.6 0.0 copy-start.3
  0.7 1.9 %broadcast_in_dim.9 = bf16[16,128,256]{2,1,0:T(8,128)(2,1)} broadcast(bf16[128,256]{1,0:T(8,128)(2,1)} %param.8), dimensions={1,2} | broadcast | bytes 1114112 | tf_op jit(solution)/shard_map/broadcast_in_dim | solution.py:92
  2.6 16.6 %all-to-all-start = ((bf16[16,128,256]{2,1,0:T(8,128)(2,1)}), bf16[16,128,256]{2,1,0:T(8,128)(2,1)S(1)}, u32[]{:S(2)}, u32[]{:S(2)}) async-start(bf16[16,128,256]{2,1,0:T(8,128)(2,1)} %broadcast_in_dim.9), calls=%async_computation | async-start | bytes 2097152 | tf_op jit(solution)/shard_map/all_to_all | solution.py:93
  19.3 47.4 %all-gather = bf16[1024,256]{1,0:T(8,128)(2,1)S(1)} all-gather(bf16[128,256]{1,0:T(8,128)(2,1)S(1)} %copy-done.3), channel_id=2, replica_groups=mesh['za'=8,'zb'=4,'core'=2,'x'=4,'y'=4] {'za'}, dimensions={0}, use_global_device_ids=true | all-gather | bytes 589824 | tf_op jit(solution)/shard_map/all_gather | solution.py:97
  66.6 0.0 all-to-all-done
  66.6 3.4 %collective-permute-start.1 = (bf16[8,128,256]{2,1,0:T(8,128)(2,1)S(1)}, bf16[8,128,256]{2,1,0:T(8,128)(2,1)S(1)}, u32[]{:S(2)}, u32[]{:S(2)}) collective-permute-start(bf16[8,128,256]{2,1,0:T(8,128)(2,1)S(1)} %bitcast.14), channel_id=1, source_target_pairs={{0,992},{32,0},{64,32},{96,64},{128,96},{160,128},{192,160},{224,1... | collective-permute-start | bytes 1572872 | tf_op jit(solution)/shard_map/ppermute | solution.py:98
  70.1 2.4 %collective-permute-start = (bf16[8,128,256]{2,1,0:T(8,128)(2,1)S(1)}, bf16[8,128,256]{2,1,0:T(8,128)(2,1)S(1)}, u32[]{:S(2)}, u32[]{:S(2)}) collective-permute-start(bf16[8,128,256]{2,1,0:T(8,128)(2,1)S(1)} %bitcast.15), channel_id=1, source_target_pairs={{0,32},{32,64},{64,96},{96,128},{128,160},{160,192},{192,224},{224... | collective-permute-start | bytes 1572872 | tf_op jit(solution)/shard_map/ppermute | solution.py:98
  72.5 6.9 %collective-permute-done.1.refs_2_ = bf16[8,128,256]{2,1,0:T(8,128)(2,1)S(1)} collective-permute-done((bf16[8,128,256]{2,1,0:T(8,128)(2,1)S(1)}, bf16[8,128,256]{2,1,0:T(8,128)(2,1)S(1)}, u32[]{:S(2)}, u32[]{:S(2)}) %collective-permute-start.1) | collective-permute-done | bytes 524320 | tf_op jit(solution)/shard_map/ppermute | solution.py:98
  79.4 3.7 %collective-permute-start.2 = (bf16[8,128,256]{2,1,0:T(8,128)(2,1)S(1)}, bf16[8,128,256]{2,1,0:T(8,128)(2,1)S(1)}, u32[]{:S(2)}, u32[]{:S(2)}) collective-permute-start(bf16[8,128,256]{2,1,0:T(8,128)(2,1)S(1)} %collective-permute-done.1.refs_2_), channel_id=1, source_target_pairs={{0,992},{32,0},{64,32},{96,64},{128,96},{160,128},{192,160},{224,1... | collective-permute-start | bytes 1572872 | tf_op jit(solution)/shard_map/ppermute | solution.py:99
  83.1 1.9 %collective-permute-start.3 = (bf16[8,128,256]{2,1,0:T(8,128)(2,1)S(1)}, bf16[8,128,256]{2,1,0:T(8,128)(2,1)}, u32[]{:S(2)}, u32[]{:S(2)}) collective-permute-start(bf16[8,128,256]{2,1,0:T(8,128)(2,1)S(1)} %bitcast.16), channel_id=1, source_target_pairs={{0,16},{16,0},{1,17},{17,1},{2,18},{18,2},{3,19},{19,3},{4,20},{20... | collective-permute-start | bytes 1572872 | tf_op jit(solution)/shard_map/ppermute | solution.py:100
  85.0 2.4 %collective-permute-start.5 = (bf16[8,128,256]{2,1,0:T(8,128)(2,1)S(1)}, bf16[8,128,256]{2,1,0:T(8,128)(2,1)}, u32[]{:S(2)}, u32[]{:S(2)}) collective-permute-start(bf16[8,128,256]{2,1,0:T(8,128)(2,1)S(1)} %collective-permute-done.1.refs_2_), channel_id=1, source_target_pairs={{0,16},{16,0},{1,17},{17,1},{2,18},{18,2},{3,19},{19,3},{4,20},{20... | collective-permute-start | bytes 1572872 | tf_op jit(solution)/shard_map/ppermute | solution.py:100
  87.5 0.0 collective-permute-done.refs_1_
  87.5 1.9 %collective-permute-start.4 = (bf16[8,128,256]{2,1,0:T(8,128)(2,1)S(1)}, bf16[8,128,256]{2,1,0:T(8,128)(2,1)}, u32[]{:S(2)}, u32[]{:S(2)}) collective-permute-start(bf16[8,128,256]{2,1,0:T(8,128)(2,1)S(1)} %collective-permute-done.refs_1_), channel_id=1, source_target_pairs={{0,16},{16,0},{1,17},{17,1},{2,18},{18,2},{3,19},{19,3},{4,20},{20... | collective-permute-start | bytes 1572872 | tf_op jit(solution)/shard_map/ppermute | solution.py:100
  89.4 1.0 collective-permute-done.2.refs_3_
  90.4 1.9 %collective-permute-start.6 = (bf16[8,128,256]{2,1,0:T(8,128)(2,1)S(1)}, bf16[8,128,256]{2,1,0:T(8,128)(2,1)}, u32[]{:S(2)}, u32[]{:S(2)}) collective-permute-start(bf16[8,128,256]{2,1,0:T(8,128)(2,1)S(1)} %collective-permute-done.2.refs_3_), channel_id=1, source_target_pairs={{0,16},{16,0},{1,17},{17,1},{2,18},{18,2},{3,19},{19,3},{4,20},{20... | collective-permute-start | bytes 1572872 | tf_op jit(solution)/shard_map/ppermute | solution.py:100
  93.0 0.0 collective-permute-done.3.refs_4_
  93.0 0.0 collective-permute-done.5.refs_6_
  93.1 0.0 collective-permute-done.4.refs_5_
  93.1 1.3 collective-permute-done.6.refs_7_
  94.4 1.7 copy-done
  96.1 5.6 %shard_map.86 = (bf16[16,128,256]{2,1,0:T(8,128)(2,1)}, bf16[16,16,256]{2,1,0:T(8,128)(2,1)S(1)}) custom-call(s32[1]{0:T(128)} %bitcast.11.count_ref, s32[80]{0:T(128)S(1)} %bitcast.18, s32[80]{0:T(128)S(1)} %add_bitcast_fusion.places_ref, bf16[80,128,128]{2,1,0:T(8,128)(2,1)S(1)} %bitcast.13, bf16[8,128,256]{2,1,0:T(8,128)(2,1)S(1)} %bitcast.17, ...), custom_call_target="tpu_custom_call" | custom-call | tf_op jit(solution)/shard_map/pallas_call | solution.py:120
  101.7 0.0 copy-start.1
  101.7 15.8 %all_to_all.25.shares_ref = bf16[16,16,256]{2,1,0:T(8,128)(2,1)S(1)} all-to-all(bf16[16,16,256]{2,1,0:T(8,128)(2,1)S(1)} %get-tuple-element.12), channel_id=1, replica_groups=mesh['za'=8,'zb'=4,'core'=2,'x'=4,'y'=4] {'x','y'}, dimensions={0} | all-to-all | bytes 262144 | tf_op jit(solution)/shard_map/all_to_all | solution.py:142
  117.6 9.2 %all_to_all.26 = f32[8,16,256]{2,1,0:T(8,128)S(1)} all-to-all(f32[8,16,256]{2,1,0:T(8,128)S(1)} %broadcast_in_dim.10), channel_id=1, replica_groups=mesh['za'=8,'zb'=4,'core'=2,'x'=4,'y'=4] {'zb','core'}, dimensions={0} | all-to-all | bytes 262144 | tf_op jit(solution)/shard_map/all_to_all | solution.py:93
  126.8 5.7 %all-to-all-start.3 = ((bf16[16,128,256]{2,1,0:T(8,128)(2,1)}), bf16[16,128,256]{2,1,0:T(8,128)(2,1)S(1)}, u32[]{:S(2)}, u32[]{:S(2)}) async-start(bf16[16,128,256]{2,1,0:T(8,128)(2,1)} %get-tuple-element.15), calls=%async_computation.3 | async-start | bytes 2097152 | tf_op jit(solution)/shard_map/all_to_all | solution.py:152
  132.6 35.6 %all-gather.1 = f32[128,256]{1,0:T(8,128)S(1)} all-gather(f32[16,256]{1,0:T(8,128)S(1)} %reduce_sum.18), channel_id=3, replica_groups=mesh['za'=8,'zb'=4,'core'=2,'x'=4,'y'=4] {'za'}, dimensions={0}, use_global_device_ids=true | all-gather | bytes 147456 | tf_op jit(solution)/shard_map/all_gather | solution.py:153
  168.2 0.0 all-to-all-done.3.parts_ref
  168.2 0.7 broadcast_in_dim.11
  168.9 7.3 %all-to-all-start.4 = ((bf16[16,16,256]{2,1,0:T(8,128)(2,1)}), bf16[16,16,256]{2,1,0:T(8,128)(2,1)S(1)}, u32[]{:S(2)}, u32[]{:S(2)}) async-start(bf16[16,16,256]{2,1,0:T(8,128)(2,1)} %broadcast_in_dim.11), calls=%async_computation.4 | async-start | bytes 262144 | tf_op jit(solution)/shard_map/all_to_all | solution.py:93
  176.2 0.9 shard_map.88
  177.1 5.0 %all-to-all-done.4 = bf16[16,16,256]{2,1,0:T(8,128)(2,1)S(1)} async-done(((bf16[16,16,256]{2,1,0:T(8,128)(2,1)}), bf16[16,16,256]{2,1,0:T(8,128)(2,1)S(1)}, u32[]{:S(2)}, u32[]{:S(2)}) %all-to-all-start.4) | async-done | bytes 131104 | tf_op jit(solution)/shard_map/all_to_all | solution.py:93
  182.1 0.7 bitcast_convert_fusion
  (12 shorter events, 0.1 us)
Async XLA Ops:
  0.6 18.6 %copy-start.3 = (bf16[128,256]{1,0:T(8,128)(2,1)S(1)}, bf16[128,256]{1,0:T(8,128)(2,1)}, u32[]{:S(2)}) copy-start(bf16[128,256]{1,0:T(8,128)(2,1)} %param.7) | copy-start | bytes 196612
  0.6 92.4 %copy-start.4 = (s32[1,1,80]{2,1,0:T(1,128)S(1)}, s32[1,1,80]{2,1,0:T(1,128)}, u32[]{:S(2)}) copy-start(s32[1,1,80]{2,1,0:T(1,128)} %param.12) | copy-start | bytes 964
  0.7 93.7 %copy-start.2 = (s32[1,1,80]{2,1,0:T(1,128)S(1)}, s32[1,1,80]{2,1,0:T(1,128)}, u32[]{:S(2)}) copy-start(s32[1,1,80]{2,1,0:T(1,128)} %param.11) | copy-start | bytes 964
  2.6 64.0 %all-to-all-start = ((bf16[16,128,256]{2,1,0:T(8,128)(2,1)}), bf16[16,128,256]{2,1,0:T(8,128)(2,1)S(1)}, u32[]{:S(2)}, u32[]{:S(2)}) async-start(bf16[16,128,256]{2,1,0:T(8,128)(2,1)} %broadcast_in_dim.9), calls=%async_computation | async-start | bytes 2097152 | tf_op jit(solution)/shard_map/all_to_all | solution.py:93
  66.6 12.7 %collective-permute-start.1 = (bf16[8,128,256]{2,1,0:T(8,128)(2,1)S(1)}, bf16[8,128,256]{2,1,0:T(8,128)(2,1)S(1)}, u32[]{:S(2)}, u32[]{:S(2)}) collective-permute-start(bf16[8,128,256]{2,1,0:T(8,128)(2,1)S(1)} %bitcast.14), channel_id=1, source_target_pairs={{0,992},{32,0},{64,32},{96,64},{128,96},{160,128},{192,160},{224,1... | collective-permute-start | bytes 1572872 | tf_op jit(solution)/shard_map/ppermute | solution.py:98
  70.1 17.4 %collective-permute-start = (bf16[8,128,256]{2,1,0:T(8,128)(2,1)S(1)}, bf16[8,128,256]{2,1,0:T(8,128)(2,1)S(1)}, u32[]{:S(2)}, u32[]{:S(2)}) collective-permute-start(bf16[8,128,256]{2,1,0:T(8,128)(2,1)S(1)} %bitcast.15), channel_id=1, source_target_pairs={{0,32},{32,64},{64,96},{96,128},{128,160},{160,192},{192,224},{224... | collective-permute-start | bytes 1572872 | tf_op jit(solution)/shard_map/ppermute | solution.py:98
  79.4 11.1 %collective-permute-start.2 = (bf16[8,128,256]{2,1,0:T(8,128)(2,1)S(1)}, bf16[8,128,256]{2,1,0:T(8,128)(2,1)S(1)}, u32[]{:S(2)}, u32[]{:S(2)}) collective-permute-start(bf16[8,128,256]{2,1,0:T(8,128)(2,1)S(1)} %collective-permute-done.1.refs_2_), channel_id=1, source_target_pairs={{0,992},{32,0},{64,32},{96,64},{128,96},{160,128},{192,160},{224,1... | collective-permute-start | bytes 1572872 | tf_op jit(solution)/shard_map/ppermute | solution.py:99
  83.1 9.9 %collective-permute-start.3 = (bf16[8,128,256]{2,1,0:T(8,128)(2,1)S(1)}, bf16[8,128,256]{2,1,0:T(8,128)(2,1)}, u32[]{:S(2)}, u32[]{:S(2)}) collective-permute-start(bf16[8,128,256]{2,1,0:T(8,128)(2,1)S(1)} %bitcast.16), channel_id=1, source_target_pairs={{0,16},{16,0},{1,17},{17,1},{2,18},{18,2},{3,19},{19,3},{4,20},{20... | collective-permute-start | bytes 1572872 | tf_op jit(solution)/shard_map/ppermute | solution.py:100
  85.0 8.0 %collective-permute-start.5 = (bf16[8,128,256]{2,1,0:T(8,128)(2,1)S(1)}, bf16[8,128,256]{2,1,0:T(8,128)(2,1)}, u32[]{:S(2)}, u32[]{:S(2)}) collective-permute-start(bf16[8,128,256]{2,1,0:T(8,128)(2,1)S(1)} %collective-permute-done.1.refs_2_), channel_id=1, source_target_pairs={{0,16},{16,0},{1,17},{17,1},{2,18},{18,2},{3,19},{19,3},{4,20},{20... | collective-permute-start | bytes 1572872 | tf_op jit(solution)/shard_map/ppermute | solution.py:100
  87.5 5.6 %collective-permute-start.4 = (bf16[8,128,256]{2,1,0:T(8,128)(2,1)S(1)}, bf16[8,128,256]{2,1,0:T(8,128)(2,1)}, u32[]{:S(2)}, u32[]{:S(2)}) collective-permute-start(bf16[8,128,256]{2,1,0:T(8,128)(2,1)S(1)} %collective-permute-done.refs_1_), channel_id=1, source_target_pairs={{0,16},{16,0},{1,17},{17,1},{2,18},{18,2},{3,19},{19,3},{4,20},{20... | collective-permute-start | bytes 1572872 | tf_op jit(solution)/shard_map/ppermute | solution.py:100
  90.4 3.9 %collective-permute-start.6 = (bf16[8,128,256]{2,1,0:T(8,128)(2,1)S(1)}, bf16[8,128,256]{2,1,0:T(8,128)(2,1)}, u32[]{:S(2)}, u32[]{:S(2)}) collective-permute-start(bf16[8,128,256]{2,1,0:T(8,128)(2,1)S(1)} %collective-permute-done.2.refs_3_), channel_id=1, source_target_pairs={{0,16},{16,0},{1,17},{17,1},{2,18},{18,2},{3,19},{19,3},{4,20},{20... | collective-permute-start | bytes 1572872 | tf_op jit(solution)/shard_map/ppermute | solution.py:100
  94.4 1.7 copy-start
  101.7 74.5 %copy-start.1 = (bf16[256,256]{1,0:T(8,128)(2,1)S(1)}, bf16[256,256]{1,0:T(8,128)(2,1)}, u32[]{:S(2)}) copy-start(bf16[256,256]{1,0:T(8,128)(2,1)} %weight_ref.1) | copy-start | bytes 393220
  126.8 41.4 %all-to-all-start.3 = ((bf16[16,128,256]{2,1,0:T(8,128)(2,1)}), bf16[16,128,256]{2,1,0:T(8,128)(2,1)S(1)}, u32[]{:S(2)}, u32[]{:S(2)}) async-start(bf16[16,128,256]{2,1,0:T(8,128)(2,1)} %get-tuple-element.15), calls=%async_computation.3 | async-start | bytes 2097152 | tf_op jit(solution)/shard_map/all_to_all | solution.py:152
  168.9 13.2 %all-to-all-start.4 = ((bf16[16,16,256]{2,1,0:T(8,128)(2,1)}), bf16[16,16,256]{2,1,0:T(8,128)(2,1)S(1)}, u32[]{:S(2)}, u32[]{:S(2)}) async-start(bf16[16,16,256]{2,1,0:T(8,128)(2,1)} %broadcast_in_dim.11), calls=%async_computation.4 | async-start | bytes 262144 | tf_op jit(solution)/shard_map/all_to_all | solution.py:93

commit v9 on v8

--- a/solution.py
+++ b/solution.py
@@ -69,8 +69,13 @@
     return summed
 
 
-def share_kernel(scale, shares_ref, share_ref):
+def sum_kernel(scale, shares_ref, share_ref):
     share_ref[...] = sum_of(shares_ref) * scale
+
+
+def sum_and_copy_kernel(scale, shares_ref, copies_ref):
+    summed = (sum_of(shares_ref) * scale).astype(copies_ref.dtype)
+    copies_ref[...] = jnp.broadcast_to(summed[None], copies_ref.shape)
 
 
 def finish_kernel(parts_ref, weight_ref, input_ref):
@@ -93,12 +98,14 @@
     return lax.all_to_all(same, axes, 0, 0, tiled=True)
 
 
-def gather_row(grad_out, beside):
-    own, beside = lax.optimization_barrier((lax.all_gather(grad_out, "za"), beside))
+def gather_row(grad_out, later):
+    own, later = lax.optimization_barrier((lax.all_gather(grad_out, "za"), later))
+    swap = [(0, 1), (1, 0)]
     left, right = lax.ppermute(own, Z, shifted(1)), lax.ppermute(own, Z, shifted(-1))
-    pieces = [own, left, right, lax.ppermute(right, Z, shifted(-1))]
-    others = [lax.ppermute(piece, "core", [(0, 1), (1, 0)]) for piece in pieces]
-    return *pieces, *others, beside
+    onward, swapped = lax.optimization_barrier((right, lax.ppermute(own, "core", swap)))
+    opposite = lax.ppermute(onward, Z, shifted(-1))
+    others = [lax.ppermute(piece, "core", swap) for piece in (left, right, opposite)]
+    return own, left, right, opposite, swapped, *others, later
 
 
 def place_of(block):
@@ -113,8 +120,8 @@
     width = grad_out.shape[1]
     cols = lax.axis_size(COL)
     share = width // cols
+    *pieces, features = gather_row(grad_out, features)
     own_features = from_all(features, COL).reshape(-1, width)
-    *pieces, own_features = gather_row(grad_out, own_features)
     smem, vmem = pl.BlockSpec(memory_space=pltpu.SMEM), pl.BlockSpec(memory_space=pltpu.VMEM)
     anywhere = pl.BlockSpec(memory_space=pl.ANY)
     parts, shares = pl.pallas_call(
@@ -140,19 +147,24 @@
         own_features,
     )
     shares = lax.all_to_all(shares, COL, 0, 0, tiled=True)
-    grad_share = pl.pallas_call(
-        functools.partial(share_kernel, nodes**-0.5),
-        out_shape=jax.ShapeDtypeStruct((share, width), jnp.float32),
-        in_specs=[vmem],
-        out_specs=vmem,
-        compiler_params=pltpu.CompilerParams(vmem_limit_bytes=4 * 2**20),
-    )(shares)
-    grad_share = jnp.sum(from_all(grad_share, ("zb", "core")), axis=0)
+
+    def summed(kernel, shape, dtype, array, scale=1.0):
+        return pl.pallas_call(
+            functools.partial(kernel, scale),
+            out_shape=jax.ShapeDtypeStruct(shape, dtype),
+            in_specs=[vmem],
+            out_specs=vmem,
+            compiler_params=pltpu.CompilerParams(vmem_limit_bytes=4 * 2**20),
+        )(array)
+
+    near, far = ("zb", "core"), "za"
+    shares = summed(sum_and_copy_kernel, (lax.axis_size(near), share, width), jnp.float32, shares, nodes**-0.5)
+    grad_share = summed(sum_kernel, (share, width), jnp.float32, lax.all_to_all(shares, near, 0, 0, tiled=True))
     grad_share, parts = lax.optimization_barrier((grad_share, parts))
     parts = lax.all_to_all(parts, COL, 0, 0, tiled=True)
-    grad_share, parts = lax.optimization_barrier((lax.all_gather(grad_share, "za"), parts))
-    grad_share = jnp.sum(grad_share, axis=0).astype(jnp.bfloat16)
-    weight_grad = from_all(grad_share, COL).reshape(width, width).astype(jnp.float32)
+    shares, parts = lax.optimization_barrier((lax.all_gather(grad_share, far), parts))
+    shares = summed(sum_and_copy_kernel, (cols, share, width), jnp.bfloat16, shares)
+    weight_grad = lax.all_to_all(shares, COL, 0, 0, tiled=True).reshape(width, width).astype(jnp.float32)
     input_grad = pl.pallas_call(
         finish_kernel,
         out_shape=jax.ShapeDtypeStruct((tile, width), jnp.bfloat16),

time: 184 us -> 192 us (1.043)
  waiting for transfers between devices: 14.2 us -> 23.2 us
  starting transfers between devices: 47.4 us -> 38.6 us
  blocking collectives: 108 us -> 116 us
    all_to_all x2 -> x1, starting transfers between devices: 24 us -> 7.43 us  [from_all(): return lax.all_to_all(same, axes, 0, 0, tiled=True)]
    all_gather x1, blocking collectives: 47.4 us -> 57.3 us  [gather_row(): lax.all_gather(grad_out, 'za')]
    all_to_all x0 -> x1, starting transfers between devices: none -> 7.32 us  [body(): lax.all_to_all(shares, COL, 0, 0, tiled=True).reshape(width, width)]
    all_to_all x0 -> x1, waiting for transfers between devices: none -> 4.95 us  [body(): lax.all_to_all(shares, COL, 0, 0, tiled=True).reshape(width, width)]
    ppermute x1, waiting for transfers between devices: 6.88 us -> 10.4 us  [gather_row(): lax.ppermute(own, Z, shifted(-1))]
    all_to_all x2 -> x1, waiting for transfers between devices: 4.96 us -> 7.86 us  [from_all(): return lax.all_to_all(same, axes, 0, 0, tiled=True)]
    all_to_all x1, blocking collectives: 15.8 us -> 13 us  [body(): shares = lax.all_to_all(shares, COL, 0, 0, tiled=True)]
    ppermute x5, waiting for transfers between devices: 2.35 us -> 0.01 us  [the longest x3 0.01 us: gather_row(): lax.ppermute(piece, 'core', swap)]
  transfers between devices with their start and end apart: 10 -> 10, of which waited for: 4 -> 3; matrix products, arithmetic and copies ran while one was open for 0% -> 1% of each run, Pallas kernels for 0% -> 0%
where the time goes in v9:
time: 192 us; the launch traced here: 191 us
  blocking collectives  116 us (60%)
  starting transfers between devices  38.6 us (20%)
  waiting for transfers between devices  23.2 us (12%)
  Pallas kernels  7.09 us (4%)
  local copies, waits for them, and re-layouts  3.68 us (2%)
    all_gather x1, blocking collectives, gather_row(): lax.all_gather(grad_out, 'za')  57.3 us
    all_gather x1, blocking collectives, body(): lax.all_gather(grad_share, far)  35.4 us
    all_to_all x1, blocking collectives, body(): shares = lax.all_to_all(shares, COL, 0, 0, tiled=True)  13 us
    ppermute x1, waiting for transfers between devices, gather_row(): lax.ppermute(own, Z, shifted(-1))  10.4 us
    all_to_all x1, blocking collectives, body(): lax.all_to_all(shares, near, 0, 0, tiled=True)  10.3 us
    all_to_all x1, waiting for transfers between devices, from_all(): return lax.all_to_all(same, axes, 0, 0, tiled=True)  7.86 us
    all_to_all x1, starting transfers between devices, from_all(): return lax.all_to_all(same, axes, 0, 0, tiled=True)  7.43 us
    all_to_all x1, starting transfers between devices, body(): lax.all_to_all(shares, COL, 0, 0, tiled=True).reshape(width, width)  7.32 us
  transfers between devices with their start and end apart: 10, of which 3 were waited for; matrix products, arithmetic and copies ran while one was open for 1% of the time, Pallas kernels for 0%

profile of v9, /device:TPU:6, one launch (start us, length us, event | category | flops | bytes accessed | tf_op | source)
XLA Modules:
  0.0 190.7 jit_solution(1945212463923083377)
XLA Ops:
  0.6 57.3 %all-gather = bf16[1024,256]{1,0:T(8,128)(2,1)S(1)} all-gather(bf16[128,256]{1,0:T(8,128)(2,1)} %param.7), channel_id=2, replica_groups=mesh['za'=8,'zb'=4,'core'=2,'x'=4,'y'=4] {'za'}, dimensions={0}, use_global_device_ids=true | all-gather | bytes 589824 | tf_op jit(solution)/shard_map/all_gather | solution.py:102
  57.9 1.9 %collective-permute-start.2 = (bf16[8,128,256]{2,1,0:T(8,128)(2,1)S(1)}, bf16[8,128,256]{2,1,0:T(8,128)(2,1)S(1)}, u32[]{:S(2)}, u32[]{:S(2)}) collective-permute-start(bf16[8,128,256]{2,1,0:T(8,128)(2,1)S(1)} %bitcast.14), channel_id=1, source_target_pairs={{0,16},{16,0},{1,17},{17,1},{2,18},{18,2},{3,19},{19,3},{4,20},{20... | collective-permute-start | bytes 1572872 | tf_op jit(solution)/shard_map/ppermute | solution.py:105
  59.9 3.0 %collective-permute-start.1 = (bf16[8,128,256]{2,1,0:T(8,128)(2,1)S(1)}, bf16[8,128,256]{2,1,0:T(8,128)(2,1)S(1)}, u32[]{:S(2)}, u32[]{:S(2)}) collective-permute-start(bf16[8,128,256]{2,1,0:T(8,128)(2,1)S(1)} %bitcast.15), channel_id=1, source_target_pairs={{0,992},{32,0},{64,32},{96,64},{128,96},{160,128},{192,160},{224,1... | collective-permute-start | bytes 1572872 | tf_op jit(solution)/shard_map/ppermute | solution.py:104
  62.9 2.8 %collective-permute-start = (bf16[8,128,256]{2,1,0:T(8,128)(2,1)S(1)}, bf16[8,128,256]{2,1,0:T(8,128)(2,1)S(1)}, u32[]{:S(2)}, u32[]{:S(2)}) collective-permute-start(bf16[8,128,256]{2,1,0:T(8,128)(2,1)S(1)} %bitcast.16), channel_id=1, source_target_pairs={{0,32},{32,64},{64,96},{96,128},{128,160},{160,192},{192,224},{224... | collective-permute-start | bytes 1572872 | tf_op jit(solution)/shard_map/ppermute | solution.py:104
  65.7 0.0 collective-permute-done.2.refs_4_
  65.7 10.4 %collective-permute-done.1.refs_2_ = bf16[8,128,256]{2,1,0:T(8,128)(2,1)S(1)} collective-permute-done((bf16[8,128,256]{2,1,0:T(8,128)(2,1)S(1)}, bf16[8,128,256]{2,1,0:T(8,128)(2,1)S(1)}, u32[]{:S(2)}, u32[]{:S(2)}) %collective-permute-start.1) | collective-permute-done | bytes 524320 | tf_op jit(solution)/shard_map/ppermute | solution.py:104
  76.1 4.2 %collective-permute-start.3 = (bf16[8,128,256]{2,1,0:T(8,128)(2,1)S(1)}, bf16[8,128,256]{2,1,0:T(8,128)(2,1)}, u32[]{:S(2)}, u32[]{:S(2)}) collective-permute-start(bf16[8,128,256]{2,1,0:T(8,128)(2,1)S(1)} %collective-permute-done.1.refs_2_), channel_id=1, source_target_pairs={{0,992},{32,0},{64,32},{96,64},{128,96},{160,128},{192,160},{224,1... | collective-permute-start | bytes 1572872 | tf_op jit(solution)/shard_map/ppermute | solution.py:106
  80.3 1.9 %broadcast_in_dim.4 = bf16[16,128,256]{2,1,0:T(8,128)(2,1)} broadcast(bf16[128,256]{1,0:T(8,128)(2,1)} %param.8), dimensions={1,2} | broadcast | bytes 1114112 | tf_op jit(solution)/shard_map/broadcast_in_dim | solution.py:97
  82.2 7.4 %all-to-all-start = ((bf16[16,128,256]{2,1,0:T(8,128)(2,1)}), bf16[16,128,256]{2,1,0:T(8,128)(2,1)S(1)}, u32[]{:S(2)}, u32[]{:S(2)}) async-start(bf16[16,128,256]{2,1,0:T(8,128)(2,1)} %broadcast_in_dim.4), calls=%async_computation | async-start | bytes 2097152 | tf_op jit(solution)/shard_map/all_to_all | solution.py:98
  89.7 1.9 %collective-permute-start.5 = (bf16[8,128,256]{2,1,0:T(8,128)(2,1)S(1)}, bf16[8,128,256]{2,1,0:T(8,128)(2,1)}, u32[]{:S(2)}, u32[]{:S(2)}) collective-permute-start(bf16[8,128,256]{2,1,0:T(8,128)(2,1)S(1)} %collective-permute-done.1.refs_2_), channel_id=1, source_target_pairs={{0,16},{16,0},{1,17},{17,1},{2,18},{18,2},{3,19},{19,3},{4,20},{20... | collective-permute-start | bytes 1572872 | tf_op jit(solution)/shard_map/ppermute | solution.py:107
  91.6 0.0 collective-permute-done.refs_1_
  91.6 2.4 %collective-permute-start.4 = (bf16[8,128,256]{2,1,0:T(8,128)(2,1)S(1)}, bf16[8,128,256]{2,1,0:T(8,128)(2,1)}, u32[]{:S(2)}, u32[]{:S(2)}) collective-permute-start(bf16[8,128,256]{2,1,0:T(8,128)(2,1)S(1)} %collective-permute-done.refs_1_), channel_id=1, source_target_pairs={{0,16},{16,0},{1,17},{17,1},{2,18},{18,2},{3,19},{19,3},{4,20},{20... | collective-permute-start | bytes 1572872 | tf_op jit(solution)/shard_map/ppermute | solution.py:107
  94.0 0.0 collective-permute-done.3.refs_3_
  94.0 1.9 %collective-permute-start.6 = (bf16[8,128,256]{2,1,0:T(8,128)(2,1)}, bf16[8,128,256]{2,1,0:T(8,128)(2,1)}, u32[]{:S(2)}, u32[]{:S(2)}) collective-permute-start(bf16[8,128,256]{2,1,0:T(8,128)(2,1)} %collective-permute-done.3.refs_3_), channel_id=1, source_target_pairs={{0,16},{16,0},{1,17},{17,1},{2,18},{18,2},{3,19},{19,3},{4,20},{20... | collective-permute-start | bytes 1572872 | tf_op jit(solution)/shard_map/ppermute | solution.py:107
  96.6 7.9 %all-to-all-done = bf16[16,128,256]{2,1,0:T(8,128)(2,1)S(1)} async-done(((bf16[16,128,256]{2,1,0:T(8,128)(2,1)}), bf16[16,128,256]{2,1,0:T(8,128)(2,1)S(1)}, u32[]{:S(2)}, u32[]{:S(2)}) %all-to-all-start) | async-done | bytes 1048608 | tf_op jit(solution)/shard_map/all_to_all | solution.py:98
  104.5 0.0 collective-permute-done.5.refs_6_
  104.5 0.0 collective-permute-done.4.refs_5_
  104.5 0.0 collective-permute-done.6.refs_7_
  104.5 0.0 copy-start
  104.5 1.7 copy-done
  106.3 5.5 %shard_map.86 = (bf16[16,128,256]{2,1,0:T(8,128)(2,1)}, bf16[16,16,256]{2,1,0:T(8,128)(2,1)S(1)}) custom-call(s32[1]{0:T(128)} %bitcast.11.count_ref, s32[80]{0:T(128)S(1)} %bitcast.19, s32[80]{0:T(128)S(1)} %add_bitcast_fusion.places_ref, bf16[80,128,128]{2,1,0:T(8,128)(2,1)S(1)} %bitcast.13, bf16[8,128,256]{2,1,0:T(8,128)(2,1)S(1)} %bitcast.17, ...), custom_call_target="tpu_custom_call" | custom-call | tf_op jit(solution)/shard_map/pallas_call | solution.py:127
  111.7 0.0 copy-start.1
  111.8 13.0 %all_to_all.25.shares_ref = bf16[16,16,256]{2,1,0:T(8,128)(2,1)S(1)} all-to-all(bf16[16,16,256]{2,1,0:T(8,128)(2,1)S(1)} %get-tuple-element.16), channel_id=1, replica_groups=mesh['za'=8,'zb'=4,'core'=2,'x'=4,'y'=4] {'x','y'}, dimensions={0} | all-to-all | bytes 262144 | tf_op jit(solution)/shard_map/all_to_all | solution.py:149
  124.8 10.3 %all_to_all.26.shares_ref = f32[8,16,256]{2,1,0:T(8,128)S(1)} all-to-all(f32[8,16,256]{2,1,0:T(8,128)S(1)} %shard_map.87), channel_id=1, replica_groups=mesh['za'=8,'zb'=4,'core'=2,'x'=4,'y'=4] {'zb','core'}, dimensions={0} | all-to-all | bytes 262144 | tf_op jit(solution)/shard_map/all_to_all | solution.py:162
  135.1 5.6 %all-to-all-start.3 = ((bf16[16,128,256]{2,1,0:T(8,128)(2,1)}), bf16[16,128,256]{2,1,0:T(8,128)(2,1)S(1)}, u32[]{:S(2)}, u32[]{:S(2)}) async-start(bf16[16,128,256]{2,1,0:T(8,128)(2,1)} %get-tuple-element.19), calls=%async_computation.3 | async-start | bytes 2097152 | tf_op jit(solution)/shard_map/all_to_all | solution.py:164
  140.7 35.4 %all-gather.1 = f32[128,256]{1,0:T(8,128)S(1)} all-gather(f32[16,256]{1,0:T(8,128)S(1)} %shard_map.88), channel_id=3, replica_groups=mesh['za'=8,'zb'=4,'core'=2,'x'=4,'y'=4] {'za'}, dimensions={0}, use_global_device_ids=true | all-gather | bytes 147456 | tf_op jit(solution)/shard_map/all_gather | solution.py:165
  176.1 0.0 all-to-all-done.3.parts_ref
  176.1 0.7 shard_map.90
  176.8 7.3 %all-to-all-start.4 = ((bf16[16,16,256]{2,1,0:T(8,128)(2,1)}), bf16[16,16,256]{2,1,0:T(8,128)(2,1)S(1)}, u32[]{:S(2)}, u32[]{:S(2)}) async-start(bf16[16,16,256]{2,1,0:T(8,128)(2,1)} %shard_map.90), calls=%async_computation.4 | async-start | bytes 262144 | tf_op jit(solution)/shard_map/all_to_all | solution.py:167
  184.1 0.9 shard_map.89
  185.0 4.9 %all-to-all-done.4 = bf16[16,16,256]{2,1,0:T(8,128)(2,1)S(1)} async-done(((bf16[16,16,256]{2,1,0:T(8,128)(2,1)}), bf16[16,16,256]{2,1,0:T(8,128)(2,1)S(1)}, u32[]{:S(2)}, u32[]{:S(2)}) %all-to-all-start.4) | async-done | bytes 131104 | tf_op jit(solution)/shard_map/all_to_all | solution.py:167
  190.0 0.7 bitcast_convert_fusion
  (8 shorter events, 0.1 us)
Async XLA Ops:
  0.6 96.0 %copy-start.3 = (s32[1,1,80]{2,1,0:T(1,128)S(1)}, s32[1,1,80]{2,1,0:T(1,128)}, u32[]{:S(2)}) copy-start(s32[1,1,80]{2,1,0:T(1,128)} %param.12) | copy-start | bytes 964
  0.6 103.9 %copy-start.2 = (s32[1,1,80]{2,1,0:T(1,128)S(1)}, s32[1,1,80]{2,1,0:T(1,128)}, u32[]{:S(2)}) copy-start(s32[1,1,80]{2,1,0:T(1,128)} %param.11) | copy-start | bytes 964
  57.9 7.8 %collective-permute-start.2 = (bf16[8,128,256]{2,1,0:T(8,128)(2,1)S(1)}, bf16[8,128,256]{2,1,0:T(8,128)(2,1)S(1)}, u32[]{:S(2)}, u32[]{:S(2)}) collective-permute-start(bf16[8,128,256]{2,1,0:T(8,128)(2,1)S(1)} %bitcast.14), channel_id=1, source_target_pairs={{0,16},{16,0},{1,17},{17,1},{2,18},{18,2},{3,19},{19,3},{4,20},{20... | collective-permute-start | bytes 1572872 | tf_op jit(solution)/shard_map/ppermute | solution.py:105
  59.9 16.2 %collective-permute-start.1 = (bf16[8,128,256]{2,1,0:T(8,128)(2,1)S(1)}, bf16[8,128,256]{2,1,0:T(8,128)(2,1)S(1)}, u32[]{:S(2)}, u32[]{:S(2)}) collective-permute-start(bf16[8,128,256]{2,1,0:T(8,128)(2,1)S(1)} %bitcast.15), channel_id=1, source_target_pairs={{0,992},{32,0},{64,32},{96,64},{128,96},{160,128},{192,160},{224,1... | collective-permute-start | bytes 1572872 | tf_op jit(solution)/shard_map/ppermute | solution.py:104
  62.9 28.7 %collective-permute-start = (bf16[8,128,256]{2,1,0:T(8,128)(2,1)S(1)}, bf16[8,128,256]{2,1,0:T(8,128)(2,1)S(1)}, u32[]{:S(2)}, u32[]{:S(2)}) collective-permute-start(bf16[8,128,256]{2,1,0:T(8,128)(2,1)S(1)} %bitcast.16), channel_id=1, source_target_pairs={{0,32},{32,64},{64,96},{96,128},{128,160},{160,192},{192,224},{224... | collective-permute-start | bytes 1572872 | tf_op jit(solution)/shard_map/ppermute | solution.py:104
  76.1 17.9 %collective-permute-start.3 = (bf16[8,128,256]{2,1,0:T(8,128)(2,1)S(1)}, bf16[8,128,256]{2,1,0:T(8,128)(2,1)}, u32[]{:S(2)}, u32[]{:S(2)}) collective-permute-start(bf16[8,128,256]{2,1,0:T(8,128)(2,1)S(1)} %collective-permute-done.1.refs_2_), channel_id=1, source_target_pairs={{0,992},{32,0},{64,32},{96,64},{128,96},{160,128},{192,160},{224,1... | collective-permute-start | bytes 1572872 | tf_op jit(solution)/shard_map/ppermute | solution.py:106
  82.2 22.3 %all-to-all-start = ((bf16[16,128,256]{2,1,0:T(8,128)(2,1)}), bf16[16,128,256]{2,1,0:T(8,128)(2,1)S(1)}, u32[]{:S(2)}, u32[]{:S(2)}) async-start(bf16[16,128,256]{2,1,0:T(8,128)(2,1)} %broadcast_in_dim.4), calls=%async_computation | async-start | bytes 2097152 | tf_op jit(solution)/shard_map/all_to_all | solution.py:98
  89.7 14.8 %collective-permute-start.5 = (bf16[8,128,256]{2,1,0:T(8,128)(2,1)S(1)}, bf16[8,128,256]{2,1,0:T(8,128)(2,1)}, u32[]{:S(2)}, u32[]{:S(2)}) collective-permute-start(bf16[8,128,256]{2,1,0:T(8,128)(2,1)S(1)} %collective-permute-done.1.refs_2_), channel_id=1, source_target_pairs={{0,16},{16,0},{1,17},{17,1},{2,18},{18,2},{3,19},{19,3},{4,20},{20... | collective-permute-start | bytes 1572872 | tf_op jit(solution)/shard_map/ppermute | solution.py:107
  91.6 12.9 %collective-permute-start.4 = (bf16[8,128,256]{2,1,0:T(8,128)(2,1)S(1)}, bf16[8,128,256]{2,1,0:T(8,128)(2,1)}, u32[]{:S(2)}, u32[]{:S(2)}) collective-permute-start(bf16[8,128,256]{2,1,0:T(8,128)(2,1)S(1)} %collective-permute-done.refs_1_), channel_id=1, source_target_pairs={{0,16},{16,0},{1,17},{17,1},{2,18},{18,2},{3,19},{19,3},{4,20},{20... | collective-permute-start | bytes 1572872 | tf_op jit(solution)/shard_map/ppermute | solution.py:107
  94.0 10.5 %collective-permute-start.6 = (bf16[8,128,256]{2,1,0:T(8,128)(2,1)}, bf16[8,128,256]{2,1,0:T(8,128)(2,1)}, u32[]{:S(2)}, u32[]{:S(2)}) collective-permute-start(bf16[8,128,256]{2,1,0:T(8,128)(2,1)} %collective-permute-done.3.refs_3_), channel_id=1, source_target_pairs={{0,16},{16,0},{1,17},{17,1},{2,18},{18,2},{3,19},{19,3},{4,20},{20... | collective-permute-start | bytes 1572872 | tf_op jit(solution)/shard_map/ppermute | solution.py:107
  104.5 1.7 copy-start
  111.7 72.4 %copy-start.1 = (bf16[256,256]{1,0:T(8,128)(2,1)S(1)}, bf16[256,256]{1,0:T(8,128)(2,1)}, u32[]{:S(2)}) copy-start(bf16[256,256]{1,0:T(8,128)(2,1)} %weight_ref.1) | copy-start | bytes 393220
  135.1 41.0 %all-to-all-start.3 = ((bf16[16,128,256]{2,1,0:T(8,128)(2,1)}), bf16[16,128,256]{2,1,0:T(8,128)(2,1)S(1)}, u32[]{:S(2)}, u32[]{:S(2)}) async-start(bf16[16,128,256]{2,1,0:T(8,128)(2,1)} %get-tuple-element.19), calls=%async_computation.3 | async-start | bytes 2097152 | tf_op jit(solution)/shard_map/all_to_all | solution.py:164
  176.8 13.2 %all-to-all-start.4 = ((bf16[16,16,256]{2,1,0:T(8,128)(2,1)}), bf16[16,16,256]{2,1,0:T(8,128)(2,1)S(1)}, u32[]{:S(2)}, u32[]{:S(2)}) async-start(bf16[16,16,256]{2,1,0:T(8,128)(2,1)} %shard_map.90), calls=%async_computation.4 | async-start | bytes 262144 | tf_op jit(solution)/shard_map/all_to_all | solution.py:167

commit v10 on v9

--- a/solution.py
+++ b/solution.py
@@ -98,14 +98,15 @@
     return lax.all_to_all(same, axes, 0, 0, tiled=True)
 
 
-def gather_row(grad_out, later):
-    own, later = lax.optimization_barrier((lax.all_gather(grad_out, "za"), later))
+def gather(grad_out, features):
+    own, features = lax.optimization_barrier((lax.all_gather(grad_out, "za"), features))
     swap = [(0, 1), (1, 0)]
     left, right = lax.ppermute(own, Z, shifted(1)), lax.ppermute(own, Z, shifted(-1))
-    onward, swapped = lax.optimization_barrier((right, lax.ppermute(own, "core", swap)))
-    opposite = lax.ppermute(onward, Z, shifted(-1))
-    others = [lax.ppermute(piece, "core", swap) for piece in (left, right, opposite)]
-    return own, left, right, opposite, swapped, *others, later
+    features = from_all(features, COL)
+    opposite = lax.ppermute(right, Z, shifted(-1))
+    left_ready, features = lax.optimization_barrier((left, features))
+    others = [lax.ppermute(piece, "core", swap) for piece in (own, left_ready, right, opposite)]
+    return own, left, right, opposite, *others, features.reshape(-1, features.shape[-1])
 
 
 def place_of(block):
@@ -120,8 +121,7 @@
     width = grad_out.shape[1]
     cols = lax.axis_size(COL)
     share = width // cols
-    *pieces, features = gather_row(grad_out, features)
-    own_features = from_all(features, COL).reshape(-1, width)
+    *pieces, own_features = gather(grad_out, features)
     smem, vmem = pl.BlockSpec(memory_space=pltpu.SMEM), pl.BlockSpec(memory_space=pltpu.VMEM)
     anywhere = pl.BlockSpec(memory_space=pl.ANY)
     parts, shares = pl.pallas_call(

time: 192 us -> 179 us (0.932)
  waiting for transfers between devices: 23.2 us -> 6.77 us
  blocking collectives: 116 us -> 120 us
    ppermute x7, waiting for transfers between devices: 10.4 us -> 1.81 us  [the longest x4 0.94 us: gather(): lax.ppermute(piece, 'core', swap)]
    all_to_all x1, waiting for transfers between devices: 7.86 us -> 0.01 us  [from_all(): return lax.all_to_all(same, axes, 0, 0, tiled=True)]
  transfers between devices with their start and end apart: 10 -> 10, of which waited for: 3 -> 3; matrix products, arithmetic and copies ran while one was open for 1% -> 1% of each run, Pallas kernels for 0% -> 1%
where the time goes in v10:
time: 179 us; the launch traced here: 178 us
  blocking collectives  120 us (67%)
  starting transfers between devices  38.8 us (22%)
  waiting for transfers between devices  6.77 us (4%)
  Pallas kernels  6.7 us (4%)
  local copies, waits for them, and re-layouts  3.68 us (2%)
    all_gather x1, blocking collectives, gather(): lax.all_gather(grad_out, 'za')  57.3 us
    all_gather x1, blocking collectives, body(): lax.all_gather(grad_share, far)  36.2 us
    all_to_all x1, blocking collectives, body(): shares = lax.all_to_all(shares, COL, 0, 0, tiled=True)  14.6 us
    all_to_all x1, blocking collectives, body(): lax.all_to_all(shares, near, 0, 0, tiled=True)  11.7 us
    ppermute x4, starting transfers between devices, gather(): lax.ppermute(piece, 'core', swap)  8.65 us
    all_to_all x1, starting transfers between devices, from_all(): return lax.all_to_all(same, axes, 0, 0, tiled=True)  7.43 us
    all_to_all x1, starting transfers between devices, body(): lax.all_to_all(shares, COL, 0, 0, tiled=True).reshape(width, width)  7.09 us
    all_to_all x1, starting transfers between devices, body(): parts = lax.all_to_all(parts, COL, 0, 0, tiled=True)  5.6 us
  transfers between devices with their start and end apart: 10, of which 3 were waited for; matrix products, arithmetic and copies ran while one was open for 1% of the time, Pallas kernels for 1%

profile of v10, /device:TPU:6, one launch (start us, length us, event | category | flops | bytes accessed | tf_op | source)
XLA Modules:
  0.0 177.9 jit_solution(6610064850577305892)
XLA Ops:
  0.6 57.3 %all-gather = bf16[1024,256]{1,0:T(8,128)(2,1)S(1)} all-gather(bf16[128,256]{1,0:T(8,128)(2,1)} %param.7), channel_id=2, replica_groups=mesh['za'=8,'zb'=4,'core'=2,'x'=4,'y'=4] {'za'}, dimensions={0}, use_global_device_ids=true | all-gather | bytes 589824 | tf_op jit(solution)/shard_map/all_gather | solution.py:102
  57.9 3.0 %collective-permute-start.1 = (bf16[8,128,256]{2,1,0:T(8,128)(2,1)S(1)}, bf16[8,128,256]{2,1,0:T(8,128)(2,1)S(1)}, u32[]{:S(2)}, u32[]{:S(2)}) collective-permute-start(bf16[8,128,256]{2,1,0:T(8,128)(2,1)S(1)} %bitcast.14), channel_id=1, source_target_pairs={{0,992},{32,0},{64,32},{96,64},{128,96},{160,128},{192,160},{224,1... | collective-permute-start | bytes 1572872 | tf_op jit(solution)/shard_map/ppermute | solution.py:104
  61.0 1.9 %broadcast_in_dim.4 = bf16[16,128,256]{2,1,0:T(8,128)(2,1)} broadcast(bf16[128,256]{1,0:T(8,128)(2,1)} %param.8), dimensions={1,2} | broadcast | bytes 1114112 | tf_op jit(solution)/shard_map/broadcast_in_dim | solution.py:97
  62.9 7.4 %all-to-all-start = ((bf16[16,128,256]{2,1,0:T(8,128)(2,1)}), bf16[16,128,256]{2,1,0:T(8,128)(2,1)S(1)}, u32[]{:S(2)}, u32[]{:S(2)}) async-start(bf16[16,128,256]{2,1,0:T(8,128)(2,1)} %broadcast_in_dim.4), calls=%async_computation | async-start | bytes 2097152 | tf_op jit(solution)/shard_map/all_to_all | solution.py:98
  70.3 2.8 %collective-permute-start = (bf16[8,128,256]{2,1,0:T(8,128)(2,1)S(1)}, bf16[8,128,256]{2,1,0:T(8,128)(2,1)S(1)}, u32[]{:S(2)}, u32[]{:S(2)}) collective-permute-start(bf16[8,128,256]{2,1,0:T(8,128)(2,1)S(1)} %bitcast.15), channel_id=1, source_target_pairs={{0,32},{32,64},{64,96},{96,128},{128,160},{160,192},{192,224},{224... | collective-permute-start | bytes 1572872 | tf_op jit(solution)/shard_map/ppermute | solution.py:104
  73.1 0.0 collective-permute-done.1.refs_2_
  73.2 4.2 %collective-permute-start.2 = (bf16[8,128,256]{2,1,0:T(8,128)(2,1)S(1)}, bf16[8,128,256]{2,1,0:T(8,128)(2,1)S(1)}, u32[]{:S(2)}, u32[]{:S(2)}) collective-permute-start(bf16[8,128,256]{2,1,0:T(8,128)(2,1)S(1)} %collective-permute-done.1.refs_2_), channel_id=1, source_target_pairs={{0,992},{32,0},{64,32},{96,64},{128,96},{160,128},{192,160},{224,1... | collective-permute-start | bytes 1572872 | tf_op jit(solution)/shard_map/ppermute | solution.py:106
  77.4 1.9 %collective-permute-start.3 = (bf16[8,128,256]{2,1,0:T(8,128)(2,1)S(1)}, bf16[8,128,256]{2,1,0:T(8,128)(2,1)}, u32[]{:S(2)}, u32[]{:S(2)}) collective-permute-start(bf16[8,128,256]{2,1,0:T(8,128)(2,1)S(1)} %bitcast.16), channel_id=1, source_target_pairs={{0,16},{16,0},{1,17},{17,1},{2,18},{18,2},{3,19},{19,3},{4,20},{20... | collective-permute-start | bytes 1572872 | tf_op jit(solution)/shard_map/ppermute | solution.py:108
  79.3 2.4 %collective-permute-start.5 = (bf16[8,128,256]{2,1,0:T(8,128)(2,1)S(1)}, bf16[8,128,256]{2,1,0:T(8,128)(2,1)}, u32[]{:S(2)}, u32[]{:S(2)}) collective-permute-start(bf16[8,128,256]{2,1,0:T(8,128)(2,1)S(1)} %collective-permute-done.1.refs_2_), channel_id=1, source_target_pairs={{0,16},{16,0},{1,17},{17,1},{2,18},{18,2},{3,19},{19,3},{4,20},{20... | collective-permute-start | bytes 1572872 | tf_op jit(solution)/shard_map/ppermute | solution.py:108
  81.7 0.9 collective-permute-done.refs_1_
  82.6 0.0 all-to-all-done
  82.6 1.9 %collective-permute-start.4 = (bf16[8,128,256]{2,1,0:T(8,128)(2,1)S(1)}, bf16[8,128,256]{2,1,0:T(8,128)(2,1)}, u32[]{:S(2)}, u32[]{:S(2)}) collective-permute-start(bf16[8,128,256]{2,1,0:T(8,128)(2,1)S(1)} %collective-permute-done.refs_1_), channel_id=1, source_target_pairs={{0,16},{16,0},{1,17},{17,1},{2,18},{18,2},{3,19},{19,3},{4,20},{20... | collective-permute-start | bytes 1572872 | tf_op jit(solution)/shard_map/ppermute | solution.py:108
  84.5 0.0 collective-permute-done.2.refs_3_
  84.5 2.4 %collective-permute-start.6 = (bf16[8,128,256]{2,1,0:T(8,128)(2,1)S(1)}, bf16[8,128,256]{2,1,0:T(8,128)(2,1)}, u32[]{:S(2)}, u32[]{:S(2)}) collective-permute-start(bf16[8,128,256]{2,1,0:T(8,128)(2,1)S(1)} %collective-permute-done.2.refs_3_), channel_id=1, source_target_pairs={{0,16},{16,0},{1,17},{17,1},{2,18},{18,2},{3,19},{19,3},{4,20},{20... | collective-permute-start | bytes 1572872 | tf_op jit(solution)/shard_map/ppermute | solution.py:108
  87.6 0.0 copy-done.3
  87.6 0.0 collective-permute-done.3.refs_4_
  87.6 0.0 collective-permute-done.5.refs_6_
  87.6 0.0 collective-permute-done.4.refs_5_
  87.7 0.9 collective-permute-done.6.refs_7_
  88.6 1.7 copy-done
  90.3 5.1 %shard_map.86 = (bf16[16,128,256]{2,1,0:T(8,128)(2,1)}, bf16[16,16,256]{2,1,0:T(8,128)(2,1)S(1)}) custom-call(s32[1]{0:T(128)} %bitcast.11.count_ref, s32[80]{0:T(128)S(1)} %bitcast.19, s32[80]{0:T(128)S(1)} %add_bitcast_fusion.places_ref, bf16[80,128,128]{2,1,0:T(8,128)(2,1)S(1)} %bitcast.13, bf16[8,128,256]{2,1,0:T(8,128)(2,1)S(1)} %bitcast.17, ...), custom_call_target="tpu_custom_call" | custom-call | tf_op jit(solution)/shard_map/pallas_call | solution.py:127
  95.4 0.0 copy-start.1
  95.4 14.6 %all_to_all.25.shares_ref = bf16[16,16,256]{2,1,0:T(8,128)(2,1)S(1)} all-to-all(bf16[16,16,256]{2,1,0:T(8,128)(2,1)S(1)} %get-tuple-element.16), channel_id=1, replica_groups=mesh['za'=8,'zb'=4,'core'=2,'x'=4,'y'=4] {'x','y'}, dimensions={0} | all-to-all | bytes 262144 | tf_op jit(solution)/shard_map/all_to_all | solution.py:149
  110.1 11.7 %all_to_all.26.shares_ref = f32[8,16,256]{2,1,0:T(8,128)S(1)} all-to-all(f32[8,16,256]{2,1,0:T(8,128)S(1)} %shard_map.87), channel_id=1, replica_groups=mesh['za'=8,'zb'=4,'core'=2,'x'=4,'y'=4] {'zb','core'}, dimensions={0} | all-to-all | bytes 262144 | tf_op jit(solution)/shard_map/all_to_all | solution.py:162
  121.7 5.6 %all-to-all-start.3 = ((bf16[16,128,256]{2,1,0:T(8,128)(2,1)}), bf16[16,128,256]{2,1,0:T(8,128)(2,1)S(1)}, u32[]{:S(2)}, u32[]{:S(2)}) async-start(bf16[16,128,256]{2,1,0:T(8,128)(2,1)} %get-tuple-element.19), calls=%async_computation.3 | async-start | bytes 2097152 | tf_op jit(solution)/shard_map/all_to_all | solution.py:164
  127.3 36.2 %all-gather.1 = f32[128,256]{1,0:T(8,128)S(1)} all-gather(f32[16,256]{1,0:T(8,128)S(1)} %shard_map.88), channel_id=3, replica_groups=mesh['za'=8,'zb'=4,'core'=2,'x'=4,'y'=4] {'za'}, dimensions={0}, use_global_device_ids=true | all-gather | bytes 147456 | tf_op jit(solution)/shard_map/all_gather | solution.py:165
  163.5 0.0 all-to-all-done.3.parts_ref
  163.5 0.7 shard_map.90
  164.2 7.1 %all-to-all-start.4 = ((bf16[16,16,256]{2,1,0:T(8,128)(2,1)}), bf16[16,16,256]{2,1,0:T(8,128)(2,1)S(1)}, u32[]{:S(2)}, u32[]{:S(2)}) async-start(bf16[16,16,256]{2,1,0:T(8,128)(2,1)} %shard_map.90), calls=%async_computation.4 | async-start | bytes 262144 | tf_op jit(solution)/shard_map/all_to_all | solution.py:167
  171.3 0.9 shard_map.89
  172.2 5.0 %all-to-all-done.4 = bf16[16,16,256]{2,1,0:T(8,128)(2,1)S(1)} async-done(((bf16[16,16,256]{2,1,0:T(8,128)(2,1)}), bf16[16,16,256]{2,1,0:T(8,128)(2,1)S(1)}, u32[]{:S(2)}, u32[]{:S(2)}) %all-to-all-start.4) | async-done | bytes 131104 | tf_op jit(solution)/shard_map/all_to_all | solution.py:167
  177.2 0.7 bitcast_convert_fusion
  (8 shorter events, 0.1 us)
Async XLA Ops:
  0.6 87.0 %copy-start.3 = (s32[1,1,80]{2,1,0:T(1,128)S(1)}, s32[1,1,80]{2,1,0:T(1,128)}, u32[]{:S(2)}) copy-start(s32[1,1,80]{2,1,0:T(1,128)} %param.12) | copy-start | bytes 964
  0.6 88.0 %copy-start.2 = (s32[1,1,80]{2,1,0:T(1,128)S(1)}, s32[1,1,80]{2,1,0:T(1,128)}, u32[]{:S(2)}) copy-start(s32[1,1,80]{2,1,0:T(1,128)} %param.11) | copy-start | bytes 964
  57.9 15.2 %collective-permute-start.1 = (bf16[8,128,256]{2,1,0:T(8,128)(2,1)S(1)}, bf16[8,128,256]{2,1,0:T(8,128)(2,1)S(1)}, u32[]{:S(2)}, u32[]{:S(2)}) collective-permute-start(bf16[8,128,256]{2,1,0:T(8,128)(2,1)S(1)} %bitcast.14), channel_id=1, source_target_pairs={{0,992},{32,0},{64,32},{96,64},{128,96},{160,128},{192,160},{224,1... | collective-permute-start | bytes 1572872 | tf_op jit(solution)/shard_map/ppermute | solution.py:104
  62.9 19.7 %all-to-all-start = ((bf16[16,128,256]{2,1,0:T(8,128)(2,1)}), bf16[16,128,256]{2,1,0:T(8,128)(2,1)S(1)}, u32[]{:S(2)}, u32[]{:S(2)}) async-start(bf16[16,128,256]{2,1,0:T(8,128)(2,1)} %broadcast_in_dim.4), calls=%async_computation | async-start | bytes 2097152 | tf_op jit(solution)/shard_map/all_to_all | solution.py:98
  70.3 12.3 %collective-permute-start = (bf16[8,128,256]{2,1,0:T(8,128)(2,1)S(1)}, bf16[8,128,256]{2,1,0:T(8,128)(2,1)S(1)}, u32[]{:S(2)}, u32[]{:S(2)}) collective-permute-start(bf16[8,128,256]{2,1,0:T(8,128)(2,1)S(1)} %bitcast.15), channel_id=1, source_target_pairs={{0,32},{32,64},{64,96},{96,128},{128,160},{160,192},{192,224},{224... | collective-permute-start | bytes 1572872 | tf_op jit(solution)/shard_map/ppermute | solution.py:104
  73.2 11.4 %collective-permute-start.2 = (bf16[8,128,256]{2,1,0:T(8,128)(2,1)S(1)}, bf16[8,128,256]{2,1,0:T(8,128)(2,1)S(1)}, u32[]{:S(2)}, u32[]{:S(2)}) collective-permute-start(bf16[8,128,256]{2,1,0:T(8,128)(2,1)S(1)} %collective-permute-done.1.refs_2_), channel_id=1, source_target_pairs={{0,992},{32,0},{64,32},{96,64},{128,96},{160,128},{192,160},{224,1... | collective-permute-start | bytes 1572872 | tf_op jit(solution)/shard_map/ppermute | solution.py:106
  77.4 10.2 %collective-permute-start.3 = (bf16[8,128,256]{2,1,0:T(8,128)(2,1)S(1)}, bf16[8,128,256]{2,1,0:T(8,128)(2,1)}, u32[]{:S(2)}, u32[]{:S(2)}) collective-permute-start(bf16[8,128,256]{2,1,0:T(8,128)(2,1)S(1)} %bitcast.16), channel_id=1, source_target_pairs={{0,16},{16,0},{1,17},{17,1},{2,18},{18,2},{3,19},{19,3},{4,20},{20... | collective-permute-start | bytes 1572872 | tf_op jit(solution)/shard_map/ppermute | solution.py:108
  79.3 8.3 %collective-permute-start.5 = (bf16[8,128,256]{2,1,0:T(8,128)(2,1)S(1)}, bf16[8,128,256]{2,1,0:T(8,128)(2,1)}, u32[]{:S(2)}, u32[]{:S(2)}) collective-permute-start(bf16[8,128,256]{2,1,0:T(8,128)(2,1)S(1)} %collective-permute-done.1.refs_2_), channel_id=1, source_target_pairs={{0,16},{16,0},{1,17},{17,1},{2,18},{18,2},{3,19},{19,3},{4,20},{20... | collective-permute-start | bytes 1572872 | tf_op jit(solution)/shard_map/ppermute | solution.py:108
  82.6 5.0 %collective-permute-start.4 = (bf16[8,128,256]{2,1,0:T(8,128)(2,1)S(1)}, bf16[8,128,256]{2,1,0:T(8,128)(2,1)}, u32[]{:S(2)}, u32[]{:S(2)}) collective-permute-start(bf16[8,128,256]{2,1,0:T(8,128)(2,1)S(1)} %collective-permute-done.refs_1_), channel_id=1, source_target_pairs={{0,16},{16,0},{1,17},{17,1},{2,18},{18,2},{3,19},{19,3},{4,20},{20... | collective-permute-start | bytes 1572872 | tf_op jit(solution)/shard_map/ppermute | solution.py:108
  84.5 4.1 %collective-permute-start.6 = (bf16[8,128,256]{2,1,0:T(8,128)(2,1)S(1)}, bf16[8,128,256]{2,1,0:T(8,128)(2,1)}, u32[]{:S(2)}, u32[]{:S(2)}) collective-permute-start(bf16[8,128,256]{2,1,0:T(8,128)(2,1)S(1)} %collective-permute-done.2.refs_3_), channel_id=1, source_target_pairs={{0,16},{16,0},{1,17},{17,1},{2,18},{18,2},{3,19},{19,3},{4,20},{20... | collective-permute-start | bytes 1572872 | tf_op jit(solution)/shard_map/ppermute | solution.py:108
  88.6 1.7 copy-start
  95.4 75.9 %copy-start.1 = (bf16[256,256]{1,0:T(8,128)(2,1)S(1)}, bf16[256,256]{1,0:T(8,128)(2,1)}, u32[]{:S(2)}) copy-start(bf16[256,256]{1,0:T(8,128)(2,1)} %weight_ref.1) | copy-start | bytes 393220
  121.7 41.8 %all-to-all-start.3 = ((bf16[16,128,256]{2,1,0:T(8,128)(2,1)}), bf16[16,128,256]{2,1,0:T(8,128)(2,1)S(1)}, u32[]{:S(2)}, u32[]{:S(2)}) async-start(bf16[16,128,256]{2,1,0:T(8,128)(2,1)} %get-tuple-element.19), calls=%async_computation.3 | async-start | bytes 2097152 | tf_op jit(solution)/shard_map/all_to_all | solution.py:164
  164.2 13.0 %all-to-all-start.4 = ((bf16[16,16,256]{2,1,0:T(8,128)(2,1)}), bf16[16,16,256]{2,1,0:T(8,128)(2,1)S(1)}, u32[]{:S(2)}, u32[]{:S(2)}) async-start(bf16[16,16,256]{2,1,0:T(8,128)(2,1)} %shard_map.90), calls=%async_computation.4 | async-start | bytes 262144 | tf_op jit(solution)/shard_map/all_to_all | solution.py:167

commit v11 on v10

--- a/solution.py
+++ b/solution.py
@@ -11,6 +11,7 @@
 Z = ("za", "zb")
 ROW = Z + ("core",)
 COL = ("x", "y")
+SHARE = ("core", "y")
 
 
 def tiles_kernel(count_ref, rows_ref, places_ref, values_ref, *refs):
@@ -120,7 +121,8 @@
     tile = tile_values.shape[-1]
     width = grad_out.shape[1]
     cols = lax.axis_size(COL)
-    share = width // cols
+    sharers = lax.axis_size(SHARE)
+    share = width // sharers
     *pieces, own_features = gather(grad_out, features)
     smem, vmem = pl.BlockSpec(memory_space=pltpu.SMEM), pl.BlockSpec(memory_space=pltpu.VMEM)
     anywhere = pl.BlockSpec(memory_space=pl.ANY)
@@ -128,7 +130,7 @@
         tiles_kernel,
         out_shape=(
             jax.ShapeDtypeStruct((cols, tile, width), jnp.bfloat16),
-            jax.ShapeDtypeStruct((cols, share, width), jnp.bfloat16),
+            jax.ShapeDtypeStruct((sharers, share, width), jnp.bfloat16),
         ),
         in_specs=[smem] * 3 + [vmem] + [anywhere] * len(pieces) + [vmem],
         out_specs=(vmem, vmem),
@@ -146,7 +148,7 @@
         *pieces,
         own_features,
     )
-    shares = lax.all_to_all(shares, COL, 0, 0, tiled=True)
+    shares = lax.all_to_all(shares, SHARE, 0, 0, tiled=True)
 
     def summed(kernel, shape, dtype, array, scale=1.0):
         return pl.pallas_call(
@@ -157,14 +159,17 @@
             compiler_params=pltpu.CompilerParams(vmem_limit_bytes=4 * 2**20),
         )(array)
 
-    near, far = ("zb", "core"), "za"
-    shares = summed(sum_and_copy_kernel, (lax.axis_size(near), share, width), jnp.float32, shares, nodes**-0.5)
-    grad_share = summed(sum_kernel, (share, width), jnp.float32, lax.all_to_all(shares, near, 0, 0, tiled=True))
+    scale = nodes**-0.5
+    for axis in ("x", "zb"):
+        copies = (lax.axis_size(axis), share, width)
+        shares = lax.all_to_all(summed(sum_and_copy_kernel, copies, jnp.float32, shares, scale), axis, 0, 0, tiled=True)
+        scale = 1.0
+    grad_share = summed(sum_kernel, (share, width), jnp.float32, shares)
     grad_share, parts = lax.optimization_barrier((grad_share, parts))
     parts = lax.all_to_all(parts, COL, 0, 0, tiled=True)
-    shares, parts = lax.optimization_barrier((lax.all_gather(grad_share, far), parts))
-    shares = summed(sum_and_copy_kernel, (cols, share, width), jnp.bfloat16, shares)
-    weight_grad = lax.all_to_all(shares, COL, 0, 0, tiled=True).reshape(width, width).astype(jnp.float32)
+    shares, parts = lax.optimization_barrier((lax.all_gather(grad_share, "za"), parts))
+    shares = summed(sum_and_copy_kernel, (sharers, share, width), jnp.bfloat16, shares)
+    weight_grad = lax.all_to_all(shares, SHARE, 0, 0, tiled=True).reshape(width, width).astype(jnp.float32)
     input_grad = pl.pallas_call(
         finish_kernel,
         out_shape=jax.ShapeDtypeStruct((tile, width), jnp.bfloat16),

time: 179 us -> 183 us (1.022)
  blocking collectives: 120 us -> 126 us
  starting transfers between devices: 38.8 us -> 36 us
    all_to_all x2 -> x3, blocking collectives: 26.2 us -> 31 us  [the longest x2 18.3 us: body(): lax.all_to_all(summed(sum_and_copy_kernel, copies, jnp.float32, shares, s...]
    all_to_all x1, starting transfers between devices: 7.09 us -> 4.2 us  [body(): lax.all_to_all(shares, SHARE, 0, 0, tiled=True).reshape(width, width)]
where the time goes in v11:
time: 183 us; the launch traced here: 181 us
  blocking collectives  126 us (69%)
  starting transfers between devices  36 us (20%)
  Pallas kernels  6.48 us (4%)
  waiting for transfers between devices  6.46 us (4%)
  local copies, waits for them, and re-layouts  3.68 us (2%)
    all_gather x1, blocking collectives, gather(): lax.all_gather(grad_out, 'za')  57.3 us
    all_gather x1, blocking collectives, body(): lax.all_gather(grad_share, 'za')  38 us
    all_to_all x2, blocking collectives, body(): lax.all_to_all(summed(sum_and_copy_kernel, copies, jnp.float32, shares, s...  18.3 us
    all_to_all x1, blocking collectives, body(): shares = lax.all_to_all(shares, SHARE, 0, 0, tiled=True)  12.7 us
    ppermute x4, starting transfers between devices, gather(): lax.ppermute(piece, 'core', swap)  8.65 us
    all_to_all x1, starting transfers between devices, from_all(): return lax.all_to_all(same, axes, 0, 0, tiled=True)  7.43 us
    all_to_all x1, starting transfers between devices, body(): parts = lax.all_to_all(parts, COL, 0, 0, tiled=True)  5.72 us
    pallas_call x1, Pallas kernels, body(): pl.pallas_call(tiles_kernel, out_shape=(jax.ShapeDtypeStruct((cols, tile,...  4.85 us
  transfers between devices with their start and end apart: 10, of which 3 were waited for; matrix products, arithmetic and copies ran while one was open for 1% of the time, Pallas kernels for 1%

profile of v11, /device:TPU:6, one launch (start us, length us, event | category | flops | bytes accessed | tf_op | source)
XLA Modules:
  0.0 181.2 jit_solution(14531161412010711920)
XLA Ops:
  0.6 57.3 %all-gather = bf16[1024,256]{1,0:T(8,128)(2,1)S(1)} all-gather(bf16[128,256]{1,0:T(8,128)(2,1)} %param.7), channel_id=2, replica_groups=mesh['za'=8,'zb'=4,'core'=2,'x'=4,'y'=4] {'za'}, dimensions={0}, use_global_device_ids=true | all-gather | bytes 589824 | tf_op jit(solution)/shard_map/all_gather | solution.py:103
  57.9 3.0 %collective-permute-start.1 = (bf16[8,128,256]{2,1,0:T(8,128)(2,1)S(1)}, bf16[8,128,256]{2,1,0:T(8,128)(2,1)S(1)}, u32[]{:S(2)}, u32[]{:S(2)}) collective-permute-start(bf16[8,128,256]{2,1,0:T(8,128)(2,1)S(1)} %bitcast.14), channel_id=1, source_target_pairs={{0,992},{32,0},{64,32},{96,64},{128,96},{160,128},{192,160},{224,1... | collective-permute-start | bytes 1572872 | tf_op jit(solution)/shard_map/ppermute | solution.py:105
  61.0 1.9 %broadcast_in_dim.4 = bf16[16,128,256]{2,1,0:T(8,128)(2,1)} broadcast(bf16[128,256]{1,0:T(8,128)(2,1)} %param.8), dimensions={1,2} | broadcast | bytes 1114112 | tf_op jit(solution)/shard_map/broadcast_in_dim | solution.py:98
  62.9 7.4 %all-to-all-start = ((bf16[16,128,256]{2,1,0:T(8,128)(2,1)}), bf16[16,128,256]{2,1,0:T(8,128)(2,1)S(1)}, u32[]{:S(2)}, u32[]{:S(2)}) async-start(bf16[16,128,256]{2,1,0:T(8,128)(2,1)} %broadcast_in_dim.4), calls=%async_computation | async-start | bytes 2097152 | tf_op jit(solution)/shard_map/all_to_all | solution.py:99
  70.3 2.8 %collective-permute-start = (bf16[8,128,256]{2,1,0:T(8,128)(2,1)S(1)}, bf16[8,128,256]{2,1,0:T(8,128)(2,1)S(1)}, u32[]{:S(2)}, u32[]{:S(2)}) collective-permute-start(bf16[8,128,256]{2,1,0:T(8,128)(2,1)S(1)} %bitcast.15), channel_id=1, source_target_pairs={{0,32},{32,64},{64,96},{96,128},{128,160},{160,192},{192,224},{224... | collective-permute-start | bytes 1572872 | tf_op jit(solution)/shard_map/ppermute | solution.py:105
  73.1 0.0 collective-permute-done.1.refs_2_
  73.2 4.2 %collective-permute-start.2 = (bf16[8,128,256]{2,1,0:T(8,128)(2,1)S(1)}, bf16[8,128,256]{2,1,0:T(8,128)(2,1)S(1)}, u32[]{:S(2)}, u32[]{:S(2)}) collective-permute-start(bf16[8,128,256]{2,1,0:T(8,128)(2,1)S(1)} %collective-permute-done.1.refs_2_), channel_id=1, source_target_pairs={{0,992},{32,0},{64,32},{96,64},{128,96},{160,128},{192,160},{224,1... | collective-permute-start | bytes 1572872 | tf_op jit(solution)/shard_map/ppermute | solution.py:107
  77.4 1.9 %collective-permute-start.3 = (bf16[8,128,256]{2,1,0:T(8,128)(2,1)S(1)}, bf16[8,128,256]{2,1,0:T(8,128)(2,1)}, u32[]{:S(2)}, u32[]{:S(2)}) collective-permute-start(bf16[8,128,256]{2,1,0:T(8,128)(2,1)S(1)} %bitcast.16), channel_id=1, source_target_pairs={{0,16},{16,0},{1,17},{17,1},{2,18},{18,2},{3,19},{19,3},{4,20},{20... | collective-permute-start | bytes 1572872 | tf_op jit(solution)/shard_map/ppermute | solution.py:109
  79.3 2.4 %collective-permute-start.5 = (bf16[8,128,256]{2,1,0:T(8,128)(2,1)S(1)}, bf16[8,128,256]{2,1,0:T(8,128)(2,1)}, u32[]{:S(2)}, u32[]{:S(2)}) collective-permute-start(bf16[8,128,256]{2,1,0:T(8,128)(2,1)S(1)} %collective-permute-done.1.refs_2_), channel_id=1, source_target_pairs={{0,16},{16,0},{1,17},{17,1},{2,18},{18,2},{3,19},{19,3},{4,20},{20... | collective-permute-start | bytes 1572872 | tf_op jit(solution)/shard_map/ppermute | solution.py:109
  81.7 0.9 collective-permute-done.refs_1_
  82.6 0.0 all-to-all-done
  82.6 1.9 %collective-permute-start.4 = (bf16[8,128,256]{2,1,0:T(8,128)(2,1)S(1)}, bf16[8,128,256]{2,1,0:T(8,128)(2,1)}, u32[]{:S(2)}, u32[]{:S(2)}) collective-permute-start(bf16[8,128,256]{2,1,0:T(8,128)(2,1)S(1)} %collective-permute-done.refs_1_), channel_id=1, source_target_pairs={{0,16},{16,0},{1,17},{17,1},{2,18},{18,2},{3,19},{19,3},{4,20},{20... | collective-permute-start | bytes 1572872 | tf_op jit(solution)/shard_map/ppermute | solution.py:109
  84.5 0.0 collective-permute-done.2.refs_3_
  84.5 2.4 %collective-permute-start.6 = (bf16[8,128,256]{2,1,0:T(8,128)(2,1)S(1)}, bf16[8,128,256]{2,1,0:T(8,128)(2,1)}, u32[]{:S(2)}, u32[]{:S(2)}) collective-permute-start(bf16[8,128,256]{2,1,0:T(8,128)(2,1)S(1)} %collective-permute-done.2.refs_3_), channel_id=1, source_target_pairs={{0,16},{16,0},{1,17},{17,1},{2,18},{18,2},{3,19},{19,3},{4,20},{20... | collective-permute-start | bytes 1572872 | tf_op jit(solution)/shard_map/ppermute | solution.py:109
  87.6 0.0 collective-permute-done.3.refs_4_
  87.6 0.0 collective-permute-done.5.refs_6_
  87.6 0.0 collective-permute-done.4.refs_5_
  87.7 0.9 collective-permute-done.6.refs_7_
  88.6 1.7 copy-done
  90.3 4.9 %shard_map.86 = (bf16[16,128,256]{2,1,0:T(8,128)(2,1)}, bf16[8,32,256]{2,1,0:T(8,128)(2,1)S(1)}) custom-call(s32[1]{0:T(128)} %bitcast.11.count_ref, s32[80]{0:T(128)S(1)} %bitcast.19, s32[80]{0:T(128)S(1)} %add_bitcast_fusion.places_ref, bf16[80,128,128]{2,1,0:T(8,128)(2,1)S(1)} %bitcast.13, bf16[8,128,256]{2,1,0:T(8,128)(2,1)S(1)} %bitcast.17, ...), custom_call_target="tpu_custom_call" | custom-call | tf_op jit(solution)/shard_map/pallas_call | solution.py:129
  95.2 0.0 copy-start.1
  95.2 12.7 %all_to_all.30.shares_ref = bf16[8,32,256]{2,1,0:T(8,128)(2,1)S(1)} all-to-all(bf16[8,32,256]{2,1,0:T(8,128)(2,1)S(1)} %get-tuple-element.16), channel_id=1, replica_groups=mesh['za'=8,'zb'=4,'core'=2,'x'=4,'y'=4] {'core','y'}, dimensions={0} | all-to-all | bytes 262144 | tf_op jit(solution)/shard_map/all_to_all | solution.py:151
  108.0 8.8 %all_to_all.31.shares_ref = f32[4,32,256]{2,1,0:T(8,128)S(1)} all-to-all(f32[4,32,256]{2,1,0:T(8,128)S(1)} %shard_map.87), channel_id=1, replica_groups=mesh['za'=8,'zb'=4,'core'=2,'x'=4,'y'=4] {'x'}, dimensions={0} | all-to-all | bytes 262144 | tf_op jit(solution)/shard_map/all_to_all | solution.py:165
  116.8 9.5 %all_to_all.32.shares_ref = f32[4,32,256]{2,1,0:T(8,128)S(1)} all-to-all(f32[4,32,256]{2,1,0:T(8,128)S(1)} %shard_map.88), channel_id=1, replica_groups=mesh['za'=8,'zb'=4,'core'=2,'x'=4,'y'=4] {'zb'}, dimensions={0} | all-to-all | bytes 262144 | tf_op jit(solution)/shard_map/all_to_all | solution.py:165
  126.3 5.7 %all-to-all-start.4 = ((bf16[16,128,256]{2,1,0:T(8,128)(2,1)}), bf16[16,128,256]{2,1,0:T(8,128)(2,1)S(1)}, u32[]{:S(2)}, u32[]{:S(2)}) async-start(bf16[16,128,256]{2,1,0:T(8,128)(2,1)} %get-tuple-element.19), calls=%async_computation.4 | async-start | bytes 2097152 | tf_op jit(solution)/shard_map/all_to_all | solution.py:169
  132.0 38.0 %all-gather.1 = f32[256,256]{1,0:T(8,128)S(1)} all-gather(f32[32,256]{1,0:T(8,128)S(1)} %shard_map.89), channel_id=3, replica_groups=mesh['za'=8,'zb'=4,'core'=2,'x'=4,'y'=4] {'za'}, dimensions={0}, use_global_device_ids=true | all-gather | bytes 294912 | tf_op jit(solution)/shard_map/all_gather | solution.py:170
  170.0 0.0 all-to-all-done.4.parts_ref
  170.0 0.7 shard_map.91
  170.7 4.2 %all-to-all-start.5 = ((bf16[8,32,256]{2,1,0:T(8,128)(2,1)}), bf16[8,32,256]{2,1,0:T(8,128)(2,1)S(1)}, u32[]{:S(2)}, u32[]{:S(2)}) async-start(bf16[8,32,256]{2,1,0:T(8,128)(2,1)} %shard_map.91), calls=%async_computation.5 | async-start | bytes 262144 | tf_op jit(solution)/shard_map/all_to_all | solution.py:172
  174.9 0.9 shard_map.90
  175.8 4.6 %all-to-all-done.5 = bf16[8,32,256]{2,1,0:T(8,128)(2,1)S(1)} async-done(((bf16[8,32,256]{2,1,0:T(8,128)(2,1)}), bf16[8,32,256]{2,1,0:T(8,128)(2,1)S(1)}, u32[]{:S(2)}, u32[]{:S(2)}) %all-to-all-start.5) | async-done | bytes 131104 | tf_op jit(solution)/shard_map/all_to_all | solution.py:172
  180.5 0.7 bitcast_convert_fusion
  (10 shorter events, 0.1 us)
Async XLA Ops:
  0.6 87.0 %copy-start.3 = (s32[1,1,80]{2,1,0:T(1,128)S(1)}, s32[1,1,80]{2,1,0:T(1,128)}, u32[]{:S(2)}) copy-start(s32[1,1,80]{2,1,0:T(1,128)} %param.12) | copy-start | bytes 964
  0.6 88.0 %copy-start.2 = (s32[1,1,80]{2,1,0:T(1,128)S(1)}, s32[1,1,80]{2,1,0:T(1,128)}, u32[]{:S(2)}) copy-start(s32[1,1,80]{2,1,0:T(1,128)} %param.11) | copy-start | bytes 964
  57.9 15.2 %collective-permute-start.1 = (bf16[8,128,256]{2,1,0:T(8,128)(2,1)S(1)}, bf16[8,128,256]{2,1,0:T(8,128)(2,1)S(1)}, u32[]{:S(2)}, u32[]{:S(2)}) collective-permute-start(bf16[8,128,256]{2,1,0:T(8,128)(2,1)S(1)} %bitcast.14), channel_id=1, source_target_pairs={{0,992},{32,0},{64,32},{96,64},{128,96},{160,128},{192,160},{224,1... | collective-permute-start | bytes 1572872 | tf_op jit(solution)/shard_map/ppermute | solution.py:105
  62.9 19.7 %all-to-all-start = ((bf16[16,128,256]{2,1,0:T(8,128)(2,1)}), bf16[16,128,256]{2,1,0:T(8,128)(2,1)S(1)}, u32[]{:S(2)}, u32[]{:S(2)}) async-start(bf16[16,128,256]{2,1,0:T(8,128)(2,1)} %broadcast_in_dim.4), calls=%async_computation | async-start | bytes 2097152 | tf_op jit(solution)/shard_map/all_to_all | solution.py:99
  70.3 12.3 %collective-permute-start = (bf16[8,128,256]{2,1,0:T(8,128)(2,1)S(1)}, bf16[8,128,256]{2,1,0:T(8,128)(2,1)S(1)}, u32[]{:S(2)}, u32[]{:S(2)}) collective-permute-start(bf16[8,128,256]{2,1,0:T(8,128)(2,1)S(1)} %bitcast.15), channel_id=1, source_target_pairs={{0,32},{32,64},{64,96},{96,128},{128,160},{160,192},{192,224},{224... | collective-permute-start | bytes 1572872 | tf_op jit(solution)/shard_map/ppermute | solution.py:105
  73.2 11.4 %collective-permute-start.2 = (bf16[8,128,256]{2,1,0:T(8,128)(2,1)S(1)}, bf16[8,128,256]{2,1,0:T(8,128)(2,1)S(1)}, u32[]{:S(2)}, u32[]{:S(2)}) collective-permute-start(bf16[8,128,256]{2,1,0:T(8,128)(2,1)S(1)} %collective-permute-done.1.refs_2_), channel_id=1, source_target_pairs={{0,992},{32,0},{64,32},{96,64},{128,96},{160,128},{192,160},{224,1... | collective-permute-start | bytes 1572872 | tf_op jit(solution)/shard_map/ppermute | solution.py:107
  77.4 10.2 %collective-permute-start.3 = (bf16[8,128,256]{2,1,0:T(8,128)(2,1)S(1)}, bf16[8,128,256]{2,1,0:T(8,128)(2,1)}, u32[]{:S(2)}, u32[]{:S(2)}) collective-permute-start(bf16[8,128,256]{2,1,0:T(8,128)(2,1)S(1)} %bitcast.16), channel_id=1, source_target_pairs={{0,16},{16,0},{1,17},{17,1},{2,18},{18,2},{3,19},{19,3},{4,20},{20... | collective-permute-start | bytes 1572872 | tf_op jit(solution)/shard_map/ppermute | solution.py:109
  79.3 8.3 %collective-permute-start.5 = (bf16[8,128,256]{2,1,0:T(8,128)(2,1)S(1)}, bf16[8,128,256]{2,1,0:T(8,128)(2,1)}, u32[]{:S(2)}, u32[]{:S(2)}) collective-permute-start(bf16[8,128,256]{2,1,0:T(8,128)(2,1)S(1)} %collective-permute-done.1.refs_2_), channel_id=1, source_target_pairs={{0,16},{16,0},{1,17},{17,1},{2,18},{18,2},{3,19},{19,3},{4,20},{20... | collective-permute-start | bytes 1572872 | tf_op jit(solution)/shard_map/ppermute | solution.py:109
  82.6 5.0 %collective-permute-start.4 = (bf16[8,128,256]{2,1,0:T(8,128)(2,1)S(1)}, bf16[8,128,256]{2,1,0:T(8,128)(2,1)}, u32[]{:S(2)}, u32[]{:S(2)}) collective-permute-start(bf16[8,128,256]{2,1,0:T(8,128)(2,1)S(1)} %collective-permute-done.refs_1_), channel_id=1, source_target_pairs={{0,16},{16,0},{1,17},{17,1},{2,18},{18,2},{3,19},{19,3},{4,20},{20... | collective-permute-start | bytes 1572872 | tf_op jit(solution)/shard_map/ppermute | solution.py:109
  84.5 4.1 %collective-permute-start.6 = (bf16[8,128,256]{2,1,0:T(8,128)(2,1)S(1)}, bf16[8,128,256]{2,1,0:T(8,128)(2,1)}, u32[]{:S(2)}, u32[]{:S(2)}) collective-permute-start(bf16[8,128,256]{2,1,0:T(8,128)(2,1)S(1)} %collective-permute-done.2.refs_3_), channel_id=1, source_target_pairs={{0,16},{16,0},{1,17},{17,1},{2,18},{18,2},{3,19},{19,3},{4,20},{20... | collective-permute-start | bytes 1572872 | tf_op jit(solution)/shard_map/ppermute | solution.py:109
  88.6 1.7 copy-start
  95.2 79.7 %copy-start.1 = (bf16[256,256]{1,0:T(8,128)(2,1)S(1)}, bf16[256,256]{1,0:T(8,128)(2,1)}, u32[]{:S(2)}) copy-start(bf16[256,256]{1,0:T(8,128)(2,1)} %weight_ref.1) | copy-start | bytes 393220
  126.3 43.7 %all-to-all-start.4 = ((bf16[16,128,256]{2,1,0:T(8,128)(2,1)}), bf16[16,128,256]{2,1,0:T(8,128)(2,1)S(1)}, u32[]{:S(2)}, u32[]{:S(2)}) async-start(bf16[16,128,256]{2,1,0:T(8,128)(2,1)} %get-tuple-element.19), calls=%async_computation.4 | async-start | bytes 2097152 | tf_op jit(solution)/shard_map/all_to_all | solution.py:169
  170.7 9.8 %all-to-all-start.5 = ((bf16[8,32,256]{2,1,0:T(8,128)(2,1)}), bf16[8,32,256]{2,1,0:T(8,128)(2,1)S(1)}, u32[]{:S(2)}, u32[]{:S(2)}) async-start(bf16[8,32,256]{2,1,0:T(8,128)(2,1)} %shard_map.91), calls=%async_computation.5 | async-start | bytes 262144 | tf_op jit(solution)/shard_map/all_to_all | solution.py:172

commit v12 on v10

--- a/solution.py
+++ b/solution.py
@@ -33,20 +33,16 @@
             values_ref[slot], gathered[places_ref[slot]], preferred_element_type=jnp.float32
         )
 
-    count = count_ref[0]
-    fours = lax.shift_right_logical(count, 2)
+    count, done = count_ref[0], 0
+    for bits in (4, 2, 0):
+        groups = lax.shift_right_logical(count - done, bits)
 
-    def four(index, carry):
-        for offset in range(4):
-            add(4 * index + offset)
-        return carry
+        def group(index, first, bits=bits):
+            for offset in range(2**bits):
+                add(first + offset)
+            return first + 2**bits
 
-    def one(slot, carry):
-        add(slot)
-        return carry
-
-    lax.fori_loop(0, fours, four, 0)
-    lax.fori_loop(4 * fours, count, one, 0)
+        done = lax.fori_loop(0, groups, group, done)
 
     step = 4
     grad = jnp.zeros((features_ref.shape[1], width), jnp.float32)

time: 179 us -> 178 us (level)
  blocking collectives: 120 us -> 117 us
    all_to_all x1, blocking collectives: 14.6 us -> 12 us  [body(): shares = lax.all_to_all(shares, COL, 0, 0, tiled=True)]
where the time goes in v12:
time: 178 us; the launch traced here: 176 us
  blocking collectives  117 us (66%)
  starting transfers between devices  39.1 us (22%)
  Pallas kernels  7.44 us (4%)
  waiting for transfers between devices  6.77 us (4%)
  local copies, waits for them, and re-layouts  3.68 us (2%)
    all_gather x1, blocking collectives, gather(): lax.all_gather(grad_out, 'za')  57.3 us
    all_gather x1, blocking collectives, body(): lax.all_gather(grad_share, far)  35.6 us
    all_to_all x1, blocking collectives, body(): lax.all_to_all(shares, near, 0, 0, tiled=True)  12.4 us
    all_to_all x1, blocking collectives, body(): shares = lax.all_to_all(shares, COL, 0, 0, tiled=True)  12 us
    ppermute x4, starting transfers between devices, gather(): lax.ppermute(piece, 'core', swap)  8.65 us
    all_to_all x1, starting transfers between devices, from_all(): return lax.all_to_all(same, axes, 0, 0, tiled=True)  7.43 us
    all_to_all x1, starting transfers between devices, body(): lax.all_to_all(shares, COL, 0, 0, tiled=True).reshape(width, width)  7.3 us
    pallas_call x1, Pallas kernels, body(): pl.pallas_call(tiles_kernel, out_shape=(jax.ShapeDtypeStruct((cols, tile,...  5.82 us
  transfers between devices with their start and end apart: 10, of which 3 were waited for; matrix products, arithmetic and copies ran while one was open for 1% of the time, Pallas kernels for 1%

profile of v12, /device:TPU:6, one launch (start us, length us, event | category | flops | bytes accessed | tf_op | source)
XLA Modules:
  0.0 176.4 jit_solution(7579202809058110622)
XLA Ops:
  0.6 57.3 %all-gather = bf16[1024,256]{1,0:T(8,128)(2,1)S(1)} all-gather(bf16[128,256]{1,0:T(8,128)(2,1)} %param.7), channel_id=2, replica_groups=mesh['za'=8,'zb'=4,'core'=2,'x'=4,'y'=4] {'za'}, dimensions={0}, use_global_device_ids=true | all-gather | bytes 589824 | tf_op jit(solution)/shard_map/all_gather | solution.py:98
  57.9 3.0 %collective-permute-start.1 = (bf16[8,128,256]{2,1,0:T(8,128)(2,1)S(1)}, bf16[8,128,256]{2,1,0:T(8,128)(2,1)S(1)}, u32[]{:S(2)}, u32[]{:S(2)}) collective-permute-start(bf16[8,128,256]{2,1,0:T(8,128)(2,1)S(1)} %bitcast.14), channel_id=1, source_target_pairs={{0,992},{32,0},{64,32},{96,64},{128,96},{160,128},{192,160},{224,1... | collective-permute-start | bytes 1572872 | tf_op jit(solution)/shard_map/ppermute | solution.py:100
  61.0 1.9 %broadcast_in_dim.4 = bf16[16,128,256]{2,1,0:T(8,128)(2,1)} broadcast(bf16[128,256]{1,0:T(8,128)(2,1)} %param.8), dimensions={1,2} | broadcast | bytes 1114112 | tf_op jit(solution)/shard_map/broadcast_in_dim | solution.py:93
  62.9 7.4 %all-to-all-start = ((bf16[16,128,256]{2,1,0:T(8,128)(2,1)}), bf16[16,128,256]{2,1,0:T(8,128)(2,1)S(1)}, u32[]{:S(2)}, u32[]{:S(2)}) async-start(bf16[16,128,256]{2,1,0:T(8,128)(2,1)} %broadcast_in_dim.4), calls=%async_computation | async-start | bytes 2097152 | tf_op jit(solution)/shard_map/all_to_all | solution.py:94
  70.3 2.8 %collective-permute-start = (bf16[8,128,256]{2,1,0:T(8,128)(2,1)S(1)}, bf16[8,128,256]{2,1,0:T(8,128)(2,1)S(1)}, u32[]{:S(2)}, u32[]{:S(2)}) collective-permute-start(bf16[8,128,256]{2,1,0:T(8,128)(2,1)S(1)} %bitcast.15), channel_id=1, source_target_pairs={{0,32},{32,64},{64,96},{96,128},{128,160},{160,192},{192,224},{224... | collective-permute-start | bytes 1572872 | tf_op jit(solution)/shard_map/ppermute | solution.py:100
  73.1 0.0 collective-permute-done.1.refs_2_
  73.2 4.2 %collective-permute-start.2 = (bf16[8,128,256]{2,1,0:T(8,128)(2,1)S(1)}, bf16[8,128,256]{2,1,0:T(8,128)(2,1)S(1)}, u32[]{:S(2)}, u32[]{:S(2)}) collective-permute-start(bf16[8,128,256]{2,1,0:T(8,128)(2,1)S(1)} %collective-permute-done.1.refs_2_), channel_id=1, source_target_pairs={{0,992},{32,0},{64,32},{96,64},{128,96},{160,128},{192,160},{224,1... | collective-permute-start | bytes 1572872 | tf_op jit(solution)/shard_map/ppermute | solution.py:102
  77.4 1.9 %collective-permute-start.3 = (bf16[8,128,256]{2,1,0:T(8,128)(2,1)S(1)}, bf16[8,128,256]{2,1,0:T(8,128)(2,1)}, u32[]{:S(2)}, u32[]{:S(2)}) collective-permute-start(bf16[8,128,256]{2,1,0:T(8,128)(2,1)S(1)} %bitcast.16), channel_id=1, source_target_pairs={{0,16},{16,0},{1,17},{17,1},{2,18},{18,2},{3,19},{19,3},{4,20},{20... | collective-permute-start | bytes 1572872 | tf_op jit(solution)/shard_map/ppermute | solution.py:104
  79.3 2.4 %collective-permute-start.5 = (bf16[8,128,256]{2,1,0:T(8,128)(2,1)S(1)}, bf16[8,128,256]{2,1,0:T(8,128)(2,1)}, u32[]{:S(2)}, u32[]{:S(2)}) collective-permute-start(bf16[8,128,256]{2,1,0:T(8,128)(2,1)S(1)} %collective-permute-done.1.refs_2_), channel_id=1, source_target_pairs={{0,16},{16,0},{1,17},{17,1},{2,18},{18,2},{3,19},{19,3},{4,20},{20... | collective-permute-start | bytes 1572872 | tf_op jit(solution)/shard_map/ppermute | solution.py:104
  81.7 0.9 collective-permute-done.refs_1_
  82.6 0.0 all-to-all-done
  82.6 1.9 %collective-permute-start.4 = (bf16[8,128,256]{2,1,0:T(8,128)(2,1)S(1)}, bf16[8,128,256]{2,1,0:T(8,128)(2,1)}, u32[]{:S(2)}, u32[]{:S(2)}) collective-permute-start(bf16[8,128,256]{2,1,0:T(8,128)(2,1)S(1)} %collective-permute-done.refs_1_), channel_id=1, source_target_pairs={{0,16},{16,0},{1,17},{17,1},{2,18},{18,2},{3,19},{19,3},{4,20},{20... | collective-permute-start | bytes 1572872 | tf_op jit(solution)/shard_map/ppermute | solution.py:104
  84.5 0.0 collective-permute-done.2.refs_3_
  84.5 2.4 %collective-permute-start.6 = (bf16[8,128,256]{2,1,0:T(8,128)(2,1)S(1)}, bf16[8,128,256]{2,1,0:T(8,128)(2,1)}, u32[]{:S(2)}, u32[]{:S(2)}) collective-permute-start(bf16[8,128,256]{2,1,0:T(8,128)(2,1)S(1)} %collective-permute-done.2.refs_3_), channel_id=1, source_target_pairs={{0,16},{16,0},{1,17},{17,1},{2,18},{18,2},{3,19},{19,3},{4,20},{20... | collective-permute-start | bytes 1572872 | tf_op jit(solution)/shard_map/ppermute | solution.py:104
  87.6 0.0 copy-done.3
  87.6 0.0 collective-permute-done.3.refs_4_
  87.6 0.0 collective-permute-done.5.refs_6_
  87.6 0.0 collective-permute-done.4.refs_5_
  87.7 0.9 collective-permute-done.6.refs_7_
  88.6 1.7 copy-done
  90.3 5.8 %shard_map.86 = (bf16[16,128,256]{2,1,0:T(8,128)(2,1)}, bf16[16,16,256]{2,1,0:T(8,128)(2,1)S(1)}) custom-call(s32[1]{0:T(128)} %bitcast.11.count_ref, s32[80]{0:T(128)S(1)} %bitcast.19, s32[80]{0:T(128)S(1)} %add_bitcast_fusion.places_ref, bf16[80,128,128]{2,1,0:T(8,128)(2,1)S(1)} %bitcast.13, bf16[8,128,256]{2,1,0:T(8,128)(2,1)S(1)} %bitcast.17, ...), custom_call_target="tpu_custom_call" | custom-call | tf_op jit(solution)/shard_map/pallas_call | solution.py:123
  96.2 0.0 copy-start.1
  96.2 12.0 %all_to_all.25.shares_ref = bf16[16,16,256]{2,1,0:T(8,128)(2,1)S(1)} all-to-all(bf16[16,16,256]{2,1,0:T(8,128)(2,1)S(1)} %get-tuple-element.16), channel_id=1, replica_groups=mesh['za'=8,'zb'=4,'core'=2,'x'=4,'y'=4] {'x','y'}, dimensions={0} | all-to-all | bytes 262144 | tf_op jit(solution)/shard_map/all_to_all | solution.py:145
  108.2 12.4 %all_to_all.26.shares_ref = f32[8,16,256]{2,1,0:T(8,128)S(1)} all-to-all(f32[8,16,256]{2,1,0:T(8,128)S(1)} %shard_map.87), channel_id=1, replica_groups=mesh['za'=8,'zb'=4,'core'=2,'x'=4,'y'=4] {'zb','core'}, dimensions={0} | all-to-all | bytes 262144 | tf_op jit(solution)/shard_map/all_to_all | solution.py:158
  120.6 5.7 %all-to-all-start.3 = ((bf16[16,128,256]{2,1,0:T(8,128)(2,1)}), bf16[16,128,256]{2,1,0:T(8,128)(2,1)S(1)}, u32[]{:S(2)}, u32[]{:S(2)}) async-start(bf16[16,128,256]{2,1,0:T(8,128)(2,1)} %get-tuple-element.19), calls=%async_computation.3 | async-start | bytes 2097152 | tf_op jit(solution)/shard_map/all_to_all | solution.py:160
  126.3 35.6 %all-gather.1 = f32[128,256]{1,0:T(8,128)S(1)} all-gather(f32[16,256]{1,0:T(8,128)S(1)} %shard_map.88), channel_id=3, replica_groups=mesh['za'=8,'zb'=4,'core'=2,'x'=4,'y'=4] {'za'}, dimensions={0}, use_global_device_ids=true | all-gather | bytes 147456 | tf_op jit(solution)/shard_map/all_gather | solution.py:161
  161.8 0.0 all-to-all-done.3.parts_ref
  161.8 0.7 shard_map.90
  162.5 7.3 %all-to-all-start.4 = ((bf16[16,16,256]{2,1,0:T(8,128)(2,1)}), bf16[16,16,256]{2,1,0:T(8,128)(2,1)S(1)}, u32[]{:S(2)}, u32[]{:S(2)}) async-start(bf16[16,16,256]{2,1,0:T(8,128)(2,1)} %shard_map.90), calls=%async_computation.4 | async-start | bytes 262144 | tf_op jit(solution)/shard_map/all_to_all | solution.py:163
  169.8 0.9 shard_map.89
  170.7 5.0 %all-to-all-done.4 = bf16[16,16,256]{2,1,0:T(8,128)(2,1)S(1)} async-done(((bf16[16,16,256]{2,1,0:T(8,128)(2,1)}), bf16[16,16,256]{2,1,0:T(8,128)(2,1)S(1)}, u32[]{:S(2)}, u32[]{:S(2)}) %all-to-all-start.4) | async-done | bytes 131104 | tf_op jit(solution)/shard_map/all_to_all | solution.py:163
  175.7 0.7 bitcast_convert_fusion
  (8 shorter events, 0.1 us)
Async XLA Ops:
  0.6 87.0 %copy-start.3 = (s32[1,1,80]{2,1,0:T(1,128)S(1)}, s32[1,1,80]{2,1,0:T(1,128)}, u32[]{:S(2)}) copy-start(s32[1,1,80]{2,1,0:T(1,128)} %param.12) | copy-start | bytes 964
  0.6 88.0 %copy-start.2 = (s32[1,1,80]{2,1,0:T(1,128)S(1)}, s32[1,1,80]{2,1,0:T(1,128)}, u32[]{:S(2)}) copy-start(s32[1,1,80]{2,1,0:T(1,128)} %param.11) | copy-start | bytes 964
  57.9 15.2 %collective-permute-start.1 = (bf16[8,128,256]{2,1,0:T(8,128)(2,1)S(1)}, bf16[8,128,256]{2,1,0:T(8,128)(2,1)S(1)}, u32[]{:S(2)}, u32[]{:S(2)}) collective-permute-start(bf16[8,128,256]{2,1,0:T(8,128)(2,1)S(1)} %bitcast.14), channel_id=1, source_target_pairs={{0,992},{32,0},{64,32},{96,64},{128,96},{160,128},{192,160},{224,1... | collective-permute-start | bytes 1572872 | tf_op jit(solution)/shard_map/ppermute | solution.py:100
  62.9 19.7 %all-to-all-start = ((bf16[16,128,256]{2,1,0:T(8,128)(2,1)}), bf16[16,128,256]{2,1,0:T(8,128)(2,1)S(1)}, u32[]{:S(2)}, u32[]{:S(2)}) async-start(bf16[16,128,256]{2,1,0:T(8,128)(2,1)} %broadcast_in_dim.4), calls=%async_computation | async-start | bytes 2097152 | tf_op jit(solution)/shard_map/all_to_all | solution.py:94
  70.3 12.3 %collective-permute-start = (bf16[8,128,256]{2,1,0:T(8,128)(2,1)S(1)}, bf16[8,128,256]{2,1,0:T(8,128)(2,1)S(1)}, u32[]{:S(2)}, u32[]{:S(2)}) collective-permute-start(bf16[8,128,256]{2,1,0:T(8,128)(2,1)S(1)} %bitcast.15), channel_id=1, source_target_pairs={{0,32},{32,64},{64,96},{96,128},{128,160},{160,192},{192,224},{224... | collective-permute-start | bytes 1572872 | tf_op jit(solution)/shard_map/ppermute | solution.py:100
  73.2 11.4 %collective-permute-start.2 = (bf16[8,128,256]{2,1,0:T(8,128)(2,1)S(1)}, bf16[8,128,256]{2,1,0:T(8,128)(2,1)S(1)}, u32[]{:S(2)}, u32[]{:S(2)}) collective-permute-start(bf16[8,128,256]{2,1,0:T(8,128)(2,1)S(1)} %collective-permute-done.1.refs_2_), channel_id=1, source_target_pairs={{0,992},{32,0},{64,32},{96,64},{128,96},{160,128},{192,160},{224,1... | collective-permute-start | bytes 1572872 | tf_op jit(solution)/shard_map/ppermute | solution.py:102
  77.4 10.2 %collective-permute-start.3 = (bf16[8,128,256]{2,1,0:T(8,128)(2,1)S(1)}, bf16[8,128,256]{2,1,0:T(8,128)(2,1)}, u32[]{:S(2)}, u32[]{:S(2)}) collective-permute-start(bf16[8,128,256]{2,1,0:T(8,128)(2,1)S(1)} %bitcast.16), channel_id=1, source_target_pairs={{0,16},{16,0},{1,17},{17,1},{2,18},{18,2},{3,19},{19,3},{4,20},{20... | collective-permute-start | bytes 1572872 | tf_op jit(solution)/shard_map/ppermute | solution.py:104
  79.3 8.3 %collective-permute-start.5 = (bf16[8,128,256]{2,1,0:T(8,128)(2,1)S(1)}, bf16[8,128,256]{2,1,0:T(8,128)(2,1)}, u32[]{:S(2)}, u32[]{:S(2)}) collective-permute-start(bf16[8,128,256]{2,1,0:T(8,128)(2,1)S(1)} %collective-permute-done.1.refs_2_), channel_id=1, source_target_pairs={{0,16},{16,0},{1,17},{17,1},{2,18},{18,2},{3,19},{19,3},{4,20},{20... | collective-permute-start | bytes 1572872 | tf_op jit(solution)/shard_map/ppermute | solution.py:104
  82.6 5.0 %collective-permute-start.4 = (bf16[8,128,256]{2,1,0:T(8,128)(2,1)S(1)}, bf16[8,128,256]{2,1,0:T(8,128)(2,1)}, u32[]{:S(2)}, u32[]{:S(2)}) collective-permute-start(bf16[8,128,256]{2,1,0:T(8,128)(2,1)S(1)} %collective-permute-done.refs_1_), channel_id=1, source_target_pairs={{0,16},{16,0},{1,17},{17,1},{2,18},{18,2},{3,19},{19,3},{4,20},{20... | collective-permute-start | bytes 1572872 | tf_op jit(solution)/shard_map/ppermute | solution.py:104
  84.5 4.1 %collective-permute-start.6 = (bf16[8,128,256]{2,1,0:T(8,128)(2,1)S(1)}, bf16[8,128,256]{2,1,0:T(8,128)(2,1)}, u32[]{:S(2)}, u32[]{:S(2)}) collective-permute-start(bf16[8,128,256]{2,1,0:T(8,128)(2,1)S(1)} %collective-permute-done.2.refs_3_), channel_id=1, source_target_pairs={{0,16},{16,0},{1,17},{17,1},{2,18},{18,2},{3,19},{19,3},{4,20},{20... | collective-permute-start | bytes 1572872 | tf_op jit(solution)/shard_map/ppermute | solution.py:104
  88.6 1.7 copy-start
  96.2 73.7 %copy-start.1 = (bf16[256,256]{1,0:T(8,128)(2,1)S(1)}, bf16[256,256]{1,0:T(8,128)(2,1)}, u32[]{:S(2)}) copy-start(bf16[256,256]{1,0:T(8,128)(2,1)} %weight_ref.1) | copy-start | bytes 393220
  120.6 41.2 %all-to-all-start.3 = ((bf16[16,128,256]{2,1,0:T(8,128)(2,1)}), bf16[16,128,256]{2,1,0:T(8,128)(2,1)S(1)}, u32[]{:S(2)}, u32[]{:S(2)}) async-start(bf16[16,128,256]{2,1,0:T(8,128)(2,1)} %get-tuple-element.19), calls=%async_computation.3 | async-start | bytes 2097152 | tf_op jit(solution)/shard_map/all_to_all | solution.py:160
  162.5 13.2 %all-to-all-start.4 = ((bf16[16,16,256]{2,1,0:T(8,128)(2,1)}), bf16[16,16,256]{2,1,0:T(8,128)(2,1)S(1)}, u32[]{:S(2)}, u32[]{:S(2)}) async-start(bf16[16,16,256]{2,1,0:T(8,128)(2,1)} %shard_map.90), calls=%async_computation.4 | async-start | bytes 262144 | tf_op jit(solution)/shard_map/all_to_all | solution.py:163

commit v13 on v12

--- a/solution.py
+++ b/solution.py
@@ -153,7 +153,7 @@
             compiler_params=pltpu.CompilerParams(vmem_limit_bytes=4 * 2**20),
         )(array)
 
-    near, far = ("zb", "core"), "za"
+    near, far = "zb", ("za", "core")
     shares = summed(sum_and_copy_kernel, (lax.axis_size(near), share, width), jnp.float32, shares, nodes**-0.5)
     grad_share = summed(sum_kernel, (share, width), jnp.float32, lax.all_to_all(shares, near, 0, 0, tiled=True))
     grad_share, parts = lax.optimization_barrier((grad_share, parts))

time: 178 us -> 165 us (0.927)
  blocking collectives: 117 us -> 104 us
    all_gather x1, blocking collectives: 35.6 us -> 22.1 us  [body(): lax.all_gather(grad_share, far)]
where the time goes in v13:
time: 165 us; the launch traced here: 162 us
  blocking collectives  104 us (63%)
  starting transfers between devices  39.1 us (24%)
  waiting for transfers between devices  6.77 us (4%)
  Pallas kernels  6.31 us (4%)
  local copies, waits for them, and re-layouts  3.68 us (2%)
    all_gather x1, blocking collectives, gather(): lax.all_gather(grad_out, 'za')  57.3 us
    all_gather x1, blocking collectives, body(): lax.all_gather(grad_share, far)  22.1 us
    all_to_all x1, blocking collectives, body(): shares = lax.all_to_all(shares, COL, 0, 0, tiled=True)  13.3 us
    all_to_all x1, blocking collectives, body(): lax.all_to_all(shares, near, 0, 0, tiled=True)  11.6 us
    ppermute x4, starting transfers between devices, gather(): lax.ppermute(piece, 'core', swap)  8.65 us
    all_to_all x1, starting transfers between devices, from_all(): return lax.all_to_all(same, axes, 0, 0, tiled=True)  7.43 us
    all_to_all x1, starting transfers between devices, body(): lax.all_to_all(shares, COL, 0, 0, tiled=True).reshape(width, width)  7.24 us
    all_to_all x1, starting transfers between devices, body(): parts = lax.all_to_all(parts, COL, 0, 0, tiled=True)  5.72 us
  transfers between devices with their start and end apart: 10, of which 3 were waited for; matrix products, arithmetic and copies ran while one was open for 1% of the time, Pallas kernels for 1%

profile of v13, /device:TPU:6, one launch (start us, length us, event | category | flops | bytes accessed | tf_op | source)
XLA Modules:
  0.0 162.3 jit_solution(4569558244832290821)
XLA Ops:
  0.6 0.0 copy-start.3
  0.6 57.3 %all-gather = bf16[1024,256]{1,0:T(8,128)(2,1)S(1)} all-gather(bf16[128,256]{1,0:T(8,128)(2,1)} %param.7), channel_id=2, replica_groups=mesh['za'=8,'zb'=4,'core'=2,'x'=4,'y'=4] {'za'}, dimensions={0}, use_global_device_ids=true | all-gather | bytes 589824 | tf_op jit(solution)/shard_map/all_gather | solution.py:98
  57.9 3.0 %collective-permute-start.1 = (bf16[8,128,256]{2,1,0:T(8,128)(2,1)S(1)}, bf16[8,128,256]{2,1,0:T(8,128)(2,1)S(1)}, u32[]{:S(2)}, u32[]{:S(2)}) collective-permute-start(bf16[8,128,256]{2,1,0:T(8,128)(2,1)S(1)} %bitcast.14), channel_id=1, source_target_pairs={{0,992},{32,0},{64,32},{96,64},{128,96},{160,128},{192,160},{224,1... | collective-permute-start | bytes 1572872 | tf_op jit(solution)/shard_map/ppermute | solution.py:100
  61.0 1.9 %broadcast_in_dim.4 = bf16[16,128,256]{2,1,0:T(8,128)(2,1)} broadcast(bf16[128,256]{1,0:T(8,128)(2,1)} %param.8), dimensions={1,2} | broadcast | bytes 1114112 | tf_op jit(solution)/shard_map/broadcast_in_dim | solution.py:93
  62.9 7.4 %all-to-all-start = ((bf16[16,128,256]{2,1,0:T(8,128)(2,1)}), bf16[16,128,256]{2,1,0:T(8,128)(2,1)S(1)}, u32[]{:S(2)}, u32[]{:S(2)}) async-start(bf16[16,128,256]{2,1,0:T(8,128)(2,1)} %broadcast_in_dim.4), calls=%async_computation | async-start | bytes 2097152 | tf_op jit(solution)/shard_map/all_to_all | solution.py:94
  70.3 2.8 %collective-permute-start = (bf16[8,128,256]{2,1,0:T(8,128)(2,1)S(1)}, bf16[8,128,256]{2,1,0:T(8,128)(2,1)S(1)}, u32[]{:S(2)}, u32[]{:S(2)}) collective-permute-start(bf16[8,128,256]{2,1,0:T(8,128)(2,1)S(1)} %bitcast.15), channel_id=1, source_target_pairs={{0,32},{32,64},{64,96},{96,128},{128,160},{160,192},{192,224},{224... | collective-permute-start | bytes 1572872 | tf_op jit(solution)/shard_map/ppermute | solution.py:100
  73.1 0.0 collective-permute-done.1.refs_2_
  73.2 4.2 %collective-permute-start.2 = (bf16[8,128,256]{2,1,0:T(8,128)(2,1)S(1)}, bf16[8,128,256]{2,1,0:T(8,128)(2,1)S(1)}, u32[]{:S(2)}, u32[]{:S(2)}) collective-permute-start(bf16[8,128,256]{2,1,0:T(8,128)(2,1)S(1)} %collective-permute-done.1.refs_2_), channel_id=1, source_target_pairs={{0,992},{32,0},{64,32},{96,64},{128,96},{160,128},{192,160},{224,1... | collective-permute-start | bytes 1572872 | tf_op jit(solution)/shard_map/ppermute | solution.py:102
  77.4 1.9 %collective-permute-start.3 = (bf16[8,128,256]{2,1,0:T(8,128)(2,1)S(1)}, bf16[8,128,256]{2,1,0:T(8,128)(2,1)}, u32[]{:S(2)}, u32[]{:S(2)}) collective-permute-start(bf16[8,128,256]{2,1,0:T(8,128)(2,1)S(1)} %bitcast.16), channel_id=1, source_target_pairs={{0,16},{16,0},{1,17},{17,1},{2,18},{18,2},{3,19},{19,3},{4,20},{20... | collective-permute-start | bytes 1572872 | tf_op jit(solution)/shard_map/ppermute | solution.py:104
  79.3 2.4 %collective-permute-start.5 = (bf16[8,128,256]{2,1,0:T(8,128)(2,1)S(1)}, bf16[8,128,256]{2,1,0:T(8,128)(2,1)}, u32[]{:S(2)}, u32[]{:S(2)}) collective-permute-start(bf16[8,128,256]{2,1,0:T(8,128)(2,1)S(1)} %collective-permute-done.1.refs_2_), channel_id=1, source_target_pairs={{0,16},{16,0},{1,17},{17,1},{2,18},{18,2},{3,19},{19,3},{4,20},{20... | collective-permute-start | bytes 1572872 | tf_op jit(solution)/shard_map/ppermute | solution.py:104
  81.7 0.9 collective-permute-done.refs_1_
  82.6 0.0 all-to-all-done
  82.6 1.9 %collective-permute-start.4 = (bf16[8,128,256]{2,1,0:T(8,128)(2,1)S(1)}, bf16[8,128,256]{2,1,0:T(8,128)(2,1)}, u32[]{:S(2)}, u32[]{:S(2)}) collective-permute-start(bf16[8,128,256]{2,1,0:T(8,128)(2,1)S(1)} %collective-permute-done.refs_1_), channel_id=1, source_target_pairs={{0,16},{16,0},{1,17},{17,1},{2,18},{18,2},{3,19},{19,3},{4,20},{20... | collective-permute-start | bytes 1572872 | tf_op jit(solution)/shard_map/ppermute | solution.py:104
  84.5 0.0 collective-permute-done.2.refs_3_
  84.5 2.4 %collective-permute-start.6 = (bf16[8,128,256]{2,1,0:T(8,128)(2,1)S(1)}, bf16[8,128,256]{2,1,0:T(8,128)(2,1)}, u32[]{:S(2)}, u32[]{:S(2)}) collective-permute-start(bf16[8,128,256]{2,1,0:T(8,128)(2,1)S(1)} %collective-permute-done.2.refs_3_), channel_id=1, source_target_pairs={{0,16},{16,0},{1,17},{17,1},{2,18},{18,2},{3,19},{19,3},{4,20},{20... | collective-permute-start | bytes 1572872 | tf_op jit(solution)/shard_map/ppermute | solution.py:104
  87.6 0.0 collective-permute-done.3.refs_4_
  87.6 0.0 collective-permute-done.5.refs_6_
  87.6 0.0 collective-permute-done.4.refs_5_
  87.7 0.9 collective-permute-done.6.refs_7_
  88.6 1.7 %copy-done = bf16[1,1,80,128,128]{4,3,2,1,0:T(8,128)(2,1)S(1)} copy-done((bf16[1,1,80,128,128]{4,3,2,1,0:T(8,128)(2,1)S(1)}, bf16[1,1,80,128,128]{4,3,2,1,0:T(8,128)(2,1)}, u32[]{:S(2)}) %copy-start) | copy-done | bytes 2621464
  90.3 4.7 %shard_map.86 = (bf16[16,128,256]{2,1,0:T(8,128)(2,1)}, bf16[16,16,256]{2,1,0:T(8,128)(2,1)S(1)}) custom-call(s32[1]{0:T(128)} %bitcast.11.count_ref, s32[80]{0:T(128)S(1)} %bitcast.19, s32[80]{0:T(128)S(1)} %add_bitcast_fusion.places_ref, bf16[80,128,128]{2,1,0:T(8,128)(2,1)S(1)} %bitcast.13, bf16[8,128,256]{2,1,0:T(8,128)(2,1)S(1)} %bitcast.17, ...), custom_call_target="tpu_custom_call" | custom-call | tf_op jit(solution)/shard_map/pallas_call | solution.py:123
  95.0 0.0 copy-start.1
  95.0 13.3 %all_to_all.25.shares_ref = bf16[16,16,256]{2,1,0:T(8,128)(2,1)S(1)} all-to-all(bf16[16,16,256]{2,1,0:T(8,128)(2,1)S(1)} %get-tuple-element.16), channel_id=1, replica_groups=mesh['za'=8,'zb'=4,'core'=2,'x'=4,'y'=4] {'x','y'}, dimensions={0} | all-to-all | bytes 262144 | tf_op jit(solution)/shard_map/all_to_all | solution.py:145
  108.3 11.6 %all_to_all.26.shares_ref = f32[4,16,256]{2,1,0:T(8,128)S(1)} all-to-all(f32[4,16,256]{2,1,0:T(8,128)S(1)} %shard_map.87), channel_id=1, replica_groups=mesh['za'=8,'zb'=4,'core'=2,'x'=4,'y'=4] {'zb'}, dimensions={0} | all-to-all | bytes 131072 | tf_op jit(solution)/shard_map/all_to_all | solution.py:158
  120.0 5.7 %all-to-all-start.3 = ((bf16[16,128,256]{2,1,0:T(8,128)(2,1)}), bf16[16,128,256]{2,1,0:T(8,128)(2,1)S(1)}, u32[]{:S(2)}, u32[]{:S(2)}) async-start(bf16[16,128,256]{2,1,0:T(8,128)(2,1)} %get-tuple-element.19), calls=%async_computation.3 | async-start | bytes 2097152 | tf_op jit(solution)/shard_map/all_to_all | solution.py:160
  125.7 22.1 %all-gather.1 = f32[256,256]{1,0:T(8,128)S(1)} all-gather(f32[16,256]{1,0:T(8,128)S(1)} %shard_map.88), channel_id=3, replica_groups=mesh['za'=8,'zb'=4,'core'=2,'x'=4,'y'=4] {'za','core'}, dimensions={0}, use_global_device_ids=true | all-gather | bytes 278528 | tf_op jit(solution)/shard_map/all_gather | solution.py:161
  147.8 0.0 all-to-all-done.3.parts_ref
  147.8 0.7 shard_map.90
  148.5 7.2 %all-to-all-start.4 = ((bf16[16,16,256]{2,1,0:T(8,128)(2,1)}), bf16[16,16,256]{2,1,0:T(8,128)(2,1)S(1)}, u32[]{:S(2)}, u32[]{:S(2)}) async-start(bf16[16,16,256]{2,1,0:T(8,128)(2,1)} %shard_map.90), calls=%async_computation.4 | async-start | bytes 262144 | tf_op jit(solution)/shard_map/all_to_all | solution.py:163
  155.7 0.9 shard_map.89
  156.6 5.0 %all-to-all-done.4 = bf16[16,16,256]{2,1,0:T(8,128)(2,1)S(1)} async-done(((bf16[16,16,256]{2,1,0:T(8,128)(2,1)}), bf16[16,16,256]{2,1,0:T(8,128)(2,1)S(1)}, u32[]{:S(2)}, u32[]{:S(2)}) %all-to-all-start.4) | async-done | bytes 131104 | tf_op jit(solution)/shard_map/all_to_all | solution.py:163
  161.6 0.7 bitcast_convert_fusion
  (8 shorter events, 0.1 us)
Async XLA Ops:
  0.6 87.0 %copy-start.3 = (s32[1,1,80]{2,1,0:T(1,128)S(1)}, s32[1,1,80]{2,1,0:T(1,128)}, u32[]{:S(2)}) copy-start(s32[1,1,80]{2,1,0:T(1,128)} %param.12) | copy-start | bytes 964
  0.6 88.0 %copy-start.2 = (s32[1,1,80]{2,1,0:T(1,128)S(1)}, s32[1,1,80]{2,1,0:T(1,128)}, u32[]{:S(2)}) copy-start(s32[1,1,80]{2,1,0:T(1,128)} %param.11) | copy-start | bytes 964
  57.9 15.2 %collective-permute-start.1 = (bf16[8,128,256]{2,1,0:T(8,128)(2,1)S(1)}, bf16[8,128,256]{2,1,0:T(8,128)(2,1)S(1)}, u32[]{:S(2)}, u32[]{:S(2)}) collective-permute-start(bf16[8,128,256]{2,1,0:T(8,128)(2,1)S(1)} %bitcast.14), channel_id=1, source_target_pairs={{0,992},{32,0},{64,32},{96,64},{128,96},{160,128},{192,160},{224,1... | collective-permute-start | bytes 1572872 | tf_op jit(solution)/shard_map/ppermute | solution.py:100
  62.9 19.7 %all-to-all-start = ((bf16[16,128,256]{2,1,0:T(8,128)(2,1)}), bf16[16,128,256]{2,1,0:T(8,128)(2,1)S(1)}, u32[]{:S(2)}, u32[]{:S(2)}) async-start(bf16[16,128,256]{2,1,0:T(8,128)(2,1)} %broadcast_in_dim.4), calls=%async_computation | async-start | bytes 2097152 | tf_op jit(solution)/shard_map/all_to_all | solution.py:94
  70.3 12.3 %collective-permute-start = (bf16[8,128,256]{2,1,0:T(8,128)(2,1)S(1)}, bf16[8,128,256]{2,1,0:T(8,128)(2,1)S(1)}, u32[]{:S(2)}, u32[]{:S(2)}) collective-permute-start(bf16[8,128,256]{2,1,0:T(8,128)(2,1)S(1)} %bitcast.15), channel_id=1, source_target_pairs={{0,32},{32,64},{64,96},{96,128},{128,160},{160,192},{192,224},{224... | collective-permute-start | bytes 1572872 | tf_op jit(solution)/shard_map/ppermute | solution.py:100
  73.2 11.4 %collective-permute-start.2 = (bf16[8,128,256]{2,1,0:T(8,128)(2,1)S(1)}, bf16[8,128,256]{2,1,0:T(8,128)(2,1)S(1)}, u32[]{:S(2)}, u32[]{:S(2)}) collective-permute-start(bf16[8,128,256]{2,1,0:T(8,128)(2,1)S(1)} %collective-permute-done.1.refs_2_), channel_id=1, source_target_pairs={{0,992},{32,0},{64,32},{96,64},{128,96},{160,128},{192,160},{224,1... | collective-permute-start | bytes 1572872 | tf_op jit(solution)/shard_map/ppermute | solution.py:102
  77.4 10.2 %collective-permute-start.3 = (bf16[8,128,256]{2,1,0:T(8,128)(2,1)S(1)}, bf16[8,128,256]{2,1,0:T(8,128)(2,1)}, u32[]{:S(2)}, u32[]{:S(2)}) collective-permute-start(bf16[8,128,256]{2,1,0:T(8,128)(2,1)S(1)} %bitcast.16), channel_id=1, source_target_pairs={{0,16},{16,0},{1,17},{17,1},{2,18},{18,2},{3,19},{19,3},{4,20},{20... | collective-permute-start | bytes 1572872 | tf_op jit(solution)/shard_map/ppermute | solution.py:104
  79.3 8.3 %collective-permute-start.5 = (bf16[8,128,256]{2,1,0:T(8,128)(2,1)S(1)}, bf16[8,128,256]{2,1,0:T(8,128)(2,1)}, u32[]{:S(2)}, u32[]{:S(2)}) collective-permute-start(bf16[8,128,256]{2,1,0:T(8,128)(2,1)S(1)} %collective-permute-done.1.refs_2_), channel_id=1, source_target_pairs={{0,16},{16,0},{1,17},{17,1},{2,18},{18,2},{3,19},{19,3},{4,20},{20... | collective-permute-start | bytes 1572872 | tf_op jit(solution)/shard_map/ppermute | solution.py:104
  82.6 5.0 %collective-permute-start.4 = (bf16[8,128,256]{2,1,0:T(8,128)(2,1)S(1)}, bf16[8,128,256]{2,1,0:T(8,128)(2,1)}, u32[]{:S(2)}, u32[]{:S(2)}) collective-permute-start(bf16[8,128,256]{2,1,0:T(8,128)(2,1)S(1)} %collective-permute-done.refs_1_), channel_id=1, source_target_pairs={{0,16},{16,0},{1,17},{17,1},{2,18},{18,2},{3,19},{19,3},{4,20},{20... | collective-permute-start | bytes 1572872 | tf_op jit(solution)/shard_map/ppermute | solution.py:104
  84.5 4.1 %collective-permute-start.6 = (bf16[8,128,256]{2,1,0:T(8,128)(2,1)S(1)}, bf16[8,128,256]{2,1,0:T(8,128)(2,1)}, u32[]{:S(2)}, u32[]{:S(2)}) collective-permute-start(bf16[8,128,256]{2,1,0:T(8,128)(2,1)S(1)} %collective-permute-done.2.refs_3_), channel_id=1, source_target_pairs={{0,16},{16,0},{1,17},{17,1},{2,18},{18,2},{3,19},{19,3},{4,20},{20... | collective-permute-start | bytes 1572872 | tf_op jit(solution)/shard_map/ppermute | solution.py:104
  88.6 1.7 %copy-start = (bf16[1,1,80,128,128]{4,3,2,1,0:T(8,128)(2,1)S(1)}, bf16[1,1,80,128,128]{4,3,2,1,0:T(8,128)(2,1)}, u32[]{:S(2)}) copy-start(bf16[1,1,80,128,128]{4,3,2,1,0:T(8,128)(2,1)} %param.10) | copy-start | bytes 7864324
  95.0 60.7 %copy-start.1 = (bf16[256,256]{1,0:T(8,128)(2,1)S(1)}, bf16[256,256]{1,0:T(8,128)(2,1)}, u32[]{:S(2)}) copy-start(bf16[256,256]{1,0:T(8,128)(2,1)} %weight_ref.1) | copy-start | bytes 393220
  120.0 27.8 %all-to-all-start.3 = ((bf16[16,128,256]{2,1,0:T(8,128)(2,1)}), bf16[16,128,256]{2,1,0:T(8,128)(2,1)S(1)}, u32[]{:S(2)}, u32[]{:S(2)}) async-start(bf16[16,128,256]{2,1,0:T(8,128)(2,1)} %get-tuple-element.19), calls=%async_computation.3 | async-start | bytes 2097152 | tf_op jit(solution)/shard_map/all_to_all | solution.py:160
  148.5 13.1 %all-to-all-start.4 = ((bf16[16,16,256]{2,1,0:T(8,128)(2,1)}), bf16[16,16,256]{2,1,0:T(8,128)(2,1)S(1)}, u32[]{:S(2)}, u32[]{:S(2)}) async-start(bf16[16,16,256]{2,1,0:T(8,128)(2,1)} %shard_map.90), calls=%async_computation.4 | async-start | bytes 262144 | tf_op jit(solution)/shard_map/all_to_all | solution.py:163
